TPU v7x, 512 devices: a whole 4x4x16 slice. The times are simulated.
512 devices in a mesh: row: 128 (over z, x, core), col: 4 (over y).
Axes of the slice: x: 4, y: 4, z: 16, core: 2. Of those that a mesh axis runs over, the one named last changes fastest.
Arguments:
- features: bfloat16 [256, 65536], P('col', 'row'), may hold values from -6 to 6
- send_pieces: int32 [128, 128], P('row'), may hold values from 0 to 7
- remote_target: int32 [128, 128], P('row'), may hold values from 0 to 3
- remote_count: int32 [128], P('row'), may hold values from 85 to 128, as said below
- local_values: bfloat16 [512, 128, 128], P('row'), may hold values from -0.29882812 to 0.29882812
- remote_values: bfloat16 [16384, 64, 128], P('row'), may hold values from -0.23925781 to 0.23925781
- hub_rows: int32 [128, 2], P('row'), may hold values from 0 to 511, as said below
- hub_adjacency: bfloat16 [256, 65536], P(None, 'row'), may hold values from -0.08984375 to 0.08984375
- weight: bfloat16 [256, 256], replicated, may hold values from -0.375 to 0.375
- cotangent: bfloat16 [256, 65536], P('col', 'row'), may hold values from -6 to 6
Outputs:
- output: bfloat16 [256, 65536], P('col', 'row')
- grad_input: bfloat16 [256, 65536], P('col', 'row')
- weight_grad: float32 [256, 256], P('col')
Inputs may be any that keep to these rules, and one draw needn't show every extreme that they name: Peers from remote_count on contribute padding tiles; some device has all 128 peers live. `hub_rows`: A device's hubs are distinct local nodes.
All inputs are finite; a program needn't handle non-finite values.
Results may differ from a plain program's by a relative error of at most 0.0066.
Values may be sent and summed in bfloat16 or wider, within the bound.
No kernel may reach another device: no remote copies, remote signals or barrier semaphores. Data moves between devices by JAX's collectives and lax.ppermute only.
A program may use at most 64 MiB of HBM per device.

v0:
```python
import jax
import jax.numpy as jnp
from jax import lax
from jax.sharding import PartitionSpec as P


def gelu_value(values):
    return jax.nn.gelu(values, approximate=True)


def shards(
    features,
    send_pieces,
    remote_target,
    remote_count,
    local_values,
    remote_values,
    hub_rows,
    hub_adjacency,
    weight,
    cotangent,
):
    feat_width, row_count = features.shape
    block_rows = local_values.shape[1]
    piece_rows = remote_values.shape[1]
    block_count = row_count // block_rows
    piece_count = row_count // piece_rows
    peer_count = lax.axis_size("row")
    col_start = lax.axis_index("col") * feat_width
    live_mask = (jnp.arange(peer_count, dtype=jnp.int32) < remote_count[0]).astype(
        remote_values.dtype
    )
    remote_live = remote_values * live_mask[:, None, None]
    block_feats = features.reshape(feat_width, block_count, block_rows)
    hub_panel = features[:, hub_rows[0]]
    adj_rows = hub_adjacency
    hub_part = jnp.dot(
        lax.all_gather(hub_panel, "row", axis=1, tiled=True),
        adj_rows,
        preferred_element_type=jnp.float32,
    )
    outgoing = features.reshape(feat_width, piece_count, piece_rows)[:, send_pieces[0], :]
    incoming = lax.all_to_all(outgoing, "row", split_axis=1, concat_axis=1, tiled=True)
    local_part = jnp.einsum(
        "fbs,bsd->fbd", block_feats, local_values, preferred_element_type=jnp.float32
    )
    remote_part = jnp.einsum(
        "fqs,qsd->fqd", incoming, remote_live, preferred_element_type=jnp.float32
    )
    tile_part = (
        local_part.at[:, remote_target[0], :].add(remote_part).reshape(feat_width, row_count)
    )
    aggregate = (tile_part + hub_part).astype(jnp.bfloat16)
    own_rows = lax.dynamic_slice_in_dim(weight, col_start, feat_width, 0)
    pre_act = lax.psum_scatter(
        jnp.einsum("io,in->on", own_rows, aggregate, preferred_element_type=jnp.float32),
        "col",
        scatter_dimension=0,
        tiled=True,
    )
    output = gelu_value(pre_act).astype(jnp.bfloat16)
    grad_pre = jax.vjp(gelu_value, pre_act)[1](cotangent.astype(jnp.float32))[0].astype(
        jnp.bfloat16
    )
    grad_full = lax.all_gather(grad_pre, "col", axis=0, tiled=True)
    local_wgrad = jnp.einsum("in,on->io", aggregate, grad_full, preferred_element_type=jnp.float32)
    weight_grad = lax.psum(local_wgrad, "row")
    grad_agg = jnp.einsum(
        "io,on->in", own_rows, grad_full, preferred_element_type=jnp.float32
    ).astype(jnp.bfloat16)
    grad_blocks = grad_agg.reshape(feat_width, block_count, block_rows)
    local_grad = jnp.einsum(
        "fbd,bsd->fbs", grad_blocks, local_values, preferred_element_type=jnp.float32
    )
    target_picked = grad_blocks[:, remote_target[0], :]
    contrib = jnp.einsum(
        "fqd,qsd->fqs", target_picked, remote_live, preferred_element_type=jnp.float32
    )
    returned = lax.all_to_all(contrib, "row", split_axis=1, concat_axis=1, tiled=True)
    piece_grad = (
        local_grad.reshape(feat_width, piece_count, piece_rows)
        .at[:, send_pieces[0], :]
        .add(returned)
    )
    adj_rows = hub_adjacency
    hub_grad = lax.psum_scatter(
        jnp.einsum("hn,fn->hf", adj_rows, grad_agg, preferred_element_type=jnp.float32),
        "row",
        scatter_dimension=0,
        tiled=True,
    )
    grad_input = piece_grad.reshape(feat_width, row_count)
    grad_input = grad_input.at[:, hub_rows[0]].add(hub_grad.T)
    return (output, grad_input.astype(jnp.bfloat16), weight_grad)


def solution(mesh):
    placed = (
        P("col", "row"),
        P("row", None),
        P("row", None),
        P("row"),
        P("row", None, None),
        P("row", None, None),
        P("row", None),
        P(None, "row"),
        P(),
        P("col", "row"),
    )
    return jax.shard_map(
        shards,
        mesh=mesh,
        in_specs=placed,
        out_specs=(P("col", "row"), P("col", "row"), P("col", None)),
        check_vma=False,
    )
```

profile of v0, /device:TPU:1, one launch (start us, length us, event | category | flops | bytes accessed | tf_op | source)
XLA Modules:
  0.0 635.6 jit_solution(17946922367729417248)
XLA Ops:
  7.2 0.7 fusion.23
  7.9 1.0 reshape.114
  8.9 1.0 gather_fusion
  9.9 1.5 bitcast_bitcast_fusion.1
  11.4 4.7 reshape.173
  16.1 20.4 %all-to-all-start = ((bf16[128,2,2048]{2,1,0:T(2,128)(2,1)}), bf16[128,2,2048]{2,1,0:T(2,128)(2,1)S(1)}, u32[]{:S(2)}, u32[]{:S(2)}) async-start(bf16[128,2,2048]{2,1,0:T(2,128)(2,1)} %reshape.173), calls=%async_computation | async-start | bytes 2097152 | tf_op jit(solution)/shard_map/all_to_all | solution.py:43
  36.5 0.0 reduce-scatter.3.cloned.1.call-start
  36.6 0.1 copy.48
  37.4 0.6 gather_fusion.1
  38.0 121.0 %all-gather.1 = bf16[128,2,64]{2,1,0:T(2,128)(2,1)} all-gather(bf16[1,2,64]{2,1,0:T(2,128)(2,1)S(1)} %bitcast.80), channel_id=2, replica_groups=mesh['row'=128,'col'=4] {'row'}, dimensions={0}, use_global_device_ids=true | all-gather | bytes 33024 | tf_op jit(solution)/shard_map/all_gather | solution.py:38
  159.0 0.1 convolution_bitcast_fusion.1
  159.2 1.4 reshape.174
  160.6 4.3 fusion.2
  164.9 13.6 %scatter_fusion = f32[64,4,128]{2,0,1:T(8,128)S(1)} fusion(f32[64,4,128]{2,0,1:T(8,128)S(1)} %convolution_bitcast_fusion.1, s32[128]{0:T(128)S(1)} %fusion.22, f32[128,64,128]{2,1,0:T(8,128)} %fusion.2), kind=kCustom, calls=%fused_computation.3 | custom fusion | flops 1048576 | bytes 12583424 | tf_op jit(solution)/shard_map/scatter-add | solution.py:51
  178.5 0.2 fusion.4
  178.7 1.0 fusion.20
  179.8 0.0 reduce-scatter.3.cloned.1.call-update
  179.8 23.3 %reduce-scatter.3.cloned.1.call-done = f32[64,512]{1,0:T(8,128)} async-done(((f32[256,512]{1,0:T(8,128)}), f32[64,512]{1,0:T(8,128)}) %reduce-scatter.3.cloned.1.call-update) | async-done | bytes 131088 | tf_op jit(solution)/shard_map/reduce_scatter | solution.py:55
  203.1 1.6 fusion.9
  204.8 10.3 %all_gather.7 = bf16[256,512]{1,0:T(8,128)(2,1)S(1)} all-gather(bf16[64,512]{1,0:T(8,128)(2,1)S(1)} %get-tuple-element.17), channel_id=1, replica_groups=mesh['row'=128,'col'=4] {'col'}, dimensions={0}, use_global_device_ids=true | all-gather | bytes 327680 | tf_op jit(solution)/shard_map/all_gather | solution.py:65
  215.0 0.2 convolution_convert_fusion
  215.2 1.0 gather_fusion.2
  216.2 4.8 fusion.27
  221.0 5.5 reshape.175
  226.5 20.4 %all-to-all-start.1 = ((f32[128,1,4096]{2,1,0:T(1,128)}), f32[128,1,4096]{2,1,0:T(1,128)S(1)}, u32[]{:S(2)}, u32[]{:S(2)}) async-start(f32[128,1,4096]{2,1,0:T(1,128)} %reshape.175), calls=%async_computation.2 | async-start | bytes 4194304 | tf_op jit(solution)/shard_map/all_to_all | solution.py:79
  246.9 0.2 all-reduce.4.cloned.1.call-start
  247.1 1.3 dynamic-slice
  249.0 0.8 fusion.33
  249.9 0.8 convolution_bitcast_fusion.3
  250.7 0.0 all-reduce.4.cloned.1.call-update
  250.7 0.2 convolution_bitcast_fusion.2
  250.9 0.1 copy.50
  251.0 0.1 reshape.117
  251.2 0.1 copy.52
  251.2 338.1 %all-reduce.4.cloned.1.call-done = (f32[256,64]{0,1:T(8,128)}, f32[64,256]{1,0:T(8,128)}) async-done(((f32[256,64]{0,1:T(8,128)}, f32[64,256]{1,0:T(8,128)}), (f32[256,64]{0,1:T(8,128)}, f32[64,256]{1,0:T(8,128)})) %all-reduce.4.cloned.1.call-update) | async-done | bytes 131088
  589.4 0.8 constant_dynamic-slice_fusion
  590.2 0.1 copy.56
  590.3 1.4 copy-done.1
  591.6 0.5 broadcast.109
  592.2 7.3 %reduce = f32[128,4096]{1,0:T(8,128)S(1)} reduce(f32[128,1,4096]{2,1,0:T(1,128)} %copy-done.1, f32[]{:T(128)} %broadcast.109), dimensions={1}, to_apply=%all_to_all.7.reduce_sub_computation | reduce | bytes 4194308 | tf_op jit(solution)/shard_map/all_to_all | solution.py:79
  599.5 3.0 reshape.176
  602.5 4.7 bitcast_bitcast_fusion
  607.3 5.7 copy.53
  612.9 13.5 %scatter_fusion.1 = f32[64,8,64]{2,0,1:T(8,128)S(1)} fusion(f32[64,8,64]{2,0,1:T(8,128)S(1)} %copy.52, s32[128]{0:T(128)S(1)} %fusion.23, f32[128,64,64]{2,1,0:T(8,128)} %copy.53), kind=kCustom, calls=%fused_computation.4 | custom fusion | flops 524288 | bytes 6291968 | tf_op jit(solution)/shard_map/scatter-add | solution.py:83
  626.5 0.1 copy.58
  626.6 0.7 scatter_fusion.2
  627.4 0.7 copy.57
  628.1 0.6 copy.78
  (32 shorter events, 0.1 us)
Async XLA Ops:
  7.2 171.3 %copy-start = (bf16[256,512]{1,0:T(8,128)(2,1)S(1)}, bf16[256,512]{1,0:T(8,128)(2,1)}, u32[]{:S(2)}) copy-start(bf16[256,512]{1,0:T(8,128)(2,1)} %param.17) | copy-start | bytes 786436
  11.4 25.2 %copy-start.2 = (bf16[64,512]{1,0:T(8,128)(2,1)S(1)}, bf16[64,512]{1,0:T(8,128)(2,1)}, u32[]{:S(2)}) copy-start(bf16[64,512]{1,0:T(8,128)(2,1)} %param.10) | copy-start | bytes 196612
  11.4 26.0 %copy-start.9 = (s32[1,2]{1,0:T(1,128)S(1)}, s32[1,2]{1,0:T(1,128)}, u32[]{:S(2)}) copy-start(s32[1,2]{1,0:T(1,128)} %param.16) | copy-start | bytes 28
  11.4 147.6 %copy-start.10 = (s32[1,128]{1,0:T(1,128)S(1)}, s32[1,128]{1,0:T(1,128)}, u32[]{:S(2)}) copy-start(s32[1,128]{1,0:T(1,128)} %param.12) | copy-start | bytes 1540
  11.4 147.6 %copy-start.3 = (bf16[4,128,128]{2,1,0:T(8,128)(2,1)S(1)}, bf16[4,128,128]{2,1,0:T(8,128)(2,1)}, u32[]{:S(2)}) copy-start(bf16[4,128,128]{2,1,0:T(8,128)(2,1)} %param.14) | copy-start | bytes 393220
  16.1 143.1 %all-to-all-start = ((bf16[128,2,2048]{2,1,0:T(2,128)(2,1)}), bf16[128,2,2048]{2,1,0:T(2,128)(2,1)S(1)}, u32[]{:S(2)}, u32[]{:S(2)}) async-start(bf16[128,2,2048]{2,1,0:T(2,128)(2,1)} %reshape.173), calls=%async_computation | async-start | bytes 2097152 | tf_op jit(solution)/shard_map/all_to_all | solution.py:43
  36.5 166.6 %reduce-scatter.3.cloned.1.call-start = ((), (), s32[]{:S(2)}) async-start(), calls=%async_computation.3 | async-start | bytes 655360 | tf_op jit(solution)/shard_map/reduce_scatter | solution.py:55
  164.9 13.6 %copy-start.5 = (bf16[128,2,64]{2,1,0:T(2,128)(2,1)S(1)}, bf16[128,2,64]{2,1,0:T(2,128)(2,1)}, u32[]{:S(2)}) copy-start(bf16[128,2,64]{2,1,0:T(2,128)(2,1)} %all-gather.1) | copy-start | bytes 98308
  164.9 13.8 %copy-start.8 = (bf16[256,256]{1,0:T(8,128)(2,1)S(1)}, bf16[256,256]{1,0:T(8,128)(2,1)}, u32[]{:S(2)}) copy-start(bf16[256,256]{1,0:T(8,128)(2,1)} %param.18) | copy-start | bytes 393220
  164.9 38.2 %copy-start.6 = (bf16[64,512]{1,0:T(8,128)(2,1)S(1)}, bf16[64,512]{1,0:T(8,128)(2,1)}, u32[]{:S(2)}) copy-start(bf16[64,512]{1,0:T(8,128)(2,1)} %param.19) | copy-start | bytes 196612
  226.5 24.2 %copy-start.4 = (bf16[4,128,128]{2,1,0:T(8,128)(2,1)S(1)}, bf16[4,128,128]{2,1,0:T(8,128)(2,1)}, u32[]{:S(2)}) copy-start(bf16[4,128,128]{2,1,0:T(8,128)(2,1)} %param.14) | copy-start | bytes 393220
  226.5 363.8 %all-to-all-start.1 = ((f32[128,1,4096]{2,1,0:T(1,128)}), f32[128,1,4096]{2,1,0:T(1,128)S(1)}, u32[]{:S(2)}, u32[]{:S(2)}) async-start(f32[128,1,4096]{2,1,0:T(1,128)} %reshape.175), calls=%async_computation.2 | async-start | bytes 4194304 | tf_op jit(solution)/shard_map/all_to_all | solution.py:79
  246.9 342.5 %all-reduce.4.cloned.1.call-start = ((), (), s32[]{:S(2)}) async-start(), calls=%async_computation.4 | async-start | bytes 262144
  590.3 1.4 copy-start.1
  612.9 15.2 %copy-start.7 = (f32[64,256]{1,0:T(8,128)S(1)}, f32[64,256]{1,0:T(8,128)}, u32[]{:S(2)}) copy-start(f32[64,256]{1,0:T(8,128)} %get-tuple-element.21) | copy-start | bytes 196612
Sparse Core Ops, SparseCore 0:
  179.9 23.1 reduce-scatter.2
  251.8 337.4 all-reduce.3
where the time goes:
time: 638 us; the launch traced here: 636 us
  waiting for transfers between devices  362 us (57%)
  blocking collectives  131 us (21%)
  starting transfers between devices  41 us (6%)
  other arithmetic  37.6 us (6%)
  local copies, waits for them, and re-layouts  36.1 us (6%)
  between operations  15.6 us (2%)
  matrix products  12.5 us (2%)
    unnamed x3, waiting for transfers between devices  338 us
    all_gather x1, blocking collectives, shards(): lax.all_gather(hub_panel, 'row', axis=1, tiled=True)  121 us
    reduce_scatter x1, waiting for transfers between devices, shards(): lax.psum_scatter(jnp.einsum('io,in->on', own_rows, aggregate, preferred_e...  23.3 us
    unnamed x32, local copies, waits for them, and re-layouts  21.2 us
    all_to_all x1, starting transfers between devices, shards(): lax.all_to_all(outgoing, 'row', split_axis=1, concat_axis=1, tiled=True)  20.4 us
    all_to_all x1, starting transfers between devices, shards(): lax.all_to_all(contrib, 'row', split_axis=1, concat_axis=1, tiled=True)  20.4 us
    scatter-add x1, other arithmetic, shards(): local_part.at[:, remote_target[0], :].add(remote_part)  13.6 us
    scatter-add x1, other arithmetic, shards(): piece_grad = local_grad.reshape(feat_width, piece_count, piece_rows).at[:...  13.5 us
  transfers between devices with their start and end apart: 4, of which 2 were waited for; matrix products, arithmetic and copies ran while one was open for 1% of the time, Pallas kernels for 0%

commit v1 on v0

v1 whole, which is shorter than its diff:
```python
import jax
import jax.numpy as jnp
from jax import lax
from jax.experimental import pallas as pl
from jax.experimental.pallas import tpu as pltpu
from jax.sharding import Mesh
from jax.sharding import PartitionSpec as P

BF = jnp.bfloat16
F32 = jnp.float32

FAR = 8
NEAR = 16
COLS = 4
PEERS = FAR * NEAR
FEAT = 64
HALF = FEAT // 2
ROWS = 512
BLK = 128
BLOCKS = ROWS // BLK
PIECE = 64
PIECES = ROWS // PIECE
DENSE = PIECES * HALF
OUT_ROWS = DENSE + 16
NEAR_ROWS = FAR * HALF + 16
BACK_ROWS = NEAR_ROWS + 16
VMEM_BYTES = 24 * 1024 * 1024

NT = (((1,), (1,)), ((), ()))
TN = (((0,), (0,)), ((), ()))
NN = (((1,), (0,)), ((), ()))


def dot(left, right, dims=NN):
    return lax.dot_general(left, right, dims, preferred_element_type=F32)


def vmem():
    return pl.BlockSpec(memory_space=pltpu.VMEM)


def smem():
    return pl.BlockSpec(memory_space=pltpu.SMEM)


def call(body, ins, outs, scratch=(), flops=1_000_000, size=1_000_000):
    return pl.pallas_call(
        body,
        in_specs=ins,
        out_specs=[vmem() for _ in outs],
        out_shape=[jax.ShapeDtypeStruct(s, t) for s, t in outs],
        scratch_shapes=list(scratch),
        compiler_params=pltpu.CompilerParams(vmem_limit_bytes=VMEM_BYTES),
        cost_estimate=pl.CostEstimate(flops=flops, bytes_accessed=size, transcendentals=0),
    )


def pack_body(hubs, feats, wanted, out):
    for k in range(PIECES):
        low = feats[:HALF, k * PIECE : (k + 1) * PIECE]
        high = feats[HALF:, k * PIECE : (k + 1) * PIECE]
        out[k * HALF : (k + 1) * HALF, :] = jnp.concatenate([low, high], axis=1)
    node = lax.broadcasted_iota(jnp.int32, (8, ROWS), 1)
    which = lax.broadcasted_iota(jnp.int32, (8, ROWS), 0)
    hub = jnp.where(which == 0, hubs[0, 0], hubs[0, 1])
    pick = ((node == hub) & (which < 2)).astype(BF)
    rows = dot(pick, feats[...], NT)
    hub_row = jnp.concatenate([rows[0:1], rows[1:2]], axis=1)
    place = lax.broadcasted_iota(jnp.int32, (16, 128), 0)
    extra = jnp.where(
        place == 0,
        jnp.broadcast_to(wanted[...].astype(F32), (16, 128)),
        jnp.where(place == 1, jnp.broadcast_to(hub_row, (16, 128)), 0.0),
    )
    out[DENSE:, :] = extra.astype(BF)


def pick_body(piece, gathered, out):
    place = lax.broadcasted_iota(jnp.int32, (16, 128), 0)
    extra = jnp.zeros((16, 128), F32)
    for s in range(FAR):
        tail = gathered[s, DENSE:, :].astype(F32)
        extra = jnp.where(place == s, jnp.broadcast_to(tail[1:2], (16, 128)), extra)
    extra = extra.astype(BF)

    def step(n, carry):
        for s in range(FAR):
            start = pl.multiple_of(piece[s, n] * HALF, HALF)
            out[n, s * HALF : (s + 1) * HALF, :] = gathered[s, pl.ds(start, HALF), :]
        out[n, FAR * HALF :, :] = extra
        return carry

    lax.fori_loop(0, NEAR, step, 0)


def twice(tile):
    zero = jnp.zeros_like(tile)
    return jnp.concatenate(
        [jnp.concatenate([tile, zero], axis=1), jnp.concatenate([zero, tile], axis=1)], axis=0
    )


def forward_body(target, came, remote, feats, local, adj, cot, out, total):
    total[...] = jnp.zeros_like(total)

    def step(s, carry):
        start = pl.multiple_of(s * HALF, HALF)
        for first in range(0, NEAR, 8):
            parts = []
            for n in range(first, first + 8):
                parts.append(dot(came[n, pl.ds(start, HALF), :], twice(remote[s * NEAR + n])))
            for n in range(first, first + 8):
                total[target[s * NEAR + n]] += parts[n - first]
        return carry

    lax.fori_loop(0, FAR, step, 0)
    hub_rows = jnp.concatenate([came[n, FAR * HALF :, :][:8] for n in range(NEAR)], axis=0)
    hub = (
        dot(hub_rows, adj[: PEERS, :], TN)[:FEAT] + dot(hub_rows, adj[PEERS:, :], TN)[FEAT:]
    )
    for b in range(BLOCKS):
        cols = slice(b * BLK, (b + 1) * BLK)
        own = dot(feats[:, cols], local[b])
        tiles = jnp.concatenate([total[b, :, :BLK], total[b, :, BLK:]], axis=0)
        value = (own + tiles + hub[:, cols]).astype(BF)
        for c in range(COLS):
            out[c, :FEAT, cols] = value
    for c in range(COLS):
        out[c, FEAT:, :] = cot[...]


def middle_body(
    col, target, came, weight, remote, local, adj, output, back, own_grad, agg, grad, pick
):
    for c in range(COLS):
        agg[c * FEAT : (c + 1) * FEAT, :] = came[c, :FEAT, :]
    scale = 0.7978845608028654
    mine = pl.multiple_of(col[0] * FEAT, FEAT)
    for c in range(COLS):
        pre = dot(weight[:, c * FEAT : (c + 1) * FEAT], agg[...], TN)
        square = pre * pre
        bend = jnp.tanh(scale * (pre + 0.044715 * (square * pre)))
        half = 0.5 * (1.0 + bend)
        slope = half + 0.5 * pre * (1.0 - bend * bend) * (
            scale * (1.0 + 3.0 * 0.044715 * square)
        )
        grad[c * FEAT : (c + 1) * FEAT, :] = (came[c, FEAT:, :].astype(F32) * slope).astype(BF)

        @pl.when(col[0] == c)
        def _():
            output[...] = (pre * half).astype(BF)

    grad_agg = dot(weight[pl.ds(mine, FEAT), :], grad[...]).astype(BF)
    weight_grad = dot(agg[pl.ds(mine, FEAT), :], grad[...], NT)
    for b in range(BLOCKS):
        cols = slice(b * BLK, (b + 1) * BLK)
        pick[b] = jnp.concatenate([grad_agg[:HALF, cols], grad_agg[HALF:, cols]], axis=1)
        own_grad[:, cols] = dot(grad_agg[:, cols], local[b], NT)
    pick[BLOCKS] = jnp.zeros((HALF, 2 * BLK), BF)
    hub = dot(adj[...], grad_agg, NT)
    hub = jnp.concatenate([hub[:PEERS], hub[PEERS:]], axis=1)
    zero = jnp.zeros((8, 128), F32)
    for n in range(NEAR):
        back[n, FAR * HALF : NEAR_ROWS, :] = jnp.concatenate(
            [hub[n * 8 : (n + 1) * 8], zero], axis=0
        ).astype(BF)
        i, j = n // 2, n % 2
        tile = weight_grad[i * 8 : (i + 1) * 8, j * 128 : (j + 1) * 128]
        high = tile.astype(BF).astype(F32)
        back[n, NEAR_ROWS:, :] = jnp.concatenate([high, tile - high], axis=0).astype(BF)

    def step(s, carry):
        start = pl.multiple_of(s * HALF, HALF)
        for n in range(NEAR):
            q = s * NEAR + n
            part = dot(pick[target[q]], twice(remote[q]), NT)
            back[n, pl.ds(start, HALF), :] = part.astype(BF)
        return carry

    lax.fori_loop(0, FAR, step, 0)


def gather_body(piece, came, out, total):
    extra = jnp.zeros((16, 128), F32)
    grads = jnp.zeros((16, 128), F32)
    for n in range(NEAR):
        extra += came[n, FAR * HALF : NEAR_ROWS, :].astype(F32)
        grads += came[n, NEAR_ROWS:, :].astype(F32)
    chunk = grads[:8] + grads[8:]
    high = chunk.astype(BF).astype(F32)
    chunk = jnp.concatenate([high, chunk - high], axis=0).astype(BF)
    total[...] = jnp.zeros_like(total)

    def step(s, carry):
        start = pl.multiple_of(s * HALF, HALF)
        for n in range(NEAR):
            at = pl.multiple_of(piece[s, n] * HALF, HALF)
            total[s, pl.ds(at, HALF), :] += came[n, pl.ds(start, HALF), :].astype(F32)
        out[s, :DENSE, :] = total[s].astype(BF)
        return carry

    lax.fori_loop(0, FAR, step, 0)
    for s in range(FAR):
        out[s, DENSE:NEAR_ROWS, :] = jnp.broadcast_to(extra[s : s + 1], (16, 128)).astype(BF)
        out[s, NEAR_ROWS:, :] = chunk


def final_body(hubs, came, own_grad, out, chunk):
    total = came[0].astype(F32)
    for s in range(1, FAR):
        total += came[s].astype(F32)
    node = lax.broadcasted_iota(jnp.int32, (8, ROWS), 1)
    which = lax.broadcasted_iota(jnp.int32, (8, ROWS), 0)
    hub = jnp.where(which == 0, hubs[0, 0], hubs[0, 1])
    pick = ((node == hub) & (which < 2)).astype(F32)
    row = total[DENSE : DENSE + 8]
    place = lax.broadcasted_iota(jnp.int32, (8, FEAT), 0)
    values = jnp.where(place == 0, row[:, :FEAT], row[:, FEAT:])
    hub_grad = lax.dot_general(
        values, pick, TN, preferred_element_type=F32, precision=lax.Precision.HIGHEST
    )
    for k in range(0, PIECES, 2):
        cols = slice(k * PIECE, (k + 2) * PIECE)
        a, b = total[k * HALF : (k + 1) * HALF], total[(k + 1) * HALF : (k + 2) * HALF]
        low = jnp.concatenate([a[:, :PIECE], b[:, :PIECE]], axis=1)
        high = jnp.concatenate([a[:, PIECE:], b[:, PIECE:]], axis=1)
        tiles = jnp.concatenate([low, high], axis=0)
        out[:, cols] = (own_grad[:, cols] + tiles + hub_grad[:, cols]).astype(BF)
    grads = total[NEAR_ROWS : NEAR_ROWS + 8] + total[NEAR_ROWS + 8 :]
    for n in range(NEAR):
        chunk[n] = grads


def exchange(values, axis):
    return lax.all_to_all(values, axis, split_axis=0, concat_axis=0, tiled=True)


def shards(
    features,
    send_pieces,
    remote_target,
    remote_count,
    local_values,
    remote_values,
    hub_rows,
    hub_adjacency,
    weight,
    cotangent,
):
    far = lax.axis_index("far")
    col = lax.axis_index("col").astype(jnp.int32).reshape(1)
    target = jnp.where(
        jnp.arange(PEERS, dtype=jnp.int32) < remote_count[0], remote_target[0], BLOCKS
    )
    adj = (
        hub_adjacency.reshape(FAR, NEAR, 2, ROWS).transpose(2, 1, 0, 3).reshape(2 * PEERS, ROWS)
    )

    (packed,) = call(pack_body, [smem(), vmem(), vmem()], [((OUT_ROWS, 128), BF)])(
        hub_rows, features, send_pieces
    )
    gathered = lax.all_gather(packed, "far", axis=0, tiled=False)
    piece = lax.dynamic_slice(
        gathered[:, DENSE, :], (jnp.int32(0), far * NEAR), (FAR, NEAR)
    ).astype(jnp.int32)
    (picked,) = call(pick_body, [smem(), vmem()], [((NEAR, NEAR_ROWS, 128), BF)])(piece, gathered)
    came = exchange(picked, "near")
    (agg_cot,) = call(
        forward_body,
        [smem()] + [vmem()] * 6,
        [((COLS, 2 * FEAT, ROWS), BF)],
        [pltpu.VMEM((BLOCKS + 1, HALF, 2 * BLK), F32)],
    )(target, came, remote_values, features, local_values, adj, cotangent)
    full = exchange(agg_cot, "col")
    output, back, own_grad = call(
        middle_body,
        [smem(), smem()] + [vmem()] * 5,
        [((FEAT, ROWS), BF), ((NEAR, BACK_ROWS, 128), BF), ((FEAT, ROWS), F32)],
        [
            pltpu.VMEM((COLS * FEAT, ROWS), BF),
            pltpu.VMEM((COLS * FEAT, ROWS), BF),
            pltpu.VMEM((BLOCKS + 1, HALF, 2 * BLK), BF),
        ],
    )(col, target, full, weight, remote_values, local_values, adj)
    back = exchange(back, "near")
    (sums,) = call(
        gather_body,
        [smem(), vmem()],
        [((FAR, BACK_ROWS, 128), BF)],
        [pltpu.VMEM((FAR, DENSE, 128), F32)],
    )(piece, back)
    sums = exchange(sums, "far")
    grad_input, chunk = call(
        final_body,
        [smem(), vmem(), vmem()],
        [((FEAT, ROWS), BF), ((NEAR, 8, 128), F32)],
    )(hub_rows, sums, own_grad)
    tiles = exchange(chunk, "near")
    weight_grad = tiles.reshape(8, 2, 8, 128).transpose(0, 2, 1, 3).reshape(FEAT, 256)
    return (output, grad_input, weight_grad)


def solution(mesh):
    fine = Mesh(mesh.devices.reshape(FAR, NEAR, COLS), ("far", "near", "col"))
    row = ("far", "near")
    placed = (
        P("col", row),
        P(row, None),
        P(row, None),
        P(row),
        P(row, None, None),
        P(row, None, None),
        P(row, None),
        P(None, row),
        P(),
        P("col", row),
    )
    return jax.shard_map(
        shards,
        mesh=fine,
        in_specs=placed,
        out_specs=(P("col", row), P("col", row), P("col", None)),
        check_vma=False,
    )
```

time: 638 us -> 171 us (0.27)
  waiting for transfers between devices: 362 us -> 22.1 us
  other arithmetic: 37.6 us -> 0.08 us
  local copies, waits for them, and re-layouts: 36.1 us -> 10 us
  starting transfers between devices: 41 us -> 14.9 us
  blocking collectives: 131 us -> 108 us
  between operations: 15.6 us -> 1.38 us
  Pallas kernels: 0 us -> 13.9 us
  matrix products: 12.5 us -> 0 us
    unnamed x3 -> x0, waiting for transfers between devices: 338 us -> none
    all_gather x2 -> x1, blocking collectives: 131 us -> 33.2 us  [shards(): gathered = lax.all_gather(packed, 'far', axis=0, tiled=False)]
    all_to_all x0 -> x3, blocking collectives: none -> 74.6 us  [exchange(): return lax.all_to_all(values, axis, split_axis=0, concat_axis=0, tiled=True)]
    scatter-add x3 -> x0, other arithmetic: 27.9 us -> none  [the longest x1 13.6 us: shards(): local_part.at[:, remote_target[0], :].add(remote_part)]
    all_to_all x2, starting transfers between devices: 40.8 us -> 14.9 us  [exchange(): return lax.all_to_all(values, axis, split_axis=0, concat_axis=0, tiled=True)]
    reduce_scatter x1 -> x0, waiting for transfers between devices: 23.3 us -> none  [shards(): lax.psum_scatter(jnp.einsum('io,in->on', own_rows, aggregate, preferred_e...]
    all_to_all x2, waiting for transfers between devices: 0.01 us -> 22.1 us  [exchange(): return lax.all_to_all(values, axis, split_axis=0, concat_axis=0, tiled=True)]
    pallas_call x0 -> x6, Pallas kernels: none -> 13.9 us  [the longest x1 6.36 us: shards(): call(middle_body, [smem(), smem()] + [vmem()] * 5, [((FEAT, ROWS), BF), (...]
  transfers between devices with their start and end apart: 4 -> 2, of which waited for: 2 -> 2; matrix products, arithmetic and copies ran while one was open for 1% -> 1% of each run, Pallas kernels for 0% -> 0%
where the time goes in v1:
time: 171 us; the launch traced here: 170 us
  blocking collectives  108 us (63%)
  waiting for transfers between devices  22.1 us (13%)
  starting transfers between devices  14.9 us (9%)
  Pallas kernels  13.9 us (8%)
  local copies, waits for them, and re-layouts  10 us (6%)
    all_to_all x3, blocking collectives, exchange(): return lax.all_to_all(values, axis, split_axis=0, concat_axis=0, tiled=True)  74.6 us
    all_gather x1, blocking collectives, shards(): gathered = lax.all_gather(packed, 'far', axis=0, tiled=False)  33.2 us
    all_to_all x2, waiting for transfers between devices, exchange(): return lax.all_to_all(values, axis, split_axis=0, concat_axis=0, tiled=True)  22.1 us
    all_to_all x2, starting transfers between devices, exchange(): return lax.all_to_all(values, axis, split_axis=0, concat_axis=0, tiled=True)  14.9 us
    unnamed x29, local copies, waits for them, and re-layouts  8.14 us
    pallas_call x1, Pallas kernels, shards(): call(middle_body, [smem(), smem()] + [vmem()] * 5, [((FEAT, ROWS), BF), (...  6.36 us
  transfers between devices with their start and end apart: 2, of which 2 were waited for; matrix products, arithmetic and copies ran while one was open for 1% of the time, Pallas kernels for 0%

profile of v1, /device:TPU:1, one launch (start us, length us, event | category | flops | bytes accessed | tf_op | source)
XLA Modules:
  0.0 170.3 jit_solution(7059836268626807990)
XLA Ops:
  0.6 0.0 copy-start.5
  0.6 0.8 copy-done.5
  1.5 0.0 copy-start.9
  1.5 0.7 copy-done.9
  2.1 0.0 copy-start.11
  2.1 0.7 copy-done.11
  2.8 0.7 shard_map.121
  3.5 33.2 %all-gather = bf16[2176,128]{1,0:T(8,128)(2,1)S(1)} all-gather(bf16[272,128]{1,0:T(8,128)(2,1)S(1)} %shard_map.121), channel_id=2, replica_groups=mesh['far'=8,'near'=16,'col'=4] {'far'}, dimensions={0}, use_global_device_ids=true | all-gather | bytes 626688 | tf_op jit(solution)/shard_map/all_gather | solution.py:262
  36.7 0.1 dynamic-slice_convert_fusion
  36.8 0.0 copy-start.12
  36.8 0.9 shard_map.122
  37.7 0.0 copy-start.1
  37.8 1.0 copy-done.1
  38.8 0.0 copy-start.13
  38.8 0.0 copy-start
  38.8 0.0 copy-start.6
  38.8 10.7 %all-to-all-start = ((bf16[16,272,128]{2,1,0:T(8,128)(2,1)}), bf16[16,272,128]{2,1,0:T(8,128)(2,1)S(1)}, u32[]{:S(2)}, u32[]{:S(2)}) async-start(bf16[16,272,128]{2,1,0:T(8,128)(2,1)} %copy-done.1), calls=%async_computation | async-start | bytes 2228224 | tf_op jit(solution)/shard_map/all_to_all | solution.py:235
  50.1 0.0 copy-done.12
  50.2 0.8 reshape.25
  51.0 1.1 copy.13
  52.1 0.0 copy-done.13
  52.1 14.0 %all-to-all-done.came = bf16[16,272,128]{2,1,0:T(8,128)(2,1)S(1)} async-done(((bf16[16,272,128]{2,1,0:T(8,128)(2,1)}), bf16[16,272,128]{2,1,0:T(8,128)(2,1)S(1)}, u32[]{:S(2)}, u32[]{:S(2)}) %all-to-all-start) | async-done | bytes 1114144 | tf_op jit(solution)/shard_map/all_to_all | solution.py:235
  66.1 0.0 copy-done
  66.1 0.0 copy-done.6
  66.1 0.0 copy-start.3
  66.1 0.9 copy-done.3
  67.0 0.0 copy-start.8
  67.0 0.8 copy-done.8
  67.8 3.1 %shard_map.123 = bf16[4,128,512]{2,1,0:T(8,128)(2,1)S(1)} custom-call(s32[128]{0:T(128)S(1)} %compare_select_fusion.target, bf16[16,272,128]{2,1,0:T(8,128)(2,1)S(1)} %all-to-all-done.came, bf16[128,64,128]{2,1,0:T(8,128)(2,1)S(1)} %copy-done, bf16[64,512]{1,0:T(8,128)(2,1)S(1)} %copy-done.6, bf16[4,128,128]{2,1,0:T(8,128)(2,1)S(1)} %copy-done.3, ...), custom_call_target="tpu_custom_call" | custom-call | flops 1000000 | bytes 1000000 | tf_op jit(solution)/shard_map/pallas_call | solution.py:268
  70.9 0.0 copy-start.2
  70.9 0.8 copy-done.2
  71.7 4.2 %all-to-all-start.1 = ((bf16[4,128,512]{2,1,0:T(8,128)(2,1)}), bf16[4,128,512]{2,1,0:T(8,128)(2,1)S(1)}, u32[]{:S(2)}, u32[]{:S(2)}) async-start(bf16[4,128,512]{2,1,0:T(8,128)(2,1)} %copy-done.2), calls=%async_computation.1 | async-start | bytes 1048576 | tf_op jit(solution)/shard_map/all_to_all | solution.py:235
  75.9 8.1 %all-to-all-done.1.came = bf16[4,128,512]{2,1,0:T(8,128)(2,1)S(1)} async-done(((bf16[4,128,512]{2,1,0:T(8,128)(2,1)}), bf16[4,128,512]{2,1,0:T(8,128)(2,1)S(1)}, u32[]{:S(2)}, u32[]{:S(2)}) %all-to-all-start.1) | async-done | bytes 524320 | tf_op jit(solution)/shard_map/all_to_all | solution.py:235
  84.0 0.0 copy-start.4
  84.0 0.9 copy-done.4
  84.9 0.0 copy-start.7
  84.9 0.9 copy-done.7
  85.8 6.4 %shard_map.124 = (bf16[64,512]{1,0:T(8,128)(2,1)}, bf16[16,288,128]{2,1,0:T(8,128)(2,1)S(1)}, f32[64,512]{1,0:T(8,128)S(1)}) custom-call(s32[1]{0:T(128)} %bitcast.col, s32[128]{0:T(128)S(1)} %compare_select_fusion.target, bf16[4,128,512]{2,1,0:T(8,128)(2,1)S(1)} %all-to-all-done.1.came, bf16[256,256]{1,0:T(8,128)(2,1)S(1)} %copy-done.7, ...), custom_call_target="tpu_custom_call" | custom-call | flops 1000000 | bytes 1000000 | tf_op jit(solution)/shard_map/pallas_call | solution.py:275
  92.1 23.0 %all_to_all.25.came = bf16[16,288,128]{2,1,0:T(8,128)(2,1)S(1)} all-to-all(bf16[16,288,128]{2,1,0:T(8,128)(2,1)S(1)} %get-tuple-element.9), channel_id=1, replica_groups=mesh['far'=8,'near'=16,'col'=4] {'near'}, dimensions={0} | all-to-all | bytes 2359296 | tf_op jit(solution)/shard_map/all_to_all | solution.py:235
  115.1 0.0 copy-start.10
  115.1 1.3 shard_map.125
  116.4 37.0 %all_to_all.26.came = bf16[8,288,128]{2,1,0:T(8,128)(2,1)S(1)} all-to-all(bf16[8,288,128]{2,1,0:T(8,128)(2,1)S(1)} %shard_map.125), channel_id=1, replica_groups=mesh['far'=8,'near'=16,'col'=4] {'far'}, dimensions={0} | all-to-all | bytes 1179648 | tf_op jit(solution)/shard_map/all_to_all | solution.py:235
  153.4 0.0 copy-done.10
  153.4 1.6 shard_map.126
  154.9 14.7 %all_to_all.27 = f32[16,8,128]{2,1,0:T(8,128)S(1)} all-to-all(f32[16,8,128]{2,1,0:T(8,128)S(1)} %get-tuple-element.12), channel_id=1, replica_groups=mesh['far'=8,'near'=16,'col'=4] {'near'}, dimensions={0} | all-to-all | bytes 131072 | tf_op jit(solution)/shard_map/all_to_all | solution.py:235
  169.6 0.6 copy.16
  (2 shorter events, 0.0 us)
Async XLA Ops:
  0.6 0.8 copy-start.5
  1.5 0.7 copy-start.9
  2.1 0.7 copy-start.11
  36.8 13.3 %copy-start.12 = (bf16[256,512]{1,0:T(8,128)(2,1)S(1)}, bf16[256,512]{1,0:T(8,128)(2,1)}, u32[]{:S(2)}) copy-start(bf16[256,512]{1,0:T(8,128)(2,1)} %param.17) | copy-start | bytes 786436
  37.7 1.0 copy-start.1
  38.8 13.3 %copy-start.13 = (s32[1,128]{1,0:T(1,128)S(1)}, s32[1,128]{1,0:T(1,128)}, u32[]{:S(2)}) copy-start(s32[1,128]{1,0:T(1,128)} %param.12) | copy-start | bytes 1540
  38.8 27.3 %copy-start = (bf16[128,64,128]{2,1,0:T(8,128)(2,1)S(1)}, bf16[128,64,128]{2,1,0:T(8,128)(2,1)}, u32[]{:S(2)}) copy-start(bf16[128,64,128]{2,1,0:T(8,128)(2,1)} %remote.3) | copy-start | bytes 6291460
  38.8 27.3 %copy-start.6 = (bf16[64,512]{1,0:T(8,128)(2,1)S(1)}, bf16[64,512]{1,0:T(8,128)(2,1)}, u32[]{:S(2)}) copy-start(bf16[64,512]{1,0:T(8,128)(2,1)} %feats.3) | copy-start | bytes 196612
  38.8 27.3 %all-to-all-start = ((bf16[16,272,128]{2,1,0:T(8,128)(2,1)}), bf16[16,272,128]{2,1,0:T(8,128)(2,1)S(1)}, u32[]{:S(2)}, u32[]{:S(2)}) async-start(bf16[16,272,128]{2,1,0:T(8,128)(2,1)} %copy-done.1), calls=%async_computation | async-start | bytes 2228224 | tf_op jit(solution)/shard_map/all_to_all | solution.py:235
  66.1 0.9 copy-start.3
  67.0 0.8 copy-start.8
  70.9 0.8 copy-start.2
  71.7 12.3 %all-to-all-start.1 = ((bf16[4,128,512]{2,1,0:T(8,128)(2,1)}), bf16[4,128,512]{2,1,0:T(8,128)(2,1)S(1)}, u32[]{:S(2)}, u32[]{:S(2)}) async-start(bf16[4,128,512]{2,1,0:T(8,128)(2,1)} %copy-done.2), calls=%async_computation.1 | async-start | bytes 1048576 | tf_op jit(solution)/shard_map/all_to_all | solution.py:235
  84.0 0.9 copy-start.4
  84.9 0.9 copy-start.7
  115.1 38.2 %copy-start.10 = (s32[1,2]{1,0:T(1,128)S(1)}, s32[1,2]{1,0:T(1,128)}, u32[]{:S(2)}) copy-start(s32[1,2]{1,0:T(1,128)} %hubs.3) | copy-start | bytes 28

commit v2 on v1

v2 whole, which is shorter than its diff:
```python
import jax
import jax.numpy as jnp
from jax import lax
from jax.experimental import pallas as pl
from jax.experimental.pallas import tpu as pltpu
from jax.sharding import Mesh
from jax.sharding import PartitionSpec as P

BF = jnp.bfloat16
F32 = jnp.float32

FAR = 8
NEAR = 16
COLS = 4
PEERS = FAR * NEAR
FEAT = 64
HALF = FEAT // 2
ROWS = 512
BLK = 128
BLOCKS = ROWS // BLK
PIECE = 64
PIECES = ROWS // PIECE
DENSE = PIECES * HALF
OUT_ROWS = DENSE + 16
NEAR_ROWS = FAR * HALF + 16
BACK_ROWS = NEAR_ROWS
VMEM_BYTES = 30 * 1024 * 1024
ORDER = (7, 0, 12, 3, 9, 14, 5, 10, 1, 15, 6, 2, 13, 8, 4, 11)
SLOT = tuple(ORDER.index(n) for n in range(NEAR))

NT = (((1,), (1,)), ((), ()))
TN = (((0,), (0,)), ((), ()))
NN = (((1,), (0,)), ((), ()))


def dot(left, right, dims=NN):
    return lax.dot_general(left, right, dims, preferred_element_type=F32)


def vmem():
    return pl.BlockSpec(memory_space=pltpu.VMEM)


def smem():
    return pl.BlockSpec(memory_space=pltpu.SMEM)


def away():
    return pl.BlockSpec(memory_space=pl.ANY)


def call(body, ins, outs, scratch=(), flops=1_000_000, size=1_000_000):
    return pl.pallas_call(
        body,
        in_specs=ins,
        out_specs=[spec for _, _, spec in outs],
        out_shape=[
            pltpu.HBM(shape, kind)
            if spec.memory_space is pl.ANY
            else jax.ShapeDtypeStruct(shape, kind)
            for shape, kind, spec in outs
        ],
        scratch_shapes=list(scratch),
        compiler_params=pltpu.CompilerParams(vmem_limit_bytes=VMEM_BYTES),
        cost_estimate=pl.CostEstimate(flops=flops, bytes_accessed=size, transcendentals=0),
    )


def start_all(pairs, sems):
    copies = [pltpu.make_async_copy(src, dst, sems.at[i]) for i, (src, dst) in enumerate(pairs)]
    for copy in copies:
        copy.start()
    return copies


def stay(value):
    return pltpu.with_memory_space_constraint(value, pltpu.HBM)


def part(ref, s):
    return ref.at[:, pl.ds(pl.multiple_of(s * HALF, HALF), HALF), :]


def tiles_of(ref, s):
    return ref.at[pl.ds(s * NEAR, NEAR)]


def pack_body(hubs, feats, wanted, out):
    for k in range(PIECES):
        low = feats[:HALF, k * PIECE : (k + 1) * PIECE]
        high = feats[HALF:, k * PIECE : (k + 1) * PIECE]
        out[k * HALF : (k + 1) * HALF, :] = jnp.concatenate([low, high], axis=1)
    node = lax.broadcasted_iota(jnp.int32, (8, ROWS), 1)
    which = lax.broadcasted_iota(jnp.int32, (8, ROWS), 0)
    hub = jnp.where(which == 0, hubs[0, 0], hubs[0, 1])
    pick = ((node == hub) & (which < 2)).astype(BF)
    rows = dot(pick, feats[...], NT)
    hub_row = jnp.concatenate([rows[0:1], rows[1:2]], axis=1)
    place = lax.broadcasted_iota(jnp.int32, (16, 128), 0)
    extra = jnp.where(
        place == 0,
        jnp.broadcast_to(wanted[...].astype(F32), (16, 128)),
        jnp.where(place == 1, jnp.broadcast_to(hub_row, (16, 128)), 0.0),
    )
    out[DENSE:, :] = extra.astype(BF)


def pick_body(piece, gathered, out, held, sems):
    place = lax.broadcasted_iota(jnp.int32, (16, 128), 0)
    extra = jnp.zeros((16, 128), F32)
    for s in range(FAR):
        tail = gathered[s, DENSE:, :].astype(F32)
        extra = jnp.where(place == s, jnp.broadcast_to(tail[1:2], (16, 128)), extra)
    extra = extra.astype(BF)
    copies = []
    for n in range(NEAR):
        for s in range(FAR):
            start = pl.multiple_of(piece[s, ORDER[n]] * HALF, HALF)
            held[n, s * HALF : (s + 1) * HALF, :] = gathered[s, pl.ds(start, HALF), :]
        held[n, FAR * HALF :, :] = extra
        copies.append(pltpu.make_async_copy(held.at[n], out.at[n], sems.at[n]))
        copies[-1].start()
    for copy in copies:
        copy.wait()


def twice(tile):
    zero = jnp.zeros_like(tile)
    return jnp.concatenate(
        [jnp.concatenate([tile, zero], axis=1), jnp.concatenate([zero, tile], axis=1)], axis=0
    )


def forward_body(
    target,
    came,
    remote_far,
    feats_far,
    local_far,
    adj_far,
    out,
    remote,
    feats,
    local,
    adj,
    own,
    value,
    total,
    sems,
    remote_sems,
    out_sems,
):
    pairs = [(feats_far, feats), (local_far, local)]
    first = start_all(pairs, sems)
    start_all([(tiles_of(remote_far, s), tiles_of(remote, s)) for s in range(FAR)], remote_sems)
    last = pltpu.make_async_copy(adj_far, adj, sems.at[2])
    last.start()
    total[...] = jnp.zeros_like(total)
    for copy in first:
        copy.wait()
    for b in range(BLOCKS):
        cols = slice(b * BLK, (b + 1) * BLK)
        own[:, cols] = dot(feats[:, cols], local[b])

    def step(s, carry):
        start = pl.multiple_of(s * HALF, HALF)
        pltpu.make_async_copy(
            tiles_of(remote_far, s), tiles_of(remote, s), remote_sems.at[s]
        ).wait()
        for first in range(0, NEAR, 8):
            parts = []
            for n in range(first, first + 8):
                parts.append(
                    dot(came[n, pl.ds(start, HALF), :], twice(remote[s * NEAR + ORDER[n]]))
                )
            for n in range(first, first + 8):
                total[target[s * NEAR + ORDER[n]]] += parts[n - first]
        return carry

    lax.fori_loop(0, FAR, step, 0)
    last.wait()
    hub_rows = jnp.concatenate([came[SLOT[n], FAR * HALF :, :][:8] for n in range(NEAR)], axis=0)
    hub = (
        dot(hub_rows, adj[: PEERS, :], TN)[:FEAT] + dot(hub_rows, adj[PEERS:, :], TN)[FEAT:]
    )
    for b in range(BLOCKS):
        cols = slice(b * BLK, (b + 1) * BLK)
        tiles = jnp.concatenate([total[b, :, :BLK], total[b, :, BLK:]], axis=0)
        value[:, cols] = (own[:, cols] + tiles + hub[:, cols]).astype(BF)
    for copy in start_all([(value, out.at[c]) for c in range(COLS)], out_sems):
        copy.wait()


def middle_body(
    col,
    target,
    agg,
    cot_far,
    weight_far,
    remote_far,
    local_far,
    adj_far,
    output,
    back,
    own_grad,
    cot,
    weight,
    remote,
    local,
    adj,
    grad,
    pick,
    held,
    sems,
    remote_sems,
    back_sems,
):
    pairs = [
        (weight_far, weight),
        (cot_far, cot),
        (local_far, local),
        (adj_far, adj),
    ]
    copies = start_all(pairs, sems)
    start_all([(tiles_of(remote_far, s), tiles_of(remote, s)) for s in range(FAR)], remote_sems)
    for copy in copies[:2]:
        copy.wait()
    scale = 0.7978845608028654
    mine = pl.multiple_of(col[0] * FEAT, FEAT)
    for c in range(COLS):
        pre = dot(weight[:, c * FEAT : (c + 1) * FEAT], agg[...], TN)
        square = pre * pre
        bend = jnp.tanh(scale * (pre + 0.044715 * (square * pre)))
        half = 0.5 * (1.0 + bend)
        slope = half + 0.5 * pre * (1.0 - bend * bend) * (
            scale * (1.0 + 3.0 * 0.044715 * square)
        )
        grad[c * FEAT : (c + 1) * FEAT, :] = (
            cot[c * FEAT : (c + 1) * FEAT, :].astype(F32) * slope
        ).astype(BF)

        @pl.when(col[0] == c)
        def _():
            output[...] = (pre * half).astype(BF)

    grad_agg = dot(weight[pl.ds(mine, FEAT), :], grad[...]).astype(BF)
    weight_grad = dot(agg[pl.ds(mine, FEAT), :], grad[...], NT)
    for copy in copies[2:]:
        copy.wait()
    for b in range(BLOCKS):
        cols = slice(b * BLK, (b + 1) * BLK)
        pick[b] = jnp.concatenate([grad_agg[:HALF, cols], grad_agg[HALF:, cols]], axis=1)
        own_grad[:, cols] = dot(grad_agg[:, cols], local[b], NT)
    pick[BLOCKS] = jnp.zeros((HALF, 2 * BLK), BF)
    hub = dot(adj[...], grad_agg, NT)
    hub = jnp.concatenate([hub[:PEERS], hub[PEERS:]], axis=1)
    for n in range(NEAR):
        m = ORDER[n]
        i, j = m // 2, m % 2
        tile = weight_grad[i * 8 : (i + 1) * 8, j * 128 : (j + 1) * 128]
        held[n, FAR * HALF :, :] = jnp.concatenate([hub[m * 8 : (m + 1) * 8], tile], axis=0).astype(BF)
    ends = slice(FAR * HALF, NEAR_ROWS)
    last = pltpu.make_async_copy(held.at[:, ends, :], back.at[:, ends, :], sems.at[4])
    last.start()

    def step(s, carry):
        start = pl.multiple_of(s * HALF, HALF)
        pltpu.make_async_copy(
            tiles_of(remote_far, s), tiles_of(remote, s), remote_sems.at[s]
        ).wait()
        for n in range(NEAR):
            q = s * NEAR + ORDER[n]
            tile = dot(pick[target[q]], twice(remote[q]), NT)
            held[n, pl.ds(start, HALF), :] = tile.astype(BF)
        pltpu.make_async_copy(part(held, s), part(back, s), back_sems.at[s]).start()
        return carry

    lax.fori_loop(0, FAR, step, 0)
    last.wait()
    for s in range(FAR):
        pltpu.make_async_copy(part(held, s), part(back, s), back_sems.at[s]).wait()


def gather_body(piece, came, out, held, total, out_sems):
    total[...] = jnp.zeros_like(total)
    extra = jnp.zeros((16, 128), F32)
    for n in range(NEAR):
        extra += came[n, FAR * HALF :, :].astype(F32)
    for s in range(FAR):
        hub = jnp.broadcast_to(extra[s : s + 1], (8, 128))
        held[s, DENSE:, :] = jnp.concatenate([hub, extra[8:]], axis=0).astype(BF)

    def step(s, carry):
        start = pl.multiple_of(s * HALF, HALF)
        for n in range(NEAR):
            at = pl.multiple_of(piece[s, ORDER[n]] * HALF, HALF)
            total[s, pl.ds(at, HALF), :] += came[n, pl.ds(start, HALF), :].astype(F32)
        held[s, :DENSE, :] = total[s].astype(BF)
        pltpu.make_async_copy(held.at[s], out.at[s], out_sems.at[s]).start()
        return carry

    lax.fori_loop(0, FAR, step, 0)
    for s in range(FAR):
        pltpu.make_async_copy(held.at[s], out.at[s], out_sems.at[s]).wait()


def chunk_body(came, chunk):
    tail = came[0, DENSE:, :].astype(F32)
    for s in range(1, FAR):
        tail += came[s, DENSE:, :].astype(F32)
    for n in range(NEAR):
        chunk[n] = tail[8:]


def final_body(hubs, came, own_grad, out):
    total = came[0].astype(F32)
    for s in range(1, FAR):
        total += came[s].astype(F32)
    node = lax.broadcasted_iota(jnp.int32, (8, ROWS), 1)
    which = lax.broadcasted_iota(jnp.int32, (8, ROWS), 0)
    hub = jnp.where(which == 0, hubs[0, 0], hubs[0, 1])
    pick = ((node == hub) & (which < 2)).astype(F32)
    row = total[DENSE : DENSE + 8]
    place = lax.broadcasted_iota(jnp.int32, (8, FEAT), 0)
    values = jnp.where(place == 0, row[:, :FEAT], row[:, FEAT:])
    hub_grad = lax.dot_general(
        values, pick, TN, preferred_element_type=F32, precision=lax.Precision.HIGHEST
    )
    for k in range(0, PIECES, 2):
        cols = slice(k * PIECE, (k + 2) * PIECE)
        a, b = total[k * HALF : (k + 1) * HALF], total[(k + 1) * HALF : (k + 2) * HALF]
        low = jnp.concatenate([a[:, :PIECE], b[:, :PIECE]], axis=1)
        high = jnp.concatenate([a[:, PIECE:], b[:, PIECE:]], axis=1)
        tiles = jnp.concatenate([low, high], axis=0)
        out[:, cols] = (own_grad[:, cols] + tiles + hub_grad[:, cols]).astype(BF)


def exchange(values, axis, order=None):
    return lax.all_to_all(
        values,
        axis,
        split_axis=0,
        concat_axis=0,
        tiled=True,
        axis_index_groups=None if order is None else [list(order)],
    )


def shards(
    features,
    send_pieces,
    remote_target,
    remote_count,
    local_values,
    remote_values,
    hub_rows,
    hub_adjacency,
    weight,
    cotangent,
):
    far = lax.axis_index("far")
    col = lax.axis_index("col").astype(jnp.int32).reshape(1)
    target = jnp.where(
        jnp.arange(PEERS, dtype=jnp.int32) < remote_count[0], remote_target[0], BLOCKS
    )
    adj = (
        hub_adjacency.reshape(FAR, NEAR, 2, ROWS).transpose(2, 1, 0, 3).reshape(2 * PEERS, ROWS)
    )
    (packed,) = call(pack_body, [smem(), vmem(), vmem()], [((OUT_ROWS, 128), BF, vmem())])(
        stay(hub_rows), stay(features), stay(send_pieces)
    )
    gathered = lax.all_gather(packed, "far", axis=0, tiled=False)
    piece = lax.dynamic_slice(
        gathered[:, DENSE, :], (jnp.int32(0), far * NEAR), (FAR, NEAR)
    ).astype(jnp.int32)
    near_all = (NEAR, NEAR_ROWS, 128)
    (picked,) = call(
        pick_body,
        [smem(), vmem()],
        [(near_all, BF, away())],
        [pltpu.VMEM(near_all, BF), pltpu.SemaphoreType.DMA((NEAR,))],
    )(piece, gathered)
    picked, cotangent = lax.optimization_barrier((picked, cotangent))
    came = exchange(picked, "near", ORDER)
    cot = lax.all_gather(cotangent, "col", axis=0, tiled=True)
    came, cot = lax.optimization_barrier((came, cot))
    (agg,) = call(
        forward_body,
        [smem(), vmem()] + [away()] * 4,
        [((COLS, FEAT, ROWS), BF, away())],
        [
            pltpu.VMEM((PEERS, PIECE, BLK), BF),
            pltpu.VMEM((FEAT, ROWS), BF),
            pltpu.VMEM((BLOCKS, BLK, BLK), BF),
            pltpu.VMEM((2 * PEERS, ROWS), BF),
            pltpu.VMEM((FEAT, ROWS), F32),
            pltpu.VMEM((FEAT, ROWS), BF),
            pltpu.VMEM((BLOCKS + 1, HALF, 2 * BLK), F32),
            pltpu.SemaphoreType.DMA((3,)),
            pltpu.SemaphoreType.DMA((FAR,)),
            pltpu.SemaphoreType.DMA((COLS,)),
        ],
    )(target, came, *map(stay, (remote_values, features, local_values, adj)))
    agg = exchange(agg, "col").reshape(COLS * FEAT, ROWS)
    wide = (COLS * FEAT, ROWS)
    output, back, own_grad = call(
        middle_body,
        [smem(), smem(), vmem()] + [away()] * 5,
        [((FEAT, ROWS), BF, vmem()), (near_all, BF, away()), ((FEAT, ROWS), F32, vmem())],
        [
            pltpu.VMEM(wide, BF),
            pltpu.VMEM((COLS * FEAT, COLS * FEAT), BF),
            pltpu.VMEM((PEERS, PIECE, BLK), BF),
            pltpu.VMEM((BLOCKS, BLK, BLK), BF),
            pltpu.VMEM((2 * PEERS, ROWS), BF),
            pltpu.VMEM(wide, BF),
            pltpu.VMEM((BLOCKS + 1, HALF, 2 * BLK), BF),
            pltpu.VMEM(near_all, BF),
            pltpu.SemaphoreType.DMA((5,)),
            pltpu.SemaphoreType.DMA((FAR,)),
            pltpu.SemaphoreType.DMA((FAR,)),
        ],
    )(col, target, agg, *map(stay, (cot, weight, remote_values, local_values, adj)))
    back = exchange(back, "near", ORDER)
    far_all = (FAR, BACK_ROWS, 128)
    (sums,) = call(
        gather_body,
        [smem(), vmem()],
        [(far_all, BF, away())],
        [
            pltpu.VMEM(far_all, BF),
            pltpu.VMEM((FAR, DENSE, 128), F32),
            pltpu.SemaphoreType.DMA((FAR,)),
        ],
    )(piece, back)
    sums = exchange(sums, "far")
    (chunk,) = call(chunk_body, [vmem()], [((NEAR, 8, 128), F32, vmem())])(sums)
    tiles = exchange(chunk, "near")
    (grad_input,) = call(
        final_body, [smem(), vmem(), vmem()], [((FEAT, ROWS), BF, vmem())]
    )(stay(hub_rows), sums, own_grad)
    weight_grad = tiles.reshape(8, 2, 8, 128).transpose(0, 2, 1, 3).reshape(FEAT, 256)
    return (output, grad_input, weight_grad)


def solution(mesh):
    fine = Mesh(mesh.devices.reshape(FAR, NEAR, COLS), ("far", "near", "col"))
    row = ("far", "near")
    placed = (
        P("col", row),
        P(row, None),
        P(row, None),
        P(row),
        P(row, None, None),
        P(row, None, None),
        P(row, None),
        P(None, row),
        P(),
        P("col", row),
    )
    return jax.shard_map(
        shards,
        mesh=fine,
        in_specs=placed,
        out_specs=(P("col", row), P("col", row), P("col", None)),
        check_vma=False,
    )
```

time: 171 us -> 165 us (0.965)
  waiting for transfers between devices: 22.1 us -> 10.6 us
  starting transfers between devices: 14.9 us -> 24.9 us
  local copies, waits for them, and re-layouts: 10 us -> 1.62 us
  Pallas kernels: 13.9 us -> 21.4 us
  blocking collectives: 108 us -> 104 us
    all_to_all x3 -> x2, blocking collectives: 74.6 us -> 59.7 us  [exchange(): lax.all_to_all(values, axis, split_axis=0, concat_axis=0, tiled=True, axi...]
    all_to_all x2 -> x3, waiting for transfers between devices: 22.1 us -> 10.6 us  [exchange(): lax.all_to_all(values, axis, split_axis=0, concat_axis=0, tiled=True, axi...]
    all_gather x0 -> x1, blocking collectives: none -> 11.2 us  [shards(): cot = lax.all_gather(cotangent, 'col', axis=0, tiled=True)]
    all_to_all x2 -> x3, starting transfers between devices: 14.9 us -> 24.9 us  [exchange(): lax.all_to_all(values, axis, split_axis=0, concat_axis=0, tiled=True, axi...]
    unnamed x29 -> x7, local copies, waits for them, and re-layouts: 8.14 us -> 0.65 us
    pallas_call x6 -> x7, Pallas kernels: 13.9 us -> 21.4 us  [the longest x1 8.87 us: shards(): call(middle_body, [smem(), smem(), vmem()] + [away()] * 5, [((FEAT, ROWS)...]
  transfers between devices with their start and end apart: 2 -> 3, of which waited for: 2 -> 3; matrix products, arithmetic and copies ran while one was open for 1% -> 1% of each run, Pallas kernels for 0% -> 1%
where the time goes in v2:
time: 165 us; the launch traced here: 164 us
  blocking collectives  104 us (63%)
  starting transfers between devices  24.9 us (15%)
  Pallas kernels  21.4 us (13%)
  waiting for transfers between devices  10.6 us (6%)
    all_to_all x2, blocking collectives, exchange(): lax.all_to_all(values, axis, split_axis=0, concat_axis=0, tiled=True, axi...  59.7 us
    all_gather x1, blocking collectives, shards(): gathered = lax.all_gather(packed, 'far', axis=0, tiled=False)  33.2 us
    all_to_all x3, starting transfers between devices, exchange(): lax.all_to_all(values, axis, split_axis=0, concat_axis=0, tiled=True, axi...  24.9 us
    all_gather x1, blocking collectives, shards(): cot = lax.all_gather(cotangent, 'col', axis=0, tiled=True)  11.2 us
    all_to_all x3, waiting for transfers between devices, exchange(): lax.all_to_all(values, axis, split_axis=0, concat_axis=0, tiled=True, axi...  10.6 us
    pallas_call x1, Pallas kernels, shards(): call(middle_body, [smem(), smem(), vmem()] + [away()] * 5, [((FEAT, ROWS)...  8.87 us
    pallas_call x1, Pallas kernels, shards(): call(forward_body, [smem(), vmem()] + [away()] * 4, [((COLS, FEAT, ROWS),...  5.43 us
  transfers between devices with their start and end apart: 3, of which 3 were waited for; matrix products, arithmetic and copies ran while one was open for 1% of the time, Pallas kernels for 1%

profile of v2, /device:TPU:1, one launch (start us, length us, event | category | flops | bytes accessed | tf_op | source)
XLA Modules:
  0.0 164.0 jit_solution(861923963849569279)
XLA Ops:
  0.6 1.1 shard_map.121
  1.7 33.2 %all-gather = bf16[2176,128]{1,0:T(8,128)(2,1)S(1)} all-gather(bf16[272,128]{1,0:T(8,128)(2,1)S(1)} %shard_map.121), channel_id=2, replica_groups=mesh['far'=8,'near'=16,'col'=4] {'far'}, dimensions={0}, use_global_device_ids=true | all-gather | bytes 626688 | tf_op jit(solution)/shard_map/all_gather | solution.py:372
  34.9 0.1 dynamic-slice_convert_fusion
  35.0 1.7 %shard_map.122 = bf16[16,272,128]{2,1,0:T(8,128)(2,1)} custom-call(s32[8,16]{1,0:T(8,128)S(1)} %bitcast.19, bf16[8,272,128]{2,1,0:T(8,128)(2,1)S(1)} %bitcast.17), custom_call_target="tpu_custom_call" | custom-call | flops 1000000 | bytes 1000000 | tf_op jit(solution)/shard_map/pallas_call | solution.py:377
  36.7 0.0 copy-start
  36.7 0.0 copy-start.1
  36.8 11.2 %all-to-all-start = ((bf16[16,272,128]{2,1,0:T(8,128)(2,1)}), bf16[16,272,128]{2,1,0:T(8,128)(2,1)S(1)}, u32[]{:S(2)}, u32[]{:S(2)}) async-start(bf16[16,272,128]{2,1,0:T(8,128)(2,1)} %shard_map.122), calls=%async_computation | async-start | bytes 2228224 | tf_op jit(solution)/shard_map/all_to_all | solution.py:339
  48.0 0.0 copy-start.2
  48.7 0.0 copy-done
  48.7 0.1 reshape.28
  48.8 0.9 copy.13
  49.6 0.0 copy-done.1
  49.6 11.2 %all_gather.11.cot_far = bf16[256,512]{1,0:T(8,128)(2,1)} all-gather(bf16[64,512]{1,0:T(8,128)(2,1)S(1)} %copy-done.1), channel_id=1, replica_groups=mesh['far'=8,'near'=16,'col'=4] {'col'}, dimensions={0}, use_global_device_ids=true | all-gather | bytes 327680 | tf_op jit(solution)/shard_map/all_gather | solution.py:385
  60.8 0.0 copy-done.2
  60.8 0.9 all-to-all-done.came
  61.8 5.4 %shard_map.123 = bf16[4,64,512]{2,1,0:T(8,128)(2,1)} custom-call(s32[128]{0:T(128)S(1)} %compare_select_fusion.target, bf16[16,272,128]{2,1,0:T(8,128)(2,1)S(1)} %all-to-all-done.came, bf16[128,64,128]{2,1,0:T(8,128)(2,1)} %remote_far.3, bf16[64,512]{1,0:T(8,128)(2,1)} %feats_far.1, bf16[4,128,128]{2,1,0:T(8,128)(2,1)} %local_far.3, bf16[256,512]{1,0:T(8,128)(2,1)} %bitcast.21), custom_call_target="tpu_custom_call" | custom-call | flops 1000000 | bytes 1000000 | tf_op jit(solution)/shard_map/pallas_call | solution.py:387
  67.2 4.1 %all-to-all-start.1 = ((bf16[4,64,512]{2,1,0:T(8,128)(2,1)}), bf16[4,64,512]{2,1,0:T(8,128)(2,1)S(1)}, u32[]{:S(2)}, u32[]{:S(2)}) async-start(bf16[4,64,512]{2,1,0:T(8,128)(2,1)} %shard_map.123), calls=%async_computation.1 | async-start | bytes 524288 | tf_op jit(solution)/shard_map/all_to_all | solution.py:339
  71.3 5.5 %all-to-all-done.1 = bf16[4,64,512]{2,1,0:T(8,128)(2,1)S(1)} async-done(((bf16[4,64,512]{2,1,0:T(8,128)(2,1)}), bf16[4,64,512]{2,1,0:T(8,128)(2,1)S(1)}, u32[]{:S(2)}, u32[]{:S(2)}) %all-to-all-start.1) | async-done | bytes 262176 | tf_op jit(solution)/shard_map/all_to_all | solution.py:339
  76.8 8.9 %shard_map.124 = (bf16[64,512]{1,0:T(8,128)(2,1)}, bf16[16,272,128]{2,1,0:T(8,128)(2,1)}, f32[64,512]{1,0:T(8,128)S(1)}) custom-call(s32[1]{0:T(128)} %bitcast.col, s32[128]{0:T(128)S(1)} %compare_select_fusion.target, bf16[256,512]{1,0:T(8,128)(2,1)S(1)} %bitcast.18, bf16[256,512]{1,0:T(8,128)(2,1)} %all_gather.11.cot_far, bf16[256,256]{1,0:T(8,128)(2,1)} %weight_far.1, ...), custom_call_target="tpu_custom_call" | custom-call | flops 1000000 | bytes 1000000 | tf_op jit(solution)/shard_map/pallas_call | solution.py:406
  85.7 23.6 %all_to_all.25.came = bf16[16,272,128]{2,1,0:T(8,128)(2,1)S(1)} all-to-all(bf16[16,272,128]{2,1,0:T(8,128)(2,1)} %get-tuple-element.15), channel_id=1, replica_groups={{28,0,48,12,36,56,20,40,4,60,24,8,52,32,16,44},{29,1,49,13,37,57,21,41,..., dimensions={0} | all-to-all | bytes 2228224 | tf_op jit(solution)/shard_map/all_to_all | solution.py:339
  109.3 1.9 %shard_map.125 = bf16[8,272,128]{2,1,0:T(8,128)(2,1)} custom-call(s32[8,16]{1,0:T(8,128)S(1)} %bitcast.20, bf16[16,272,128]{2,1,0:T(8,128)(2,1)S(1)} %all_to_all.25.came), custom_call_target="tpu_custom_call" | custom-call | flops 1000000 | bytes 1000000 | tf_op jit(solution)/shard_map/pallas_call | solution.py:426
  111.2 36.1 %all_to_all.26.came = bf16[8,272,128]{2,1,0:T(8,128)(2,1)S(1)} all-to-all(bf16[8,272,128]{2,1,0:T(8,128)(2,1)} %shard_map.125), channel_id=1, replica_groups=mesh['far'=8,'near'=16,'col'=4] {'far'}, dimensions={0} | all-to-all | bytes 1114112 | tf_op jit(solution)/shard_map/all_to_all | solution.py:339
  147.4 0.6 shard_map.127
  148.0 9.6 %all-to-all-start.4 = ((f32[16,8,128]{2,1,0:T(8,128)}), f32[16,8,128]{2,1,0:T(8,128)S(1)}, u32[]{:S(2)}, u32[]{:S(2)}) async-start(f32[16,8,128]{2,1,0:T(8,128)} %shard_map.127), calls=%async_computation.4 | async-start | bytes 131072 | tf_op jit(solution)/shard_map/all_to_all | solution.py:339
  157.6 1.7 %shard_map.126 = bf16[64,512]{1,0:T(8,128)(2,1)} custom-call(s32[1,2]{1,0:T(1,128)} %hubs.3, bf16[8,272,128]{2,1,0:T(8,128)(2,1)S(1)} %all_to_all.26.came, f32[64,512]{1,0:T(8,128)S(1)} %get-tuple-element.16.own_grad), custom_call_target="tpu_custom_call" | custom-call | flops 1000000 | bytes 1000000 | tf_op jit(solution)/shard_map/pallas_call | solution.py:439
  159.3 4.1 %all-to-all-done.4 = f32[16,8,128]{2,1,0:T(8,128)S(1)} async-done(((f32[16,8,128]{2,1,0:T(8,128)}), f32[16,8,128]{2,1,0:T(8,128)S(1)}, u32[]{:S(2)}, u32[]{:S(2)}) %all-to-all-start.4) | async-done | bytes 65568 | tf_op jit(solution)/shard_map/all_to_all | solution.py:339
  163.4 0.6 copy.16
  (2 shorter events, 0.0 us)
Async XLA Ops:
  36.7 11.9 %copy-start = (bf16[256,512]{1,0:T(8,128)(2,1)S(1)}, bf16[256,512]{1,0:T(8,128)(2,1)}, u32[]{:S(2)}) copy-start(bf16[256,512]{1,0:T(8,128)(2,1)} %param.17) | copy-start | bytes 786436
  36.7 12.9 %copy-start.1 = (bf16[64,512]{1,0:T(8,128)(2,1)S(1)}, bf16[64,512]{1,0:T(8,128)(2,1)}, u32[]{:S(2)}) copy-start(bf16[64,512]{1,0:T(8,128)(2,1)} %param.19) | copy-start | bytes 196612
  36.8 25.0 %all-to-all-start = ((bf16[16,272,128]{2,1,0:T(8,128)(2,1)}), bf16[16,272,128]{2,1,0:T(8,128)(2,1)S(1)}, u32[]{:S(2)}, u32[]{:S(2)}) async-start(bf16[16,272,128]{2,1,0:T(8,128)(2,1)} %shard_map.122), calls=%async_computation | async-start | bytes 2228224 | tf_op jit(solution)/shard_map/all_to_all | solution.py:339
  48.0 12.8 %copy-start.2 = (s32[1,128]{1,0:T(1,128)S(1)}, s32[1,128]{1,0:T(1,128)}, u32[]{:S(2)}) copy-start(s32[1,128]{1,0:T(1,128)} %param.12) | copy-start | bytes 1540
  67.2 9.6 %all-to-all-start.1 = ((bf16[4,64,512]{2,1,0:T(8,128)(2,1)}), bf16[4,64,512]{2,1,0:T(8,128)(2,1)S(1)}, u32[]{:S(2)}, u32[]{:S(2)}) async-start(bf16[4,64,512]{2,1,0:T(8,128)(2,1)} %shard_map.123), calls=%async_computation.1 | async-start | bytes 524288 | tf_op jit(solution)/shard_map/all_to_all | solution.py:339
  148.0 15.4 %all-to-all-start.4 = ((f32[16,8,128]{2,1,0:T(8,128)}), f32[16,8,128]{2,1,0:T(8,128)S(1)}, u32[]{:S(2)}, u32[]{:S(2)}) async-start(f32[16,8,128]{2,1,0:T(8,128)} %shard_map.127), calls=%async_computation.4 | async-start | bytes 131072 | tf_op jit(solution)/shard_map/all_to_all | solution.py:339

commit v3 on v2

--- a/solution.py
+++ b/solution.py
@@ -77,14 +77,6 @@
     return pltpu.with_memory_space_constraint(value, pltpu.HBM)
 
 
-def part(ref, s):
-    return ref.at[:, pl.ds(pl.multiple_of(s * HALF, HALF), HALF), :]
-
-
-def tiles_of(ref, s):
-    return ref.at[pl.ds(s * NEAR, NEAR)]
-
-
 def pack_body(hubs, feats, wanted, out):
     for k in range(PIECES):
         low = feats[:HALF, k * PIECE : (k + 1) * PIECE]
@@ -134,39 +126,24 @@
 def forward_body(
     target,
     came,
-    remote_far,
+    remote,
     feats_far,
     local_far,
     adj_far,
     out,
-    remote,
     feats,
     local,
     adj,
-    own,
     value,
     total,
     sems,
-    remote_sems,
     out_sems,
 ):
-    pairs = [(feats_far, feats), (local_far, local)]
-    first = start_all(pairs, sems)
-    start_all([(tiles_of(remote_far, s), tiles_of(remote, s)) for s in range(FAR)], remote_sems)
-    last = pltpu.make_async_copy(adj_far, adj, sems.at[2])
-    last.start()
+    copies = start_all([(feats_far, feats), (local_far, local), (adj_far, adj)], sems)
     total[...] = jnp.zeros_like(total)
-    for copy in first:
-        copy.wait()
-    for b in range(BLOCKS):
-        cols = slice(b * BLK, (b + 1) * BLK)
-        own[:, cols] = dot(feats[:, cols], local[b])
 
     def step(s, carry):
         start = pl.multiple_of(s * HALF, HALF)
-        pltpu.make_async_copy(
-            tiles_of(remote_far, s), tiles_of(remote, s), remote_sems.at[s]
-        ).wait()
         for first in range(0, NEAR, 8):
             parts = []
             for n in range(first, first + 8):
@@ -178,7 +155,8 @@
         return carry
 
     lax.fori_loop(0, FAR, step, 0)
-    last.wait()
+    for copy in copies:
+        copy.wait()
     hub_rows = jnp.concatenate([came[SLOT[n], FAR * HALF :, :][:8] for n in range(NEAR)], axis=0)
     hub = (
         dot(hub_rows, adj[: PEERS, :], TN)[:FEAT] + dot(hub_rows, adj[PEERS:, :], TN)[FEAT:]
@@ -186,7 +164,8 @@
     for b in range(BLOCKS):
         cols = slice(b * BLK, (b + 1) * BLK)
         tiles = jnp.concatenate([total[b, :, :BLK], total[b, :, BLK:]], axis=0)
-        value[:, cols] = (own[:, cols] + tiles + hub[:, cols]).astype(BF)
+        own = dot(feats[:, cols], local[b])
+        value[:, cols] = (own + tiles + hub[:, cols]).astype(BF)
     for copy in start_all([(value, out.at[c]) for c in range(COLS)], out_sems):
         copy.wait()
 
@@ -195,36 +174,25 @@
     col,
     target,
     agg,
+    remote,
+    weight_far,
     cot_far,
-    weight_far,
-    remote_far,
     local_far,
     adj_far,
     output,
     back,
     own_grad,
+    weight,
     cot,
-    weight,
-    remote,
     local,
     adj,
     grad,
     pick,
-    held,
     sems,
-    remote_sems,
-    back_sems,
 ):
-    pairs = [
-        (weight_far, weight),
-        (cot_far, cot),
-        (local_far, local),
-        (adj_far, adj),
-    ]
+    pairs = [(weight_far, weight), (cot_far, cot), (local_far, local), (adj_far, adj)]
     copies = start_all(pairs, sems)
-    start_all([(tiles_of(remote_far, s), tiles_of(remote, s)) for s in range(FAR)], remote_sems)
-    for copy in copies[:2]:
-        copy.wait()
+    copies[0].wait()
     scale = 0.7978845608028654
     mine = pl.multiple_of(col[0] * FEAT, FEAT)
     for c in range(COLS):
@@ -235,6 +203,8 @@
         slope = half + 0.5 * pre * (1.0 - bend * bend) * (
             scale * (1.0 + 3.0 * 0.044715 * square)
         )
+        if c == 0:
+            copies[1].wait()
         grad[c * FEAT : (c + 1) * FEAT, :] = (
             cot[c * FEAT : (c + 1) * FEAT, :].astype(F32) * slope
         ).astype(BF)
@@ -245,63 +215,51 @@
 
     grad_agg = dot(weight[pl.ds(mine, FEAT), :], grad[...]).astype(BF)
     weight_grad = dot(agg[pl.ds(mine, FEAT), :], grad[...], NT)
-    for copy in copies[2:]:
-        copy.wait()
+    copies[2].wait()
     for b in range(BLOCKS):
         cols = slice(b * BLK, (b + 1) * BLK)
-        pick[b] = jnp.concatenate([grad_agg[:HALF, cols], grad_agg[HALF:, cols]], axis=1)
+        pick[b] = grad_agg[:, cols]
         own_grad[:, cols] = dot(grad_agg[:, cols], local[b], NT)
-    pick[BLOCKS] = jnp.zeros((HALF, 2 * BLK), BF)
+    copies[3].wait()
+    pick[BLOCKS] = jnp.zeros((FEAT, BLK), BF)
     hub = dot(adj[...], grad_agg, NT)
     hub = jnp.concatenate([hub[:PEERS], hub[PEERS:]], axis=1)
     for n in range(NEAR):
         m = ORDER[n]
         i, j = m // 2, m % 2
         tile = weight_grad[i * 8 : (i + 1) * 8, j * 128 : (j + 1) * 128]
-        held[n, FAR * HALF :, :] = jnp.concatenate([hub[m * 8 : (m + 1) * 8], tile], axis=0).astype(BF)
-    ends = slice(FAR * HALF, NEAR_ROWS)
-    last = pltpu.make_async_copy(held.at[:, ends, :], back.at[:, ends, :], sems.at[4])
-    last.start()
+        back[n, FAR * HALF :, :] = jnp.concatenate([hub[m * 8 : (m + 1) * 8], tile], axis=0).astype(BF)
 
     def step(s, carry):
         start = pl.multiple_of(s * HALF, HALF)
-        pltpu.make_async_copy(
-            tiles_of(remote_far, s), tiles_of(remote, s), remote_sems.at[s]
-        ).wait()
         for n in range(NEAR):
             q = s * NEAR + ORDER[n]
-            tile = dot(pick[target[q]], twice(remote[q]), NT)
-            held[n, pl.ds(start, HALF), :] = tile.astype(BF)
-        pltpu.make_async_copy(part(held, s), part(back, s), back_sems.at[s]).start()
+            tile = dot(pick[target[q]], remote[q], NT)
+            tile = jnp.concatenate([tile[:HALF], tile[HALF:]], axis=1)
+            back[n, pl.ds(start, HALF), :] = tile.astype(BF)
         return carry
 
     lax.fori_loop(0, FAR, step, 0)
-    last.wait()
-    for s in range(FAR):
-        pltpu.make_async_copy(part(held, s), part(back, s), back_sems.at[s]).wait()
-
-
-def gather_body(piece, came, out, held, total, out_sems):
+
+
+def gather_body(piece, came, out, total):
     total[...] = jnp.zeros_like(total)
     extra = jnp.zeros((16, 128), F32)
     for n in range(NEAR):
         extra += came[n, FAR * HALF :, :].astype(F32)
     for s in range(FAR):
         hub = jnp.broadcast_to(extra[s : s + 1], (8, 128))
-        held[s, DENSE:, :] = jnp.concatenate([hub, extra[8:]], axis=0).astype(BF)
+        out[s, DENSE:, :] = jnp.concatenate([hub, extra[8:]], axis=0).astype(BF)
 
     def step(s, carry):
         start = pl.multiple_of(s * HALF, HALF)
         for n in range(NEAR):
             at = pl.multiple_of(piece[s, ORDER[n]] * HALF, HALF)
             total[s, pl.ds(at, HALF), :] += came[n, pl.ds(start, HALF), :].astype(F32)
-        held[s, :DENSE, :] = total[s].astype(BF)
-        pltpu.make_async_copy(held.at[s], out.at[s], out_sems.at[s]).start()
+        out[s, :DENSE, :] = total[s].astype(BF)
         return carry
 
     lax.fori_loop(0, FAR, step, 0)
-    for s in range(FAR):
-        pltpu.make_async_copy(held.at[s], out.at[s], out_sems.at[s]).wait()
 
 
 def chunk_body(came, chunk):
@@ -384,54 +342,41 @@
     came = exchange(picked, "near", ORDER)
     cot = lax.all_gather(cotangent, "col", axis=0, tiled=True)
     came, cot = lax.optimization_barrier((came, cot))
+    small = [pltpu.VMEM((BLOCKS, BLK, BLK), BF), pltpu.VMEM((2 * PEERS, ROWS), BF)]
     (agg,) = call(
         forward_body,
-        [smem(), vmem()] + [away()] * 4,
+        [smem(), vmem(), vmem()] + [away()] * 3,
         [((COLS, FEAT, ROWS), BF, away())],
-        [
-            pltpu.VMEM((PEERS, PIECE, BLK), BF),
-            pltpu.VMEM((FEAT, ROWS), BF),
-            pltpu.VMEM((BLOCKS, BLK, BLK), BF),
-            pltpu.VMEM((2 * PEERS, ROWS), BF),
-            pltpu.VMEM((FEAT, ROWS), F32),
+        [pltpu.VMEM((FEAT, ROWS), BF)]
+        + small
+        + [
             pltpu.VMEM((FEAT, ROWS), BF),
             pltpu.VMEM((BLOCKS + 1, HALF, 2 * BLK), F32),
             pltpu.SemaphoreType.DMA((3,)),
-            pltpu.SemaphoreType.DMA((FAR,)),
             pltpu.SemaphoreType.DMA((COLS,)),
         ],
-    )(target, came, *map(stay, (remote_values, features, local_values, adj)))
-    agg = exchange(agg, "col").reshape(COLS * FEAT, ROWS)
+    )(target, came, remote_values, *map(stay, (features, local_values, adj)))
     wide = (COLS * FEAT, ROWS)
+    agg = exchange(agg, "col").reshape(wide)
     output, back, own_grad = call(
         middle_body,
-        [smem(), smem(), vmem()] + [away()] * 5,
-        [((FEAT, ROWS), BF, vmem()), (near_all, BF, away()), ((FEAT, ROWS), F32, vmem())],
-        [
+        [smem(), smem(), vmem(), vmem()] + [away()] * 4,
+        [((FEAT, ROWS), BF, vmem()), (near_all, BF, vmem()), ((FEAT, ROWS), F32, vmem())],
+        [pltpu.VMEM((COLS * FEAT, COLS * FEAT), BF), pltpu.VMEM(wide, BF)]
+        + small
+        + [
             pltpu.VMEM(wide, BF),
-            pltpu.VMEM((COLS * FEAT, COLS * FEAT), BF),
-            pltpu.VMEM((PEERS, PIECE, BLK), BF),
-            pltpu.VMEM((BLOCKS, BLK, BLK), BF),
-            pltpu.VMEM((2 * PEERS, ROWS), BF),
-            pltpu.VMEM(wide, BF),
-            pltpu.VMEM((BLOCKS + 1, HALF, 2 * BLK), BF),
-            pltpu.VMEM(near_all, BF),
-            pltpu.SemaphoreType.DMA((5,)),
-            pltpu.SemaphoreType.DMA((FAR,)),
-            pltpu.SemaphoreType.DMA((FAR,)),
+            pltpu.VMEM((BLOCKS + 1, FEAT, BLK), BF),
+            pltpu.SemaphoreType.DMA((4,)),
         ],
-    )(col, target, agg, *map(stay, (cot, weight, remote_values, local_values, adj)))
+    )(col, target, agg, remote_values, *map(stay, (weight, cot, local_values, adj)))
     back = exchange(back, "near", ORDER)
     far_all = (FAR, BACK_ROWS, 128)
     (sums,) = call(
         gather_body,
         [smem(), vmem()],
-        [(far_all, BF, away())],
-        [
-            pltpu.VMEM(far_all, BF),
-            pltpu.VMEM((FAR, DENSE, 128), F32),
-            pltpu.SemaphoreType.DMA((FAR,)),
-        ],
+        [(far_all, BF, vmem())],
+        [pltpu.VMEM((FAR, DENSE, 128), F32)],
     )(piece, back)
     sums = exchange(sums, "far")
     (chunk,) = call(chunk_body, [vmem()], [((NEAR, 8, 128), F32, vmem())])(sums)

time: 165 us -> 160 us (0.970)
  Pallas kernels: 21.4 us -> 16.9 us
    pallas_call x3, Pallas kernels: 16.2 us -> 11.7 us  [the longest x1 6.6 us: shards(): call(middle_body, [smem(), smem(), vmem(), vmem()] + [away()] * 4, [((FEA...]
  transfers between devices with their start and end apart: 3 -> 3, of which waited for: 3 -> 2; matrix products, arithmetic and copies ran while one was open for 1% -> 1% of each run, Pallas kernels for 1% -> 1%
where the time goes in v3:
time: 160 us
  blocking collectives  104 us (65%)
  starting transfers between devices  25.1 us (16%)
  Pallas kernels  16.9 us (11%)
  waiting for transfers between devices  9.71 us (6%)
  local copies, waits for them, and re-layouts  2.57 us (2%)
    all_to_all x2, blocking collectives, exchange(): lax.all_to_all(values, axis, split_axis=0, concat_axis=0, tiled=True, axi...  59.7 us
    all_gather x1, blocking collectives, shards(): gathered = lax.all_gather(packed, 'far', axis=0, tiled=False)  33.2 us
    all_to_all x3, starting transfers between devices, exchange(): lax.all_to_all(values, axis, split_axis=0, concat_axis=0, tiled=True, axi...  25.1 us
    all_gather x1, blocking collectives, shards(): cot = lax.all_gather(cotangent, 'col', axis=0, tiled=True)  11 us
    all_to_all x3, waiting for transfers between devices, exchange(): lax.all_to_all(values, axis, split_axis=0, concat_axis=0, tiled=True, axi...  9.71 us
    pallas_call x1, Pallas kernels, shards(): call(middle_body, [smem(), smem(), vmem(), vmem()] + [away()] * 4, [((FEA...  6.6 us
    pallas_call x1, Pallas kernels, shards(): call(forward_body, [smem(), vmem(), vmem()] + [away()] * 3, [((COLS, FEAT...  3.86 us
  transfers between devices with their start and end apart: 3, of which 2 were waited for; matrix products, arithmetic and copies ran while one was open for 1% of the time, Pallas kernels for 1%

profile of v3, /device:TPU:1, one launch (start us, length us, event | category | flops | bytes accessed | tf_op | source)
XLA Modules:
  0.0 159.5 jit_solution(9385055172951079847)
XLA Ops:
  0.6 1.1 shard_map.121
  1.7 33.2 %all-gather = bf16[2176,128]{1,0:T(8,128)(2,1)S(1)} all-gather(bf16[272,128]{1,0:T(8,128)(2,1)S(1)} %shard_map.121), channel_id=2, replica_groups=mesh['far'=8,'near'=16,'col'=4] {'far'}, dimensions={0}, use_global_device_ids=true | all-gather | bytes 626688 | tf_op jit(solution)/shard_map/all_gather | solution.py:330
  34.9 0.1 dynamic-slice_convert_fusion
  35.0 1.7 %shard_map.122 = bf16[16,272,128]{2,1,0:T(8,128)(2,1)} custom-call(s32[8,16]{1,0:T(8,128)S(1)} %bitcast.19, bf16[8,272,128]{2,1,0:T(8,128)(2,1)S(1)} %bitcast.17), custom_call_target="tpu_custom_call" | custom-call | flops 1000000 | bytes 1000000 | tf_op jit(solution)/shard_map/pallas_call | solution.py:335
  36.7 0.0 copy-start.1
  36.7 0.0 copy-start
  36.8 11.2 %all-to-all-start = ((bf16[16,272,128]{2,1,0:T(8,128)(2,1)}), bf16[16,272,128]{2,1,0:T(8,128)(2,1)S(1)}, u32[]{:S(2)}, u32[]{:S(2)}) async-start(bf16[16,272,128]{2,1,0:T(8,128)(2,1)} %shard_map.122), calls=%async_computation | async-start | bytes 2228224 | tf_op jit(solution)/shard_map/all_to_all | solution.py:297
  48.0 0.0 copy-start.2
  48.7 1.1 reshape.28
  49.7 0.9 copy.13
  50.6 0.0 copy-done.1
  50.6 11.0 %all_gather.11.cot_far = bf16[256,512]{1,0:T(8,128)(2,1)} all-gather(bf16[64,512]{1,0:T(8,128)(2,1)S(1)} %copy-done.1), channel_id=1, replica_groups=mesh['far'=8,'near'=16,'col'=4] {'col'}, dimensions={0}, use_global_device_ids=true | all-gather | bytes 327680 | tf_op jit(solution)/shard_map/all_gather | solution.py:343
  61.6 0.0 copy-done.2
  61.6 0.0 all-to-all-done.came
  61.7 0.0 copy-done
  61.7 3.9 %shard_map.123 = bf16[4,64,512]{2,1,0:T(8,128)(2,1)} custom-call(s32[128]{0:T(128)S(1)} %compare_select_fusion.target, bf16[16,272,128]{2,1,0:T(8,128)(2,1)S(1)} %all-to-all-done.came, bf16[128,64,128]{2,1,0:T(8,128)(2,1)S(1)} %copy-done, bf16[64,512]{1,0:T(8,128)(2,1)} %feats_far.1, bf16[4,128,128]{2,1,0:T(8,128)(2,1)} %local_far.3, bf16[256,512]{1,0:T(8,128)(2,1)} %bitcast.21), custom_call_target="tpu_custom_call" | custom-call | flops 1000000 | bytes 1000000 | tf_op jit(solution)/shard_map/pallas_call | solution.py:346
  65.5 4.2 %all-to-all-start.1 = ((bf16[4,64,512]{2,1,0:T(8,128)(2,1)}), bf16[4,64,512]{2,1,0:T(8,128)(2,1)S(1)}, u32[]{:S(2)}, u32[]{:S(2)}) async-start(bf16[4,64,512]{2,1,0:T(8,128)(2,1)} %shard_map.123), calls=%async_computation.1 | async-start | bytes 524288 | tf_op jit(solution)/shard_map/all_to_all | solution.py:297
  69.8 5.5 %all-to-all-done.1 = bf16[4,64,512]{2,1,0:T(8,128)(2,1)S(1)} async-done(((bf16[4,64,512]{2,1,0:T(8,128)(2,1)}), bf16[4,64,512]{2,1,0:T(8,128)(2,1)S(1)}, u32[]{:S(2)}, u32[]{:S(2)}) %all-to-all-start.1) | async-done | bytes 262176 | tf_op jit(solution)/shard_map/all_to_all | solution.py:297
  75.3 6.6 %shard_map.124 = (bf16[64,512]{1,0:T(8,128)(2,1)}, bf16[16,272,128]{2,1,0:T(8,128)(2,1)S(1)}, f32[64,512]{1,0:T(8,128)S(1)}) custom-call(s32[1]{0:T(128)} %bitcast.col, s32[128]{0:T(128)S(1)} %compare_select_fusion.target, bf16[256,512]{1,0:T(8,128)(2,1)S(1)} %bitcast.18, bf16[128,64,128]{2,1,0:T(8,128)(2,1)S(1)} %copy-done, bf16[256,256]{1,0:T(8,128)(2,1)} %weight_far.1, ...), custom_call_target="tpu_custom_call" | custom-call | flops 1000000 | bytes 1000000 | tf_op jit(solution)/shard_map/pallas_call | solution.py:361
  81.9 23.8 %all_to_all.25.came = bf16[16,272,128]{2,1,0:T(8,128)(2,1)S(1)} all-to-all(bf16[16,272,128]{2,1,0:T(8,128)(2,1)S(1)} %get-tuple-element.15), channel_id=1, replica_groups={{28,0,48,12,36,56,20,40,4,60,24,8,52,32,16,44},{29,1,49,13,37,57,21,41,..., dimensions={0} | all-to-all | bytes 2228224 | tf_op jit(solution)/shard_map/all_to_all | solution.py:297
  105.7 1.3 shard_map.125
  106.9 35.9 %all_to_all.26.came = bf16[8,272,128]{2,1,0:T(8,128)(2,1)S(1)} all-to-all(bf16[8,272,128]{2,1,0:T(8,128)(2,1)S(1)} %shard_map.125), channel_id=1, replica_groups=mesh['far'=8,'near'=16,'col'=4] {'far'}, dimensions={0} | all-to-all | bytes 1114112 | tf_op jit(solution)/shard_map/all_to_all | solution.py:297
  142.9 0.6 shard_map.127
  143.5 9.6 %all-to-all-start.4 = ((f32[16,8,128]{2,1,0:T(8,128)}), f32[16,8,128]{2,1,0:T(8,128)S(1)}, u32[]{:S(2)}, u32[]{:S(2)}) async-start(f32[16,8,128]{2,1,0:T(8,128)} %shard_map.127), calls=%async_computation.4 | async-start | bytes 131072 | tf_op jit(solution)/shard_map/all_to_all | solution.py:297
  153.1 1.7 %shard_map.126 = bf16[64,512]{1,0:T(8,128)(2,1)} custom-call(s32[1,2]{1,0:T(1,128)} %hubs.3, bf16[8,272,128]{2,1,0:T(8,128)(2,1)S(1)} %all_to_all.26.came, f32[64,512]{1,0:T(8,128)S(1)} %get-tuple-element.16.own_grad), custom_call_target="tpu_custom_call" | custom-call | flops 1000000 | bytes 1000000 | tf_op jit(solution)/shard_map/pallas_call | solution.py:384
  154.8 4.1 %all-to-all-done.4 = f32[16,8,128]{2,1,0:T(8,128)S(1)} async-done(((f32[16,8,128]{2,1,0:T(8,128)}), f32[16,8,128]{2,1,0:T(8,128)S(1)}, u32[]{:S(2)}, u32[]{:S(2)}) %all-to-all-start.4) | async-done | bytes 65568 | tf_op jit(solution)/shard_map/all_to_all | solution.py:297
  158.9 0.6 copy.16
  (2 shorter events, 0.0 us)
Async XLA Ops:
  36.7 13.9 %copy-start.1 = (bf16[64,512]{1,0:T(8,128)(2,1)S(1)}, bf16[64,512]{1,0:T(8,128)(2,1)}, u32[]{:S(2)}) copy-start(bf16[64,512]{1,0:T(8,128)(2,1)} %param.19) | copy-start | bytes 196612
  36.7 24.9 %copy-start = (bf16[128,64,128]{2,1,0:T(8,128)(2,1)S(1)}, bf16[128,64,128]{2,1,0:T(8,128)(2,1)}, u32[]{:S(2)}) copy-start(bf16[128,64,128]{2,1,0:T(8,128)(2,1)} %remote.3) | copy-start | bytes 6291460
  36.8 24.9 %all-to-all-start = ((bf16[16,272,128]{2,1,0:T(8,128)(2,1)}), bf16[16,272,128]{2,1,0:T(8,128)(2,1)S(1)}, u32[]{:S(2)}, u32[]{:S(2)}) async-start(bf16[16,272,128]{2,1,0:T(8,128)(2,1)} %shard_map.122), calls=%async_computation | async-start | bytes 2228224 | tf_op jit(solution)/shard_map/all_to_all | solution.py:297
  48.0 13.6 %copy-start.2 = (s32[1,128]{1,0:T(1,128)S(1)}, s32[1,128]{1,0:T(1,128)}, u32[]{:S(2)}) copy-start(s32[1,128]{1,0:T(1,128)} %param.12) | copy-start | bytes 1540
  65.5 9.8 %all-to-all-start.1 = ((bf16[4,64,512]{2,1,0:T(8,128)(2,1)}), bf16[4,64,512]{2,1,0:T(8,128)(2,1)S(1)}, u32[]{:S(2)}, u32[]{:S(2)}) async-start(bf16[4,64,512]{2,1,0:T(8,128)(2,1)} %shard_map.123), calls=%async_computation.1 | async-start | bytes 524288 | tf_op jit(solution)/shard_map/all_to_all | solution.py:297
  143.5 15.4 %all-to-all-start.4 = ((f32[16,8,128]{2,1,0:T(8,128)}), f32[16,8,128]{2,1,0:T(8,128)S(1)}, u32[]{:S(2)}, u32[]{:S(2)}) async-start(f32[16,8,128]{2,1,0:T(8,128)} %shard_map.127), calls=%async_computation.4 | async-start | bytes 131072 | tf_op jit(solution)/shard_map/all_to_all | solution.py:297

commit v4 on v3

--- a/solution.py
+++ b/solution.py
@@ -116,6 +116,13 @@
         copy.wait()
 
 
+def hub_places():
+    hub = lax.broadcasted_iota(jnp.int32, (2 * PEERS, 2 * PEERS), 0)
+    place = lax.broadcasted_iota(jnp.int32, (2 * PEERS, 2 * PEERS), 1)
+    owner = ((place & 7) << 5) + (((place >> 3) & 15) << 1) + (place >> 7)
+    return (hub == owner).astype(BF)
+
+
 def twice(tile):
     zero = jnp.zeros_like(tile)
     return jnp.concatenate(
@@ -157,10 +164,10 @@
     lax.fori_loop(0, FAR, step, 0)
     for copy in copies:
         copy.wait()
-    hub_rows = jnp.concatenate([came[SLOT[n], FAR * HALF :, :][:8] for n in range(NEAR)], axis=0)
-    hub = (
-        dot(hub_rows, adj[: PEERS, :], TN)[:FEAT] + dot(hub_rows, adj[PEERS:, :], TN)[FEAT:]
-    )
+    rows = jnp.concatenate([came[SLOT[n], FAR * HALF :, :][:8] for n in range(NEAR)], axis=0)
+    rows = jnp.concatenate([rows[:, :FEAT], rows[:, FEAT:]], axis=0)
+    hubs = dot(hub_places(), rows).astype(BF)
+    hub = dot(hubs, adj[...], TN)
     for b in range(BLOCKS):
         cols = slice(b * BLK, (b + 1) * BLK)
         tiles = jnp.concatenate([total[b, :, :BLK], total[b, :, BLK:]], axis=0)
@@ -222,7 +229,8 @@
         own_grad[:, cols] = dot(grad_agg[:, cols], local[b], NT)
     copies[3].wait()
     pick[BLOCKS] = jnp.zeros((FEAT, BLK), BF)
-    hub = dot(adj[...], grad_agg, NT)
+    hub = dot(adj[...], grad_agg, NT).astype(BF)
+    hub = dot(hub_places(), hub, TN)
     hub = jnp.concatenate([hub[:PEERS], hub[PEERS:]], axis=1)
     for n in range(NEAR):
         m = ORDER[n]
@@ -242,32 +250,36 @@
     lax.fori_loop(0, FAR, step, 0)
 
 
-def gather_body(piece, came, out, total):
+def gather_body(piece, came, out, chunk, held, total, sems):
     total[...] = jnp.zeros_like(total)
     extra = jnp.zeros((16, 128), F32)
     for n in range(NEAR):
         extra += came[n, FAR * HALF :, :].astype(F32)
-    for s in range(FAR):
-        hub = jnp.broadcast_to(extra[s : s + 1], (8, 128))
-        out[s, DENSE:, :] = jnp.concatenate([hub, extra[8:]], axis=0).astype(BF)
+    chunk[...] = extra[8:]
 
     def step(s, carry):
         start = pl.multiple_of(s * HALF, HALF)
         for n in range(NEAR):
             at = pl.multiple_of(piece[s, ORDER[n]] * HALF, HALF)
             total[s, pl.ds(at, HALF), :] += came[n, pl.ds(start, HALF), :].astype(F32)
-        out[s, :DENSE, :] = total[s].astype(BF)
         return carry
 
     lax.fori_loop(0, FAR, step, 0)
-
-
-def chunk_body(came, chunk):
-    tail = came[0, DENSE:, :].astype(F32)
+    copies = []
+    for s in range(FAR):
+        held[s, :DENSE, :] = total[s].astype(BF)
+        held[s, DENSE:, :] = jnp.broadcast_to(extra[s : s + 1], (16, 128)).astype(BF)
+        copies.append(pltpu.make_async_copy(held.at[s], out.at[s], sems.at[s]))
+        copies[-1].start()
+    for copy in copies:
+        copy.wait()
+
+
+def add_body(parts, out):
+    total = parts[0]
     for s in range(1, FAR):
-        tail += came[s, DENSE:, :].astype(F32)
-    for n in range(NEAR):
-        chunk[n] = tail[8:]
+        total += parts[s]
+    out[...] = total
 
 
 def final_body(hubs, came, own_grad, out):
@@ -320,9 +332,6 @@
     col = lax.axis_index("col").astype(jnp.int32).reshape(1)
     target = jnp.where(
         jnp.arange(PEERS, dtype=jnp.int32) < remote_count[0], remote_target[0], BLOCKS
-    )
-    adj = (
-        hub_adjacency.reshape(FAR, NEAR, 2, ROWS).transpose(2, 1, 0, 3).reshape(2 * PEERS, ROWS)
     )
     (packed,) = call(pack_body, [smem(), vmem(), vmem()], [((OUT_ROWS, 128), BF, vmem())])(
         stay(hub_rows), stay(features), stay(send_pieces)
@@ -355,7 +364,7 @@
             pltpu.SemaphoreType.DMA((3,)),
             pltpu.SemaphoreType.DMA((COLS,)),
         ],
-    )(target, came, remote_values, *map(stay, (features, local_values, adj)))
+    )(target, came, remote_values, *map(stay, (features, local_values, hub_adjacency)))
     wide = (COLS * FEAT, ROWS)
     agg = exchange(agg, "col").reshape(wide)
     output, back, own_grad = call(
@@ -369,18 +378,24 @@
             pltpu.VMEM((BLOCKS + 1, FEAT, BLK), BF),
             pltpu.SemaphoreType.DMA((4,)),
         ],
-    )(col, target, agg, remote_values, *map(stay, (weight, cot, local_values, adj)))
+    )(col, target, agg, remote_values, *map(stay, (weight, cot, local_values, hub_adjacency)))
     back = exchange(back, "near", ORDER)
     far_all = (FAR, BACK_ROWS, 128)
-    (sums,) = call(
+    sums, chunk = call(
         gather_body,
         [smem(), vmem()],
-        [(far_all, BF, vmem())],
-        [pltpu.VMEM((FAR, DENSE, 128), F32)],
+        [(far_all, BF, away()), ((8, 128), F32, vmem())],
+        [
+            pltpu.VMEM(far_all, BF),
+            pltpu.VMEM((FAR, DENSE, 128), F32),
+            pltpu.SemaphoreType.DMA((FAR,)),
+        ],
     )(piece, back)
     sums = exchange(sums, "far")
-    (chunk,) = call(chunk_body, [vmem()], [((NEAR, 8, 128), F32, vmem())])(sums)
-    tiles = exchange(chunk, "near")
+    parts = lax.all_gather(chunk, "far", axis=0, tiled=False)
+    (chunk,) = call(add_body, [vmem()], [((8, 128), F32, vmem())])(parts)
+    tiles = lax.all_gather(chunk, "near", axis=0, tiled=False)
+    sums, tiles = lax.optimization_barrier((sums, tiles))
     (grad_input,) = call(
         final_body, [smem(), vmem(), vmem()], [((FEAT, ROWS), BF, vmem())]
     )(stay(hub_rows), sums, own_grad)

time: 160 us -> 188 us (1.18)
  blocking collectives: 104 us -> 138 us
  starting transfers between devices: 25.1 us -> 22.5 us
  waiting for transfers between devices: 9.71 us -> 7.45 us
  local copies, waits for them, and re-layouts: 2.57 us -> 0.65 us
    all_gather x0 -> x2, blocking collectives: none -> 69.8 us  [the longest x1 45.2 us: shards(): parts = lax.all_gather(chunk, 'far', axis=0, tiled=False)]
    all_to_all x2 -> x1, blocking collectives: 59.7 us -> 23.4 us  [exchange(): lax.all_to_all(values, axis, split_axis=0, concat_axis=0, tiled=True, axi...]
    all_to_all x3, starting transfers between devices: 25.1 us -> 22.5 us  [exchange(): lax.all_to_all(values, axis, split_axis=0, concat_axis=0, tiled=True, axi...]
    all_to_all x3, waiting for transfers between devices: 9.71 us -> 7.45 us  [exchange(): lax.all_to_all(values, axis, split_axis=0, concat_axis=0, tiled=True, axi...]
    reshape x2 -> x0, local copies, waits for them, and re-layouts: 1.92 us -> none  [shards(): hub_adjacency.reshape(FAR, NEAR, 2, ROWS).transpose(2, 1, 0, 3)]
  transfers between devices with their start and end apart: 3 -> 3, of which waited for: 2 -> 2; matrix products, arithmetic and copies ran while one was open for 1% -> 0% of each run, Pallas kernels for 1% -> 0%
where the time goes in v4:
time: 188 us; the launch traced here: 187 us
  blocking collectives  138 us (73%)
  starting transfers between devices  22.5 us (12%)
  Pallas kernels  17.5 us (9%)
  waiting for transfers between devices  7.45 us (4%)
    all_gather x1, blocking collectives, shards(): parts = lax.all_gather(chunk, 'far', axis=0, tiled=False)  45.2 us
    all_gather x1, blocking collectives, shards(): gathered = lax.all_gather(packed, 'far', axis=0, tiled=False)  33.2 us
    all_gather x1, blocking collectives, shards(): tiles = lax.all_gather(chunk, 'near', axis=0, tiled=False)  24.6 us
    all_to_all x1, blocking collectives, exchange(): lax.all_to_all(values, axis, split_axis=0, concat_axis=0, tiled=True, axi...  23.4 us
    all_to_all x3, starting transfers between devices, exchange(): lax.all_to_all(values, axis, split_axis=0, concat_axis=0, tiled=True, axi...  22.5 us
    all_gather x1, blocking collectives, shards(): cot = lax.all_gather(cotangent, 'col', axis=0, tiled=True)  11.2 us
    all_to_all x3, waiting for transfers between devices, exchange(): lax.all_to_all(values, axis, split_axis=0, concat_axis=0, tiled=True, axi...  7.45 us
    pallas_call x1, Pallas kernels, shards(): call(middle_body, [smem(), smem(), vmem(), vmem()] + [away()] * 4, [((FEA...  6.84 us
  transfers between devices with their start and end apart: 3, of which 2 were waited for; matrix products, arithmetic and copies ran while one was open for 0% of the time, Pallas kernels for 0%

profile of v4, /device:TPU:1, one launch (start us, length us, event | category | flops | bytes accessed | tf_op | source)
XLA Modules:
  0.0 187.2 jit_solution(1016156517586385759)
XLA Ops:
  0.6 1.1 shard_map.121
  1.7 33.2 %all-gather = bf16[2176,128]{1,0:T(8,128)(2,1)S(1)} all-gather(bf16[272,128]{1,0:T(8,128)(2,1)S(1)} %shard_map.121), channel_id=2, replica_groups=mesh['far'=8,'near'=16,'col'=4] {'far'}, dimensions={0}, use_global_device_ids=true | all-gather | bytes 626688 | tf_op jit(solution)/shard_map/all_gather | solution.py:339
  34.9 0.1 dynamic-slice_convert_fusion
  35.0 1.8 shard_map.122
  36.7 0.0 copy-start.1
  36.8 0.0 copy-start.2
  36.8 0.0 copy-start
  36.8 11.2 %all-to-all-start = ((bf16[16,272,128]{2,1,0:T(8,128)(2,1)}), bf16[16,272,128]{2,1,0:T(8,128)(2,1)S(1)}, u32[]{:S(2)}, u32[]{:S(2)}) async-start(bf16[16,272,128]{2,1,0:T(8,128)(2,1)} %shard_map.122), calls=%async_computation | async-start | bytes 2228224 | tf_op jit(solution)/shard_map/all_to_all | solution.py:309
  48.7 0.0 copy-done.1
  48.7 11.2 %all_gather.23.cot_far = bf16[256,512]{1,0:T(8,128)(2,1)} all-gather(bf16[64,512]{1,0:T(8,128)(2,1)S(1)} %copy-done.1), channel_id=1, replica_groups=mesh['far'=8,'near'=16,'col'=4] {'col'}, dimensions={0}, use_global_device_ids=true | all-gather | bytes 327680 | tf_op jit(solution)/shard_map/all_gather | solution.py:352
  59.9 0.0 copy-done.2
  59.9 1.9 %all-to-all-done.came = bf16[16,272,128]{2,1,0:T(8,128)(2,1)S(1)} async-done(((bf16[16,272,128]{2,1,0:T(8,128)(2,1)}), bf16[16,272,128]{2,1,0:T(8,128)(2,1)S(1)}, u32[]{:S(2)}, u32[]{:S(2)}) %all-to-all-start) | async-done | bytes 1114144 | tf_op jit(solution)/shard_map/all_to_all | solution.py:309
  61.8 0.0 copy-done
  61.8 4.1 %shard_map.123 = bf16[4,64,512]{2,1,0:T(8,128)(2,1)} custom-call(s32[128]{0:T(128)S(1)} %compare_select_fusion.target, bf16[16,272,128]{2,1,0:T(8,128)(2,1)S(1)} %all-to-all-done.came, bf16[128,64,128]{2,1,0:T(8,128)(2,1)S(1)} %copy-done, bf16[64,512]{1,0:T(8,128)(2,1)} %feats_far.1, bf16[4,128,128]{2,1,0:T(8,128)(2,1)} %local_far.3, bf16[256,512]{1,0:T(8,128)(2,1)} %adj_far.3), custom_call_target="tpu_custom_call" | custom-call | flops 1000000 | bytes 1000000 | tf_op jit(solution)/shard_map/pallas_call | solution.py:355
  65.9 4.1 %all-to-all-start.1 = ((bf16[4,64,512]{2,1,0:T(8,128)(2,1)}), bf16[4,64,512]{2,1,0:T(8,128)(2,1)S(1)}, u32[]{:S(2)}, u32[]{:S(2)}) async-start(bf16[4,64,512]{2,1,0:T(8,128)(2,1)} %shard_map.123), calls=%async_computation.1 | async-start | bytes 524288 | tf_op jit(solution)/shard_map/all_to_all | solution.py:309
  70.0 5.5 %all-to-all-done.1 = bf16[4,64,512]{2,1,0:T(8,128)(2,1)S(1)} async-done(((bf16[4,64,512]{2,1,0:T(8,128)(2,1)}), bf16[4,64,512]{2,1,0:T(8,128)(2,1)S(1)}, u32[]{:S(2)}, u32[]{:S(2)}) %all-to-all-start.1) | async-done | bytes 262176 | tf_op jit(solution)/shard_map/all_to_all | solution.py:309
  75.5 6.8 %shard_map.124 = (bf16[64,512]{1,0:T(8,128)(2,1)}, bf16[16,272,128]{2,1,0:T(8,128)(2,1)S(1)}, f32[64,512]{1,0:T(8,128)S(1)}) custom-call(s32[1]{0:T(128)} %bitcast.col, s32[128]{0:T(128)S(1)} %compare_select_fusion.target, bf16[256,512]{1,0:T(8,128)(2,1)S(1)} %bitcast.17, bf16[128,64,128]{2,1,0:T(8,128)(2,1)S(1)} %copy-done, bf16[256,256]{1,0:T(8,128)(2,1)} %weight_far.1, ...), custom_call_target="tpu_custom_call" | custom-call | flops 1000000 | bytes 1000000 | tf_op jit(solution)/shard_map/pallas_call | solution.py:370
  82.4 23.4 %all_to_all.20.came = bf16[16,272,128]{2,1,0:T(8,128)(2,1)S(1)} all-to-all(bf16[16,272,128]{2,1,0:T(8,128)(2,1)S(1)} %get-tuple-element.19), channel_id=1, replica_groups={{28,0,48,12,36,56,20,40,4,60,24,8,52,32,16,44},{29,1,49,13,37,57,21,41,..., dimensions={0} | all-to-all | bytes 2228224 | tf_op jit(solution)/shard_map/all_to_all | solution.py:309
  105.7 2.1 %shard_map.125 = (bf16[8,272,128]{2,1,0:T(8,128)(2,1)}, f32[8,128]{1,0:T(8,128)S(1)}) custom-call(s32[8,16]{1,0:T(8,128)S(1)} %bitcast.20, bf16[16,272,128]{2,1,0:T(8,128)(2,1)S(1)} %all_to_all.20.came), custom_call_target="tpu_custom_call" | custom-call | flops 1000000 | bytes 1000000 | tf_op jit(solution)/shard_map/pallas_call | solution.py:384
  107.8 7.2 %all-to-all-start.3 = ((bf16[8,272,128]{2,1,0:T(8,128)(2,1)}), bf16[8,272,128]{2,1,0:T(8,128)(2,1)S(1)}, u32[]{:S(2)}, u32[]{:S(2)}) async-start(bf16[8,272,128]{2,1,0:T(8,128)(2,1)} %get-tuple-element.20), calls=%async_computation.3 | async-start | bytes 1114112 | tf_op jit(solution)/shard_map/all_to_all | solution.py:309
  115.0 45.2 %all-gather.1 = f32[64,128]{1,0:T(8,128)S(1)} all-gather(f32[8,128]{1,0:T(8,128)S(1)} %get-tuple-element.21), channel_id=3, replica_groups=mesh['far'=8,'near'=16,'col'=4] {'far'}, dimensions={0}, use_global_device_ids=true | all-gather | bytes 36864 | tf_op jit(solution)/shard_map/all_gather | solution.py:395
  160.3 24.6 %all-gather.2 = f32[128,128]{1,0:T(8,128)S(1)} all-gather(f32[8,128]{1,0:T(8,128)S(1)} %shard_map.126), channel_id=4, replica_groups=mesh['far'=8,'near'=16,'col'=4] {'near'}, dimensions={0}, use_global_device_ids=true | all-gather | bytes 69632 | tf_op jit(solution)/shard_map/all_gather | solution.py:397
  184.8 0.0 all-to-all-done.3.came
  184.8 1.7 shard_map.127
  186.5 0.6 copy.15
  (3 shorter events, 0.0 us)
Async XLA Ops:
  36.7 11.9 %copy-start.1 = (bf16[64,512]{1,0:T(8,128)(2,1)S(1)}, bf16[64,512]{1,0:T(8,128)(2,1)}, u32[]{:S(2)}) copy-start(bf16[64,512]{1,0:T(8,128)(2,1)} %param.19) | copy-start | bytes 196612
  36.8 23.1 %copy-start.2 = (s32[1,128]{1,0:T(1,128)S(1)}, s32[1,128]{1,0:T(1,128)}, u32[]{:S(2)}) copy-start(s32[1,128]{1,0:T(1,128)} %param.12) | copy-start | bytes 1540
  36.8 25.0 %copy-start = (bf16[128,64,128]{2,1,0:T(8,128)(2,1)S(1)}, bf16[128,64,128]{2,1,0:T(8,128)(2,1)}, u32[]{:S(2)}) copy-start(bf16[128,64,128]{2,1,0:T(8,128)(2,1)} %remote.3) | copy-start | bytes 6291460
  36.8 25.0 %all-to-all-start = ((bf16[16,272,128]{2,1,0:T(8,128)(2,1)}), bf16[16,272,128]{2,1,0:T(8,128)(2,1)S(1)}, u32[]{:S(2)}, u32[]{:S(2)}) async-start(bf16[16,272,128]{2,1,0:T(8,128)(2,1)} %shard_map.122), calls=%async_computation | async-start | bytes 2228224 | tf_op jit(solution)/shard_map/all_to_all | solution.py:309
  65.9 9.6 %all-to-all-start.1 = ((bf16[4,64,512]{2,1,0:T(8,128)(2,1)}), bf16[4,64,512]{2,1,0:T(8,128)(2,1)S(1)}, u32[]{:S(2)}, u32[]{:S(2)}) async-start(bf16[4,64,512]{2,1,0:T(8,128)(2,1)} %shard_map.123), calls=%async_computation.1 | async-start | bytes 524288 | tf_op jit(solution)/shard_map/all_to_all | solution.py:309
  107.8 77.0 %all-to-all-start.3 = ((bf16[8,272,128]{2,1,0:T(8,128)(2,1)}), bf16[8,272,128]{2,1,0:T(8,128)(2,1)S(1)}, u32[]{:S(2)}, u32[]{:S(2)}) async-start(bf16[8,272,128]{2,1,0:T(8,128)(2,1)} %get-tuple-element.20), calls=%async_computation.3 | async-start | bytes 1114112 | tf_op jit(solution)/shard_map/all_to_all | solution.py:309

commit v5 on v3

--- a/solution.py
+++ b/solution.py
@@ -3,7 +3,6 @@
 from jax import lax
 from jax.experimental import pallas as pl
 from jax.experimental.pallas import tpu as pltpu
-from jax.sharding import Mesh
 from jax.sharding import PartitionSpec as P
 
 BF = jnp.bfloat16
@@ -26,6 +25,25 @@
 BACK_ROWS = NEAR_ROWS
 VMEM_BYTES = 30 * 1024 * 1024
 ORDER = (7, 0, 12, 3, 9, 14, 5, 10, 1, 15, 6, 2, 13, 8, 4, 11)
+FAR_ORDERS = (
+    (6, 2, 7, 0, 5, 3, 1, 4),
+    (6, 1, 3, 0, 5, 4, 2, 7),
+    (0, 7, 6, 2, 1, 5, 3, 4),
+    (5, 6, 3, 2, 0, 7, 4, 1),
+)
+FAR_SLOTS = tuple(tuple(order.index(s) for s in range(FAR)) for order in FAR_ORDERS)
+NEAR_IDS = tuple(tuple(f * NEAR + n for n in range(NEAR)) for f in range(FAR))
+FAR_IDS = tuple(tuple(f * NEAR + n for f in range(FAR)) for n in range(NEAR))
+NEAR_GROUPS = tuple(tuple(ids[n] for n in ORDER) for ids in NEAR_IDS)
+
+
+def place_of(near):
+    return 2 * (near // 8) + near % 2
+
+
+FAR_GROUPS = tuple(
+    tuple(FAR_IDS[n][f] for f in FAR_ORDERS[place_of(n)]) for n in range(NEAR)
+)
 SLOT = tuple(ORDER.index(n) for n in range(NEAR))
 
 NT = (((1,), (1,)), ((), ()))
@@ -134,10 +152,8 @@
     feats,
     local,
     adj,
-    value,
     total,
     sems,
-    out_sems,
 ):
     copies = start_all([(feats_far, feats), (local_far, local), (adj_far, adj)], sems)
     total[...] = jnp.zeros_like(total)
@@ -165,9 +181,9 @@
         cols = slice(b * BLK, (b + 1) * BLK)
         tiles = jnp.concatenate([total[b, :, :BLK], total[b, :, BLK:]], axis=0)
         own = dot(feats[:, cols], local[b])
-        value[:, cols] = (own + tiles + hub[:, cols]).astype(BF)
-    for copy in start_all([(value, out.at[c]) for c in range(COLS)], out_sems):
-        copy.wait()
+        value = (own + tiles + hub[:, cols]).astype(BF)
+        for c in range(COLS):
+            out[c, :, cols] = value
 
 
 def middle_body(
@@ -242,21 +258,21 @@
     lax.fori_loop(0, FAR, step, 0)
 
 
-def gather_body(piece, came, out, total):
+def gather_body(slot, piece, came, out, total):
     total[...] = jnp.zeros_like(total)
     extra = jnp.zeros((16, 128), F32)
     for n in range(NEAR):
         extra += came[n, FAR * HALF :, :].astype(F32)
     for s in range(FAR):
         hub = jnp.broadcast_to(extra[s : s + 1], (8, 128))
-        out[s, DENSE:, :] = jnp.concatenate([hub, extra[8:]], axis=0).astype(BF)
+        out[slot[s], DENSE:, :] = jnp.concatenate([hub, extra[8:]], axis=0).astype(BF)
 
     def step(s, carry):
         start = pl.multiple_of(s * HALF, HALF)
         for n in range(NEAR):
             at = pl.multiple_of(piece[s, ORDER[n]] * HALF, HALF)
             total[s, pl.ds(at, HALF), :] += came[n, pl.ds(start, HALF), :].astype(F32)
-        out[s, :DENSE, :] = total[s].astype(BF)
+        out[slot[s], :DENSE, :] = total[s].astype(BF)
         return carry
 
     lax.fori_loop(0, FAR, step, 0)
@@ -293,14 +309,14 @@
         out[:, cols] = (own_grad[:, cols] + tiles + hub_grad[:, cols]).astype(BF)
 
 
-def exchange(values, axis, order=None):
+def exchange(values, axis, groups=None):
     return lax.all_to_all(
         values,
         axis,
         split_axis=0,
         concat_axis=0,
         tiled=True,
-        axis_index_groups=None if order is None else [list(order)],
+        axis_index_groups=groups,
     )
 
 
@@ -316,7 +332,9 @@
     weight,
     cotangent,
 ):
-    far = lax.axis_index("far")
+    row = lax.axis_index("row").astype(jnp.int32)
+    far, near = row // NEAR, row % NEAR
+    slot = jnp.array(FAR_SLOTS, jnp.int32)[place_of(near)]
     col = lax.axis_index("col").astype(jnp.int32).reshape(1)
     target = jnp.where(
         jnp.arange(PEERS, dtype=jnp.int32) < remote_count[0], remote_target[0], BLOCKS
@@ -327,7 +345,7 @@
     (packed,) = call(pack_body, [smem(), vmem(), vmem()], [((OUT_ROWS, 128), BF, vmem())])(
         stay(hub_rows), stay(features), stay(send_pieces)
     )
-    gathered = lax.all_gather(packed, "far", axis=0, tiled=False)
+    gathered = lax.all_gather(packed, "row", axis=0, axis_index_groups=FAR_IDS)
     piece = lax.dynamic_slice(
         gathered[:, DENSE, :], (jnp.int32(0), far * NEAR), (FAR, NEAR)
     ).astype(jnp.int32)
@@ -339,21 +357,19 @@
         [pltpu.VMEM(near_all, BF), pltpu.SemaphoreType.DMA((NEAR,))],
     )(piece, gathered)
     picked, cotangent = lax.optimization_barrier((picked, cotangent))
-    came = exchange(picked, "near", ORDER)
+    came = exchange(picked, "row", NEAR_GROUPS)
     cot = lax.all_gather(cotangent, "col", axis=0, tiled=True)
-    came, cot = lax.optimization_barrier((came, cot))
+    came, cot, col, slot = lax.optimization_barrier((came, cot, col, slot))
     small = [pltpu.VMEM((BLOCKS, BLK, BLK), BF), pltpu.VMEM((2 * PEERS, ROWS), BF)]
     (agg,) = call(
         forward_body,
         [smem(), vmem(), vmem()] + [away()] * 3,
-        [((COLS, FEAT, ROWS), BF, away())],
+        [((COLS, FEAT, ROWS), BF, vmem())],
         [pltpu.VMEM((FEAT, ROWS), BF)]
         + small
         + [
-            pltpu.VMEM((FEAT, ROWS), BF),
             pltpu.VMEM((BLOCKS + 1, HALF, 2 * BLK), F32),
             pltpu.SemaphoreType.DMA((3,)),
-            pltpu.SemaphoreType.DMA((COLS,)),
         ],
     )(target, came, remote_values, *map(stay, (features, local_values, adj)))
     wide = (COLS * FEAT, ROWS)
@@ -370,17 +386,17 @@
             pltpu.SemaphoreType.DMA((4,)),
         ],
     )(col, target, agg, remote_values, *map(stay, (weight, cot, local_values, adj)))
-    back = exchange(back, "near", ORDER)
+    back = exchange(back, "row", NEAR_GROUPS)
     far_all = (FAR, BACK_ROWS, 128)
     (sums,) = call(
         gather_body,
-        [smem(), vmem()],
+        [smem(), smem(), vmem()],
         [(far_all, BF, vmem())],
         [pltpu.VMEM((FAR, DENSE, 128), F32)],
-    )(piece, back)
-    sums = exchange(sums, "far")
+    )(slot, piece, back)
+    sums = exchange(sums, "row", FAR_GROUPS)
     (chunk,) = call(chunk_body, [vmem()], [((NEAR, 8, 128), F32, vmem())])(sums)
-    tiles = exchange(chunk, "near")
+    tiles = exchange(chunk, "row", NEAR_IDS)
     (grad_input,) = call(
         final_body, [smem(), vmem(), vmem()], [((FEAT, ROWS), BF, vmem())]
     )(stay(hub_rows), sums, own_grad)
@@ -389,8 +405,7 @@
 
 
 def solution(mesh):
-    fine = Mesh(mesh.devices.reshape(FAR, NEAR, COLS), ("far", "near", "col"))
-    row = ("far", "near")
+    row = "row"
     placed = (
         P("col", row),
         P(row, None),
@@ -405,7 +420,7 @@
     )
     return jax.shard_map(
         shards,
-        mesh=fine,
+        mesh=mesh,
         in_specs=placed,
         out_specs=(P("col", row), P("col", row), P("col", None)),
         check_vma=False,

time: 160 us -> 156 us (0.975)
  blocking collectives: 104 us -> 114 us
  starting transfers between devices: 25.1 us -> 16.4 us
  waiting for transfers between devices: 9.71 us -> 4.14 us
    all_to_all x2 -> x3, blocking collectives: 59.7 us -> 69.9 us  [exchange(): lax.all_to_all(values, axis, split_axis=0, concat_axis=0, tiled=True, axi...]
    all_to_all x3 -> x2, starting transfers between devices: 25.1 us -> 16.4 us  [exchange(): lax.all_to_all(values, axis, split_axis=0, concat_axis=0, tiled=True, axi...]
    all_to_all x3 -> x2, waiting for transfers between devices: 9.71 us -> 4.14 us  [exchange(): lax.all_to_all(values, axis, split_axis=0, concat_axis=0, tiled=True, axi...]
  transfers between devices with their start and end apart: 3 -> 2, of which waited for: 2 -> 1; matrix products, arithmetic and copies ran while one was open for 1% -> 2% of each run, Pallas kernels for 1% -> 1%
where the time goes in v5:
time: 156 us; the launch traced here: 155 us
  blocking collectives  114 us (73%)
  starting transfers between devices  16.4 us (11%)
  Pallas kernels  16.1 us (10%)
  waiting for transfers between devices  4.14 us (3%)
  local copies, waits for them, and re-layouts  3.25 us (2%)
    all_to_all x3, blocking collectives, exchange(): lax.all_to_all(values, axis, split_axis=0, concat_axis=0, tiled=True, axi...  69.9 us
    all_gather x1, blocking collectives, shards(): gathered = lax.all_gather(packed, 'row', axis=0, axis_index_groups=FAR_IDS)  33.2 us
    all_to_all x2, starting transfers between devices, exchange(): lax.all_to_all(values, axis, split_axis=0, concat_axis=0, tiled=True, axi...  16.4 us
    all_gather x1, blocking collectives, shards(): cot = lax.all_gather(cotangent, 'col', axis=0, tiled=True)  11 us
    pallas_call x1, Pallas kernels, shards(): call(middle_body, [smem(), smem(), vmem(), vmem()] + [away()] * 4, [((FEA...  6.6 us
    all_to_all x2, waiting for transfers between devices, exchange(): lax.all_to_all(values, axis, split_axis=0, concat_axis=0, tiled=True, axi...  4.14 us
    pallas_call x1, Pallas kernels, shards(): call(forward_body, [smem(), vmem(), vmem()] + [away()] * 3, [((COLS, FEAT...  3.13 us
  transfers between devices with their start and end apart: 2, of which 1 were waited for; matrix products, arithmetic and copies ran while one was open for 2% of the time, Pallas kernels for 1%

profile of v5, /device:TPU:1, one launch (start us, length us, event | category | flops | bytes accessed | tf_op | source)
XLA Modules:
  0.0 155.5 jit_solution(14922201504979202244)
XLA Ops:
  0.6 1.1 shard_map.130
  1.7 33.2 %all-gather = bf16[2176,128]{1,0:T(8,128)(2,1)S(1)} all-gather(bf16[272,128]{1,0:T(8,128)(2,1)S(1)} %shard_map.130), channel_id=2, replica_groups={{0,64,128,192,256,320,384,448},{4,68,132,196,260,324,388,452},{8,72,136..., dimensions={0}, use_global_device_ids=true | all-gather | bytes 626688 | tf_op jit(solution)/shard_map/all_gather | solution.py:348
  34.9 0.1 dynamic-slice_convert_fusion
  35.0 1.7 %shard_map.131 = bf16[16,272,128]{2,1,0:T(8,128)(2,1)} custom-call(s32[8,16]{1,0:T(8,128)S(1)} %bitcast.21, bf16[8,272,128]{2,1,0:T(8,128)(2,1)S(1)} %bitcast.19), custom_call_target="tpu_custom_call" | custom-call | flops 1000000 | bytes 1000000 | tf_op jit(solution)/shard_map/pallas_call | solution.py:353
  36.7 0.0 copy-start
  36.7 11.2 %all-to-all-start = ((bf16[16,272,128]{2,1,0:T(8,128)(2,1)}), bf16[16,272,128]{2,1,0:T(8,128)(2,1)S(1)}, u32[]{:S(2)}, u32[]{:S(2)}) async-start(bf16[16,272,128]{2,1,0:T(8,128)(2,1)} %shard_map.131), calls=%async_computation | async-start | bytes 2228224 | tf_op jit(solution)/shard_map/all_to_all | solution.py:313
  48.0 0.0 copy-start.1
  48.0 0.0 copy-start.2
  48.7 1.1 reshape.28
  49.8 0.9 copy.14
  50.6 0.0 copy-done.1
  50.6 11.0 %all_gather.11.cot_far = bf16[256,512]{1,0:T(8,128)(2,1)} all-gather(bf16[64,512]{1,0:T(8,128)(2,1)S(1)} %copy-done.1), channel_id=1, replica_groups=mesh['row'=128,'col'=4] {'col'}, dimensions={0}, use_global_device_ids=true | all-gather | bytes 327680 | tf_op jit(solution)/shard_map/all_gather | solution.py:361
  61.6 0.7 dynamic-slice_bitcast_fusion.slot
  62.3 0.0 copy-done.2
  62.3 0.0 all-to-all-done.came
  62.3 0.0 copy-done
  62.4 3.1 %shard_map.132 = bf16[4,64,512]{2,1,0:T(8,128)(2,1)S(1)} custom-call(s32[128]{0:T(128)S(1)} %compare_select_fusion.target, bf16[16,272,128]{2,1,0:T(8,128)(2,1)S(1)} %all-to-all-done.came, bf16[128,64,128]{2,1,0:T(8,128)(2,1)S(1)} %copy-done, bf16[64,512]{1,0:T(8,128)(2,1)} %feats_far.1, bf16[4,128,128]{2,1,0:T(8,128)(2,1)} %local_far.3, ...), custom_call_target="tpu_custom_call" | custom-call | flops 1000000 | bytes 1000000 | tf_op jit(solution)/shard_map/pallas_call | solution.py:364
  65.5 8.9 %all_to_all.25 = bf16[4,64,512]{2,1,0:T(8,128)(2,1)S(1)} all-to-all(bf16[4,64,512]{2,1,0:T(8,128)(2,1)S(1)} %shard_map.132), channel_id=1, replica_groups=mesh['row'=128,'col'=4] {'col'}, dimensions={0} | all-to-all | bytes 524288 | tf_op jit(solution)/shard_map/all_to_all | solution.py:313
  74.4 6.6 %shard_map.133 = (bf16[64,512]{1,0:T(8,128)(2,1)}, bf16[16,272,128]{2,1,0:T(8,128)(2,1)S(1)}, f32[64,512]{1,0:T(8,128)S(1)}) custom-call(s32[1]{0:T(128)} %bitcast.2.col, s32[128]{0:T(128)S(1)} %compare_select_fusion.target, bf16[256,512]{1,0:T(8,128)(2,1)S(1)} %bitcast.20, bf16[128,64,128]{2,1,0:T(8,128)(2,1)S(1)} %copy-done, bf16[256,256]{1,0:T(8,128)(2,1)} %weight_far.1, ...), custom_call_target="tpu_custom_call" | custom-call | flops 1000000 | bytes 1000000 | tf_op jit(solution)/shard_map/pallas_call | solution.py:377
  81.0 24.5 %all_to_all.26.came = bf16[16,272,128]{2,1,0:T(8,128)(2,1)S(1)} all-to-all(bf16[16,272,128]{2,1,0:T(8,128)(2,1)S(1)} %get-tuple-element.19), channel_id=1, replica_groups={{28,0,48,12,36,56,20,40,4,60,24,8,52,32,16,44},{92,64,112,76,100,120,84..., dimensions={0} | all-to-all | bytes 2228224 | tf_op jit(solution)/shard_map/all_to_all | solution.py:313
  105.5 1.3 shard_map.134
  106.8 36.5 %all_to_all.27.came = bf16[8,272,128]{2,1,0:T(8,128)(2,1)S(1)} all-to-all(bf16[8,272,128]{2,1,0:T(8,128)(2,1)S(1)} %shard_map.134), channel_id=1, replica_groups={{384,128,448,0,320,192,64,256},{388,68,196,4,324,260,132,452},{392,136,..., dimensions={0} | all-to-all | bytes 1114112 | tf_op jit(solution)/shard_map/all_to_all | solution.py:313
  143.3 0.6 shard_map.136
  143.9 5.1 %all-to-all-start.4 = ((f32[16,8,128]{2,1,0:T(8,128)}), f32[16,8,128]{2,1,0:T(8,128)S(1)}, u32[]{:S(2)}, u32[]{:S(2)}) async-start(f32[16,8,128]{2,1,0:T(8,128)} %shard_map.136), calls=%async_computation.4 | async-start | bytes 131072 | tf_op jit(solution)/shard_map/all_to_all | solution.py:313
  149.0 1.7 %shard_map.135 = bf16[64,512]{1,0:T(8,128)(2,1)} custom-call(s32[1,2]{1,0:T(1,128)} %hubs.3, bf16[8,272,128]{2,1,0:T(8,128)(2,1)S(1)} %all_to_all.27.came, f32[64,512]{1,0:T(8,128)S(1)} %get-tuple-element.20.own_grad), custom_call_target="tpu_custom_call" | custom-call | flops 1000000 | bytes 1000000 | tf_op jit(solution)/shard_map/pallas_call | solution.py:400
  150.7 4.1 %all-to-all-done.4 = f32[16,8,128]{2,1,0:T(8,128)S(1)} async-done(((f32[16,8,128]{2,1,0:T(8,128)}), f32[16,8,128]{2,1,0:T(8,128)S(1)}, u32[]{:S(2)}, u32[]{:S(2)}) %all-to-all-start.4) | async-done | bytes 65568 | tf_op jit(solution)/shard_map/all_to_all | solution.py:313
  154.8 0.6 copy.17
  (2 shorter events, 0.0 us)
Async XLA Ops:
  36.7 25.6 %copy-start = (bf16[128,64,128]{2,1,0:T(8,128)(2,1)S(1)}, bf16[128,64,128]{2,1,0:T(8,128)(2,1)}, u32[]{:S(2)}) copy-start(bf16[128,64,128]{2,1,0:T(8,128)(2,1)} %remote.3) | copy-start | bytes 6291460
  36.7 25.6 %all-to-all-start = ((bf16[16,272,128]{2,1,0:T(8,128)(2,1)}), bf16[16,272,128]{2,1,0:T(8,128)(2,1)S(1)}, u32[]{:S(2)}, u32[]{:S(2)}) async-start(bf16[16,272,128]{2,1,0:T(8,128)(2,1)} %shard_map.131), calls=%async_computation | async-start | bytes 2228224 | tf_op jit(solution)/shard_map/all_to_all | solution.py:313
  48.0 2.6 %copy-start.1 = (bf16[64,512]{1,0:T(8,128)(2,1)S(1)}, bf16[64,512]{1,0:T(8,128)(2,1)}, u32[]{:S(2)}) copy-start(bf16[64,512]{1,0:T(8,128)(2,1)} %param.20) | copy-start | bytes 196612
  48.0 14.3 %copy-start.2 = (s32[1,128]{1,0:T(1,128)S(1)}, s32[1,128]{1,0:T(1,128)}, u32[]{:S(2)}) copy-start(s32[1,128]{1,0:T(1,128)} %param.13) | copy-start | bytes 1540
  143.9 11.0 %all-to-all-start.4 = ((f32[16,8,128]{2,1,0:T(8,128)}), f32[16,8,128]{2,1,0:T(8,128)S(1)}, u32[]{:S(2)}, u32[]{:S(2)}) async-start(f32[16,8,128]{2,1,0:T(8,128)} %shard_map.136), calls=%async_computation.4 | async-start | bytes 131072 | tf_op jit(solution)/shard_map/all_to_all | solution.py:313

commit v6 on v5

--- a/solution.py
+++ b/solution.py
@@ -158,19 +158,14 @@
     copies = start_all([(feats_far, feats), (local_far, local), (adj_far, adj)], sems)
     total[...] = jnp.zeros_like(total)
 
-    def step(s, carry):
-        start = pl.multiple_of(s * HALF, HALF)
+    for s in range(FAR):
         for first in range(0, NEAR, 8):
             parts = []
             for n in range(first, first + 8):
-                parts.append(
-                    dot(came[n, pl.ds(start, HALF), :], twice(remote[s * NEAR + ORDER[n]]))
-                )
+                q = s * NEAR + ORDER[n]
+                parts.append(dot(came[n, s * HALF : (s + 1) * HALF, :], twice(remote[q])))
             for n in range(first, first + 8):
                 total[target[s * NEAR + ORDER[n]]] += parts[n - first]
-        return carry
-
-    lax.fori_loop(0, FAR, step, 0)
     for copy in copies:
         copy.wait()
     hub_rows = jnp.concatenate([came[SLOT[n], FAR * HALF :, :][:8] for n in range(NEAR)], axis=0)
@@ -246,16 +241,12 @@
         tile = weight_grad[i * 8 : (i + 1) * 8, j * 128 : (j + 1) * 128]
         back[n, FAR * HALF :, :] = jnp.concatenate([hub[m * 8 : (m + 1) * 8], tile], axis=0).astype(BF)
 
-    def step(s, carry):
-        start = pl.multiple_of(s * HALF, HALF)
+    for s in range(FAR):
         for n in range(NEAR):
             q = s * NEAR + ORDER[n]
             tile = dot(pick[target[q]], remote[q], NT)
             tile = jnp.concatenate([tile[:HALF], tile[HALF:]], axis=1)
-            back[n, pl.ds(start, HALF), :] = tile.astype(BF)
-        return carry
-
-    lax.fori_loop(0, FAR, step, 0)
+            back[n, s * HALF : (s + 1) * HALF, :] = tile.astype(BF)
 
 
 def gather_body(slot, piece, came, out, total):
@@ -267,15 +258,11 @@
         hub = jnp.broadcast_to(extra[s : s + 1], (8, 128))
         out[slot[s], DENSE:, :] = jnp.concatenate([hub, extra[8:]], axis=0).astype(BF)
 
-    def step(s, carry):
-        start = pl.multiple_of(s * HALF, HALF)
+    for s in range(FAR):
         for n in range(NEAR):
             at = pl.multiple_of(piece[s, ORDER[n]] * HALF, HALF)
-            total[s, pl.ds(at, HALF), :] += came[n, pl.ds(start, HALF), :].astype(F32)
+            total[s, pl.ds(at, HALF), :] += came[n, s * HALF : (s + 1) * HALF, :].astype(F32)
         out[slot[s], :DENSE, :] = total[s].astype(BF)
-        return carry
-
-    lax.fori_loop(0, FAR, step, 0)
 
 
 def chunk_body(came, chunk):

time: 156 us -> 154 us (0.987)
  no operation moved by 1% of the time
where the time goes in v6:
time: 154 us
  blocking collectives  114 us (74%)
  starting transfers between devices  16.4 us (11%)
  Pallas kernels  14.6 us (9%)
  waiting for transfers between devices  4.17 us (3%)
  local copies, waits for them, and re-layouts  3.25 us (2%)
    all_to_all x3, blocking collectives, exchange(): lax.all_to_all(values, axis, split_axis=0, concat_axis=0, tiled=True, axi...  69.7 us
    all_gather x1, blocking collectives, shards(): gathered = lax.all_gather(packed, 'row', axis=0, axis_index_groups=FAR_IDS)  33.2 us
    all_to_all x2, starting transfers between devices, exchange(): lax.all_to_all(values, axis, split_axis=0, concat_axis=0, tiled=True, axi...  16.4 us
    all_gather x1, blocking collectives, shards(): cot = lax.all_gather(cotangent, 'col', axis=0, tiled=True)  11 us
    pallas_call x1, Pallas kernels, shards(): call(middle_body, [smem(), smem(), vmem(), vmem()] + [away()] * 4, [((FEA...  5.17 us
    all_to_all x2, waiting for transfers between devices, exchange(): lax.all_to_all(values, axis, split_axis=0, concat_axis=0, tiled=True, axi...  4.17 us
  transfers between devices with their start and end apart: 2, of which 1 were waited for; matrix products, arithmetic and copies ran while one was open for 2% of the time, Pallas kernels for 1%

profile of v6, /device:TPU:1, one launch (start us, length us, event | category | flops | bytes accessed | tf_op | source)
XLA Modules:
  0.0 153.9 jit_solution(5292210869505579636)
XLA Ops:
  0.6 1.1 shard_map.130
  1.7 33.2 %all-gather = bf16[2176,128]{1,0:T(8,128)(2,1)S(1)} all-gather(bf16[272,128]{1,0:T(8,128)(2,1)S(1)} %shard_map.130), channel_id=2, replica_groups={{0,64,128,192,256,320,384,448},{4,68,132,196,260,324,388,452},{8,72,136..., dimensions={0}, use_global_device_ids=true | all-gather | bytes 626688 | tf_op jit(solution)/shard_map/all_gather | solution.py:335
  34.9 0.1 dynamic-slice_convert_fusion
  35.0 1.7 %shard_map.131 = bf16[16,272,128]{2,1,0:T(8,128)(2,1)} custom-call(s32[8,16]{1,0:T(8,128)S(1)} %bitcast.21, bf16[8,272,128]{2,1,0:T(8,128)(2,1)S(1)} %bitcast.19), custom_call_target="tpu_custom_call" | custom-call | flops 1000000 | bytes 1000000 | tf_op jit(solution)/shard_map/pallas_call | solution.py:340
  36.7 0.0 copy-start
  36.7 11.2 %all-to-all-start = ((bf16[16,272,128]{2,1,0:T(8,128)(2,1)}), bf16[16,272,128]{2,1,0:T(8,128)(2,1)S(1)}, u32[]{:S(2)}, u32[]{:S(2)}) async-start(bf16[16,272,128]{2,1,0:T(8,128)(2,1)} %shard_map.131), calls=%async_computation | async-start | bytes 2228224 | tf_op jit(solution)/shard_map/all_to_all | solution.py:300
  48.0 0.0 copy-start.1
  48.0 0.0 copy-start.2
  48.7 1.1 reshape.28
  49.8 0.9 copy.14
  50.6 0.0 copy-done.1
  50.6 11.0 %all_gather.11.cot_far = bf16[256,512]{1,0:T(8,128)(2,1)} all-gather(bf16[64,512]{1,0:T(8,128)(2,1)S(1)} %copy-done.1), channel_id=1, replica_groups=mesh['row'=128,'col'=4] {'col'}, dimensions={0}, use_global_device_ids=true | all-gather | bytes 327680 | tf_op jit(solution)/shard_map/all_gather | solution.py:348
  61.6 0.7 dynamic-slice_bitcast_fusion.slot
  62.3 0.0 copy-done.2
  62.3 0.0 all-to-all-done.came
  62.3 0.0 copy-done
  62.4 3.0 %shard_map.132 = bf16[4,64,512]{2,1,0:T(8,128)(2,1)S(1)} custom-call(s32[128]{0:T(128)S(1)} %compare_select_fusion.target, bf16[16,272,128]{2,1,0:T(8,128)(2,1)S(1)} %all-to-all-done.came, bf16[128,64,128]{2,1,0:T(8,128)(2,1)S(1)} %copy-done, bf16[64,512]{1,0:T(8,128)(2,1)} %feats_far.1, bf16[4,128,128]{2,1,0:T(8,128)(2,1)} %local_far.3, ...), custom_call_target="tpu_custom_call" | custom-call | flops 1000000 | bytes 1000000 | tf_op jit(solution)/shard_map/pallas_call | solution.py:351
  65.4 8.9 %all_to_all.25 = bf16[4,64,512]{2,1,0:T(8,128)(2,1)S(1)} all-to-all(bf16[4,64,512]{2,1,0:T(8,128)(2,1)S(1)} %shard_map.132), channel_id=1, replica_groups=mesh['row'=128,'col'=4] {'col'}, dimensions={0} | all-to-all | bytes 524288 | tf_op jit(solution)/shard_map/all_to_all | solution.py:300
  74.3 5.2 %shard_map.133 = (bf16[64,512]{1,0:T(8,128)(2,1)}, bf16[16,272,128]{2,1,0:T(8,128)(2,1)S(1)}, f32[64,512]{1,0:T(8,128)S(1)}) custom-call(s32[1]{0:T(128)} %bitcast.2.col, s32[128]{0:T(128)S(1)} %compare_select_fusion.target, bf16[256,512]{1,0:T(8,128)(2,1)S(1)} %bitcast.20, bf16[128,64,128]{2,1,0:T(8,128)(2,1)S(1)} %copy-done, bf16[256,256]{1,0:T(8,128)(2,1)} %weight_far.1, ...), custom_call_target="tpu_custom_call" | custom-call | flops 1000000 | bytes 1000000 | tf_op jit(solution)/shard_map/pallas_call | solution.py:364
  79.5 24.5 %all_to_all.26.came = bf16[16,272,128]{2,1,0:T(8,128)(2,1)S(1)} all-to-all(bf16[16,272,128]{2,1,0:T(8,128)(2,1)S(1)} %get-tuple-element.19), channel_id=1, replica_groups={{28,0,48,12,36,56,20,40,4,60,24,8,52,32,16,44},{92,64,112,76,100,120,84..., dimensions={0} | all-to-all | bytes 2228224 | tf_op jit(solution)/shard_map/all_to_all | solution.py:300
  104.0 1.2 shard_map.134
  105.2 36.4 %all_to_all.27.came = bf16[8,272,128]{2,1,0:T(8,128)(2,1)S(1)} all-to-all(bf16[8,272,128]{2,1,0:T(8,128)(2,1)S(1)} %shard_map.134), channel_id=1, replica_groups={{384,128,448,0,320,192,64,256},{388,68,196,4,324,260,132,452},{392,136,..., dimensions={0} | all-to-all | bytes 1114112 | tf_op jit(solution)/shard_map/all_to_all | solution.py:300
  141.5 0.6 shard_map.136
  142.2 5.2 %all-to-all-start.4 = ((f32[16,8,128]{2,1,0:T(8,128)}), f32[16,8,128]{2,1,0:T(8,128)S(1)}, u32[]{:S(2)}, u32[]{:S(2)}) async-start(f32[16,8,128]{2,1,0:T(8,128)} %shard_map.136), calls=%async_computation.4 | async-start | bytes 131072 | tf_op jit(solution)/shard_map/all_to_all | solution.py:300
  147.4 1.7 %shard_map.135 = bf16[64,512]{1,0:T(8,128)(2,1)} custom-call(s32[1,2]{1,0:T(1,128)} %hubs.3, bf16[8,272,128]{2,1,0:T(8,128)(2,1)S(1)} %all_to_all.27.came, f32[64,512]{1,0:T(8,128)S(1)} %get-tuple-element.20.own_grad), custom_call_target="tpu_custom_call" | custom-call | flops 1000000 | bytes 1000000 | tf_op jit(solution)/shard_map/pallas_call | solution.py:387
  149.1 4.2 %all-to-all-done.4 = f32[16,8,128]{2,1,0:T(8,128)S(1)} async-done(((f32[16,8,128]{2,1,0:T(8,128)}), f32[16,8,128]{2,1,0:T(8,128)S(1)}, u32[]{:S(2)}, u32[]{:S(2)}) %all-to-all-start.4) | async-done | bytes 65568 | tf_op jit(solution)/shard_map/all_to_all | solution.py:300
  153.2 0.6 copy.17
  (2 shorter events, 0.0 us)
Async XLA Ops:
  36.7 25.6 %copy-start = (bf16[128,64,128]{2,1,0:T(8,128)(2,1)S(1)}, bf16[128,64,128]{2,1,0:T(8,128)(2,1)}, u32[]{:S(2)}) copy-start(bf16[128,64,128]{2,1,0:T(8,128)(2,1)} %remote.3) | copy-start | bytes 6291460
  36.7 25.6 %all-to-all-start = ((bf16[16,272,128]{2,1,0:T(8,128)(2,1)}), bf16[16,272,128]{2,1,0:T(8,128)(2,1)S(1)}, u32[]{:S(2)}, u32[]{:S(2)}) async-start(bf16[16,272,128]{2,1,0:T(8,128)(2,1)} %shard_map.131), calls=%async_computation | async-start | bytes 2228224 | tf_op jit(solution)/shard_map/all_to_all | solution.py:300
  48.0 2.6 %copy-start.1 = (bf16[64,512]{1,0:T(8,128)(2,1)S(1)}, bf16[64,512]{1,0:T(8,128)(2,1)}, u32[]{:S(2)}) copy-start(bf16[64,512]{1,0:T(8,128)(2,1)} %param.20) | copy-start | bytes 196612
  48.0 14.3 %copy-start.2 = (s32[1,128]{1,0:T(1,128)S(1)}, s32[1,128]{1,0:T(1,128)}, u32[]{:S(2)}) copy-start(s32[1,128]{1,0:T(1,128)} %param.13) | copy-start | bytes 1540
  142.2 11.1 %all-to-all-start.4 = ((f32[16,8,128]{2,1,0:T(8,128)}), f32[16,8,128]{2,1,0:T(8,128)S(1)}, u32[]{:S(2)}, u32[]{:S(2)}) async-start(f32[16,8,128]{2,1,0:T(8,128)} %shard_map.136), calls=%async_computation.4 | async-start | bytes 131072 | tf_op jit(solution)/shard_map/all_to_all | solution.py:300

commit v7 on v6

--- a/solution.py
+++ b/solution.py
@@ -41,6 +41,13 @@
     return 2 * (near // 8) + near % 2
 
 
+def slot_of(place, s):
+    chosen = jnp.int32(FAR_SLOTS[0][s])
+    for other in range(1, len(FAR_SLOTS)):
+        chosen = jnp.where(place == other, FAR_SLOTS[other][s], chosen)
+    return chosen
+
+
 FAR_GROUPS = tuple(
     tuple(FAR_IDS[n][f] for f in FAR_ORDERS[place_of(n)]) for n in range(NEAR)
 )
@@ -169,9 +176,8 @@
     for copy in copies:
         copy.wait()
     hub_rows = jnp.concatenate([came[SLOT[n], FAR * HALF :, :][:8] for n in range(NEAR)], axis=0)
-    hub = (
-        dot(hub_rows, adj[: PEERS, :], TN)[:FEAT] + dot(hub_rows, adj[PEERS:, :], TN)[FEAT:]
-    )
+    hub_rows = jnp.concatenate([hub_rows[:, :FEAT], hub_rows[:, FEAT:]], axis=0)
+    hub = dot(hub_rows, adj[...], TN)
     for b in range(BLOCKS):
         cols = slice(b * BLK, (b + 1) * BLK)
         tiles = jnp.concatenate([total[b, :, :BLK], total[b, :, BLK:]], axis=0)
@@ -186,24 +192,16 @@
     target,
     agg,
     remote,
-    weight_far,
-    cot_far,
-    local_far,
-    adj_far,
-    output,
-    back,
-    own_grad,
     weight,
     cot,
     local,
     adj,
+    output,
+    back,
+    own_grad,
     grad,
     pick,
-    sems,
 ):
-    pairs = [(weight_far, weight), (cot_far, cot), (local_far, local), (adj_far, adj)]
-    copies = start_all(pairs, sems)
-    copies[0].wait()
     scale = 0.7978845608028654
     mine = pl.multiple_of(col[0] * FEAT, FEAT)
     for c in range(COLS):
@@ -214,8 +212,6 @@
         slope = half + 0.5 * pre * (1.0 - bend * bend) * (
             scale * (1.0 + 3.0 * 0.044715 * square)
         )
-        if c == 0:
-            copies[1].wait()
         grad[c * FEAT : (c + 1) * FEAT, :] = (
             cot[c * FEAT : (c + 1) * FEAT, :].astype(F32) * slope
         ).astype(BF)
@@ -226,12 +222,10 @@
 
     grad_agg = dot(weight[pl.ds(mine, FEAT), :], grad[...]).astype(BF)
     weight_grad = dot(agg[pl.ds(mine, FEAT), :], grad[...], NT)
-    copies[2].wait()
     for b in range(BLOCKS):
         cols = slice(b * BLK, (b + 1) * BLK)
         pick[b] = grad_agg[:, cols]
         own_grad[:, cols] = dot(grad_agg[:, cols], local[b], NT)
-    copies[3].wait()
     pick[BLOCKS] = jnp.zeros((FEAT, BLK), BF)
     hub = dot(adj[...], grad_agg, NT)
     hub = jnp.concatenate([hub[:PEERS], hub[PEERS:]], axis=1)
@@ -249,7 +243,8 @@
             back[n, s * HALF : (s + 1) * HALF, :] = tile.astype(BF)
 
 
-def gather_body(slot, piece, came, out, total):
+def gather_body(place, piece, came, out, total):
+    slot = [slot_of(place[0], s) for s in range(FAR)]
     total[...] = jnp.zeros_like(total)
     extra = jnp.zeros((16, 128), F32)
     for n in range(NEAR):
@@ -321,7 +316,7 @@
 ):
     row = lax.axis_index("row").astype(jnp.int32)
     far, near = row // NEAR, row % NEAR
-    slot = jnp.array(FAR_SLOTS, jnp.int32)[place_of(near)]
+    place = place_of(near).reshape(1)
     col = lax.axis_index("col").astype(jnp.int32).reshape(1)
     target = jnp.where(
         jnp.arange(PEERS, dtype=jnp.int32) < remote_count[0], remote_target[0], BLOCKS
@@ -346,7 +341,7 @@
     picked, cotangent = lax.optimization_barrier((picked, cotangent))
     came = exchange(picked, "row", NEAR_GROUPS)
     cot = lax.all_gather(cotangent, "col", axis=0, tiled=True)
-    came, cot, col, slot = lax.optimization_barrier((came, cot, col, slot))
+    came, cot, col, place = lax.optimization_barrier((came, cot, col, place))
     small = [pltpu.VMEM((BLOCKS, BLK, BLK), BF), pltpu.VMEM((2 * PEERS, ROWS), BF)]
     (agg,) = call(
         forward_body,
@@ -363,16 +358,10 @@
     agg = exchange(agg, "col").reshape(wide)
     output, back, own_grad = call(
         middle_body,
-        [smem(), smem(), vmem(), vmem()] + [away()] * 4,
+        [smem(), smem()] + [vmem()] * 6,
         [((FEAT, ROWS), BF, vmem()), (near_all, BF, vmem()), ((FEAT, ROWS), F32, vmem())],
-        [pltpu.VMEM((COLS * FEAT, COLS * FEAT), BF), pltpu.VMEM(wide, BF)]
-        + small
-        + [
-            pltpu.VMEM(wide, BF),
-            pltpu.VMEM((BLOCKS + 1, FEAT, BLK), BF),
-            pltpu.SemaphoreType.DMA((4,)),
-        ],
-    )(col, target, agg, remote_values, *map(stay, (weight, cot, local_values, adj)))
+        [pltpu.VMEM(wide, BF), pltpu.VMEM((BLOCKS + 1, FEAT, BLK), BF)],
+    )(col, target, agg, remote_values, weight, cot, local_values, adj)
     back = exchange(back, "row", NEAR_GROUPS)
     far_all = (FAR, BACK_ROWS, 128)
     (sums,) = call(
@@ -380,7 +369,7 @@
         [smem(), smem(), vmem()],
         [(far_all, BF, vmem())],
         [pltpu.VMEM((FAR, DENSE, 128), F32)],
-    )(slot, piece, back)
+    )(place, piece, back)
     sums = exchange(sums, "row", FAR_GROUPS)
     (chunk,) = call(chunk_body, [vmem()], [((NEAR, 8, 128), F32, vmem())])(sums)
     tiles = exchange(chunk, "row", NEAR_IDS)

time: 154 us -> 152 us (0.987)
  transfers between devices with their start and end apart: 2 -> 2, of which waited for: 1 -> 2; matrix products, arithmetic and copies ran while one was open for 2% -> 1% of each run, Pallas kernels for 1% -> 1%
where the time goes in v7:
time: 152 us; the launch traced here: 151 us
  blocking collectives  113 us (74%)
  starting transfers between devices  16.4 us (11%)
  Pallas kernels  13.2 us (9%)
  waiting for transfers between devices  4.57 us (3%)
  local copies, waits for them, and re-layouts  2.59 us (2%)
    all_to_all x3, blocking collectives, exchange(): lax.all_to_all(values, axis, split_axis=0, concat_axis=0, tiled=True, axi...  69.3 us
    all_gather x1, blocking collectives, shards(): gathered = lax.all_gather(packed, 'row', axis=0, axis_index_groups=FAR_IDS)  33.2 us
    all_to_all x2, starting transfers between devices, exchange(): lax.all_to_all(values, axis, split_axis=0, concat_axis=0, tiled=True, axi...  16.4 us
    all_gather x1, blocking collectives, shards(): cot = lax.all_gather(cotangent, 'col', axis=0, tiled=True)  10.6 us
    all_to_all x2, waiting for transfers between devices, exchange(): lax.all_to_all(values, axis, split_axis=0, concat_axis=0, tiled=True, axi...  4.57 us
    pallas_call x1, Pallas kernels, shards(): call(middle_body, [smem(), smem()] + [vmem()] * 6, [((FEAT, ROWS), BF, vm...  3.81 us
  transfers between devices with their start and end apart: 2, of which 2 were waited for; matrix products, arithmetic and copies ran while one was open for 1% of the time, Pallas kernels for 1%

profile of v7, /device:TPU:1, one launch (start us, length us, event | category | flops | bytes accessed | tf_op | source)
XLA Modules:
  0.0 151.4 jit_solution(17712794880709962913)
XLA Ops:
  0.6 1.1 shard_map.121
  1.7 33.2 %all-gather = bf16[2176,128]{1,0:T(8,128)(2,1)S(1)} all-gather(bf16[272,128]{1,0:T(8,128)(2,1)S(1)} %shard_map.121), channel_id=2, replica_groups={{0,64,128,192,256,320,384,448},{4,68,132,196,260,324,388,452},{8,72,136..., dimensions={0}, use_global_device_ids=true | all-gather | bytes 626688 | tf_op jit(solution)/shard_map/all_gather | solution.py:330
  34.9 0.1 dynamic-slice_convert_fusion
  35.0 1.8 %shard_map.122 = bf16[16,272,128]{2,1,0:T(8,128)(2,1)} custom-call(s32[8,16]{1,0:T(8,128)S(1)} %bitcast.22, bf16[8,272,128]{2,1,0:T(8,128)(2,1)S(1)} %bitcast.20), custom_call_target="tpu_custom_call" | custom-call | flops 1000000 | bytes 1000000 | tf_op jit(solution)/shard_map/pallas_call | solution.py:335
  36.7 0.0 copy-start.4
  36.8 0.0 copy-start
  36.8 11.2 %all-to-all-start = ((bf16[16,272,128]{2,1,0:T(8,128)(2,1)}), bf16[16,272,128]{2,1,0:T(8,128)(2,1)S(1)}, u32[]{:S(2)}, u32[]{:S(2)}) async-start(bf16[16,272,128]{2,1,0:T(8,128)(2,1)} %shard_map.122), calls=%async_computation | async-start | bytes 2228224 | tf_op jit(solution)/shard_map/all_to_all | solution.py:295
  48.0 0.0 copy-start.5
  48.7 1.1 reshape.32
  49.8 0.9 copy.13
  50.6 0.0 copy-done.4
  50.6 10.6 %all_gather.11.cot = bf16[256,512]{1,0:T(8,128)(2,1)S(1)} all-gather(bf16[64,512]{1,0:T(8,128)(2,1)S(1)} %copy-done.4), channel_id=1, replica_groups=mesh['row'=128,'col'=4] {'col'}, dimensions={0}, use_global_device_ids=true | all-gather | bytes 327680 | tf_op jit(solution)/shard_map/all_gather | solution.py:343
  61.2 0.0 copy-done.5
  61.2 0.4 all-to-all-done.came
  61.7 0.0 copy-done
  61.7 0.0 copy-start.1
  61.7 0.0 copy-start.2
  61.7 0.0 copy-start.3
  61.7 3.0 %shard_map.123 = bf16[4,64,512]{2,1,0:T(8,128)(2,1)S(1)} custom-call(s32[128]{0:T(128)S(1)} %compare_select_fusion.target, bf16[16,272,128]{2,1,0:T(8,128)(2,1)S(1)} %all-to-all-done.came, bf16[128,64,128]{2,1,0:T(8,128)(2,1)S(1)} %copy-done, bf16[64,512]{1,0:T(8,128)(2,1)} %feats_far.1, bf16[4,128,128]{2,1,0:T(8,128)(2,1)} %local.1, bf16[256,512]{1,0:T(8,128)(2,1)} %bitcast.17), custom_call_target="tpu_custom_call" | custom-call | flops 1000000 | bytes 1000000 | tf_op jit(solution)/shard_map/pallas_call | solution.py:346
  64.7 9.5 %all_to_all.25 = bf16[4,64,512]{2,1,0:T(8,128)(2,1)S(1)} all-to-all(bf16[4,64,512]{2,1,0:T(8,128)(2,1)S(1)} %shard_map.123), channel_id=1, replica_groups=mesh['row'=128,'col'=4] {'col'}, dimensions={0} | all-to-all | bytes 524288 | tf_op jit(solution)/shard_map/all_to_all | solution.py:295
  74.3 0.0 copy-done.1
  74.3 0.0 copy-done.2
  74.3 0.0 copy-done.3
  74.3 3.8 %shard_map.124 = (bf16[64,512]{1,0:T(8,128)(2,1)}, bf16[16,272,128]{2,1,0:T(8,128)(2,1)S(1)}, f32[64,512]{1,0:T(8,128)S(1)}) custom-call(s32[1]{0:T(128)} %bitcast.2.col, s32[128]{0:T(128)S(1)} %compare_select_fusion.target, bf16[256,512]{1,0:T(8,128)(2,1)S(1)} %bitcast.21, bf16[128,64,128]{2,1,0:T(8,128)(2,1)S(1)} %copy-done, ...), custom_call_target="tpu_custom_call" | custom-call | flops 1000000 | bytes 1000000 | tf_op jit(solution)/shard_map/pallas_call | solution.py:359
  78.1 23.3 %all_to_all.26.came = bf16[16,272,128]{2,1,0:T(8,128)(2,1)S(1)} all-to-all(bf16[16,272,128]{2,1,0:T(8,128)(2,1)S(1)} %get-tuple-element.19), channel_id=1, replica_groups={{28,0,48,12,36,56,20,40,4,60,24,8,52,32,16,44},{92,64,112,76,100,120,84..., dimensions={0} | all-to-all | bytes 2228224 | tf_op jit(solution)/shard_map/all_to_all | solution.py:295
  101.4 1.2 shard_map.125
  102.7 36.4 %all_to_all.27.came = bf16[8,272,128]{2,1,0:T(8,128)(2,1)S(1)} all-to-all(bf16[8,272,128]{2,1,0:T(8,128)(2,1)S(1)} %shard_map.125), channel_id=1, replica_groups={{384,128,448,0,320,192,64,256},{388,68,196,4,324,260,132,452},{392,136,..., dimensions={0} | all-to-all | bytes 1114112 | tf_op jit(solution)/shard_map/all_to_all | solution.py:295
  139.1 0.6 shard_map.127
  139.7 5.2 %all-to-all-start.4 = ((f32[16,8,128]{2,1,0:T(8,128)}), f32[16,8,128]{2,1,0:T(8,128)S(1)}, u32[]{:S(2)}, u32[]{:S(2)}) async-start(f32[16,8,128]{2,1,0:T(8,128)} %shard_map.127), calls=%async_computation.4 | async-start | bytes 131072 | tf_op jit(solution)/shard_map/all_to_all | solution.py:295
  144.9 1.7 %shard_map.126 = bf16[64,512]{1,0:T(8,128)(2,1)} custom-call(s32[1,2]{1,0:T(1,128)} %hubs.3, bf16[8,272,128]{2,1,0:T(8,128)(2,1)S(1)} %all_to_all.27.came, f32[64,512]{1,0:T(8,128)S(1)} %get-tuple-element.20.own_grad), custom_call_target="tpu_custom_call" | custom-call | flops 1000000 | bytes 1000000 | tf_op jit(solution)/shard_map/pallas_call | solution.py:376
  146.6 4.1 %all-to-all-done.4 = f32[16,8,128]{2,1,0:T(8,128)S(1)} async-done(((f32[16,8,128]{2,1,0:T(8,128)}), f32[16,8,128]{2,1,0:T(8,128)S(1)}, u32[]{:S(2)}, u32[]{:S(2)}) %all-to-all-start.4) | async-done | bytes 65568 | tf_op jit(solution)/shard_map/all_to_all | solution.py:295
  150.8 0.6 copy.16
  (2 shorter events, 0.0 us)
Async XLA Ops:
  36.7 13.9 %copy-start.4 = (bf16[64,512]{1,0:T(8,128)(2,1)S(1)}, bf16[64,512]{1,0:T(8,128)(2,1)}, u32[]{:S(2)}) copy-start(bf16[64,512]{1,0:T(8,128)(2,1)} %param.19) | copy-start | bytes 196612
  36.8 24.9 %copy-start = (bf16[128,64,128]{2,1,0:T(8,128)(2,1)S(1)}, bf16[128,64,128]{2,1,0:T(8,128)(2,1)}, u32[]{:S(2)}) copy-start(bf16[128,64,128]{2,1,0:T(8,128)(2,1)} %remote.3) | copy-start | bytes 6291460
  36.8 24.9 %all-to-all-start = ((bf16[16,272,128]{2,1,0:T(8,128)(2,1)}), bf16[16,272,128]{2,1,0:T(8,128)(2,1)S(1)}, u32[]{:S(2)}, u32[]{:S(2)}) async-start(bf16[16,272,128]{2,1,0:T(8,128)(2,1)} %shard_map.122), calls=%async_computation | async-start | bytes 2228224 | tf_op jit(solution)/shard_map/all_to_all | solution.py:295
  48.0 13.2 %copy-start.5 = (s32[1,128]{1,0:T(1,128)S(1)}, s32[1,128]{1,0:T(1,128)}, u32[]{:S(2)}) copy-start(s32[1,128]{1,0:T(1,128)} %param.12) | copy-start | bytes 1540
  61.7 12.6 %copy-start.1 = (bf16[8,16,2,512]{3,0,1,2:T(8,128)(2,1)S(1)}, bf16[8,16,2,512]{3,0,1,2:T(8,128)(2,1)}, u32[]{:S(2)}) copy-start(bf16[8,16,2,512]{3,0,1,2:T(8,128)(2,1)} %copy.13) | copy-start | bytes 786436
  61.7 12.6 %copy-start.2 = (bf16[4,128,128]{2,1,0:T(8,128)(2,1)S(1)}, bf16[4,128,128]{2,1,0:T(8,128)(2,1)}, u32[]{:S(2)}) copy-start(bf16[4,128,128]{2,1,0:T(8,128)(2,1)} %local.1) | copy-start | bytes 393220
  61.7 12.6 %copy-start.3 = (bf16[256,256]{1,0:T(8,128)(2,1)S(1)}, bf16[256,256]{1,0:T(8,128)(2,1)}, u32[]{:S(2)}) copy-start(bf16[256,256]{1,0:T(8,128)(2,1)} %weight.1) | copy-start | bytes 393220
  139.7 11.0 %all-to-all-start.4 = ((f32[16,8,128]{2,1,0:T(8,128)}), f32[16,8,128]{2,1,0:T(8,128)S(1)}, u32[]{:S(2)}, u32[]{:S(2)}) async-start(f32[16,8,128]{2,1,0:T(8,128)} %shard_map.127), calls=%async_computation.4 | async-start | bytes 131072 | tf_op jit(solution)/shard_map/all_to_all | solution.py:295

commit v8 on v7

--- a/solution.py
+++ b/solution.py
@@ -148,21 +148,9 @@
     )
 
 
-def forward_body(
-    target,
-    came,
-    remote,
-    feats_far,
-    local_far,
-    adj_far,
-    out,
-    feats,
-    local,
-    adj,
-    total,
-    sems,
-):
-    copies = start_all([(feats_far, feats), (local_far, local), (adj_far, adj)], sems)
+def forward_body(target, came, remote, feats, adj, local_far, out, local, total, sem):
+    fetch = pltpu.make_async_copy(local_far, local, sem)
+    fetch.start()
     total[...] = jnp.zeros_like(total)
 
     for s in range(FAR):
@@ -173,8 +161,7 @@
                 parts.append(dot(came[n, s * HALF : (s + 1) * HALF, :], twice(remote[q])))
             for n in range(first, first + 8):
                 total[target[s * NEAR + ORDER[n]]] += parts[n - first]
-    for copy in copies:
-        copy.wait()
+    fetch.wait()
     hub_rows = jnp.concatenate([came[SLOT[n], FAR * HALF :, :][:8] for n in range(NEAR)], axis=0)
     hub_rows = jnp.concatenate([hub_rows[:, :FEAT], hub_rows[:, FEAT:]], axis=0)
     hub = dot(hub_rows, adj[...], TN)
@@ -231,7 +218,7 @@
     hub = jnp.concatenate([hub[:PEERS], hub[PEERS:]], axis=1)
     for n in range(NEAR):
         m = ORDER[n]
-        i, j = m // 2, m % 2
+        i, j = n // 2, n % 2
         tile = weight_grad[i * 8 : (i + 1) * 8, j * 128 : (j + 1) * 128]
         back[n, FAR * HALF :, :] = jnp.concatenate([hub[m * 8 : (m + 1) * 8], tile], axis=0).astype(BF)
 
@@ -342,18 +329,16 @@
     came = exchange(picked, "row", NEAR_GROUPS)
     cot = lax.all_gather(cotangent, "col", axis=0, tiled=True)
     came, cot, col, place = lax.optimization_barrier((came, cot, col, place))
-    small = [pltpu.VMEM((BLOCKS, BLK, BLK), BF), pltpu.VMEM((2 * PEERS, ROWS), BF)]
     (agg,) = call(
         forward_body,
-        [smem(), vmem(), vmem()] + [away()] * 3,
+        [smem()] + [vmem()] * 4 + [away()],
         [((COLS, FEAT, ROWS), BF, vmem())],
-        [pltpu.VMEM((FEAT, ROWS), BF)]
-        + small
-        + [
+        [
+            pltpu.VMEM((BLOCKS, BLK, BLK), BF),
             pltpu.VMEM((BLOCKS + 1, HALF, 2 * BLK), F32),
-            pltpu.SemaphoreType.DMA((3,)),
+            pltpu.SemaphoreType.DMA,
         ],
-    )(target, came, remote_values, *map(stay, (features, local_values, adj)))
+    )(target, came, remote_values, features, adj, stay(local_values))
     wide = (COLS * FEAT, ROWS)
     agg = exchange(agg, "col").reshape(wide)
     output, back, own_grad = call(
@@ -372,7 +357,7 @@
     )(place, piece, back)
     sums = exchange(sums, "row", FAR_GROUPS)
     (chunk,) = call(chunk_body, [vmem()], [((NEAR, 8, 128), F32, vmem())])(sums)
-    tiles = exchange(chunk, "row", NEAR_IDS)
+    tiles = exchange(chunk, "row", NEAR_GROUPS)
     (grad_input,) = call(
         final_body, [smem(), vmem(), vmem()], [((FEAT, ROWS), BF, vmem())]
     )(stay(hub_rows), sums, own_grad)

time: 152 us -> 151 us (level)
  waiting for transfers between devices: 4.57 us -> 2.17 us
    all_to_all x2, waiting for transfers between devices: 4.57 us -> 2.17 us  [exchange(): lax.all_to_all(values, axis, split_axis=0, concat_axis=0, tiled=True, axi...]
    all_gather x1, blocking collectives: 10.6 us -> 12.2 us  [shards(): cot = lax.all_gather(cotangent, 'col', axis=0, tiled=True)]
  transfers between devices with their start and end apart: 2 -> 2, of which waited for: 2 -> 1; matrix products, arithmetic and copies ran while one was open for 1% -> 1% of each run, Pallas kernels for 1% -> 1%
where the time goes in v8:
time: 151 us; the launch traced here: 150 us
  blocking collectives  114 us (75%)
  starting transfers between devices  17.1 us (11%)
  Pallas kernels  13.1 us (9%)
  local copies, waits for them, and re-layouts  2.59 us (2%)
  waiting for transfers between devices  2.17 us (1%)
    all_to_all x3, blocking collectives, exchange(): lax.all_to_all(values, axis, split_axis=0, concat_axis=0, tiled=True, axi...  68.6 us
    all_gather x1, blocking collectives, shards(): gathered = lax.all_gather(packed, 'row', axis=0, axis_index_groups=FAR_IDS)  33.2 us
    all_to_all x2, starting transfers between devices, exchange(): lax.all_to_all(values, axis, split_axis=0, concat_axis=0, tiled=True, axi...  17.1 us
    all_gather x1, blocking collectives, shards(): cot = lax.all_gather(cotangent, 'col', axis=0, tiled=True)  12.2 us
    pallas_call x1, Pallas kernels, shards(): call(middle_body, [smem(), smem()] + [vmem()] * 6, [((FEAT, ROWS), BF, vm...  3.81 us
  transfers between devices with their start and end apart: 2, of which 1 were waited for; matrix products, arithmetic and copies ran while one was open for 1% of the time, Pallas kernels for 1%

profile of v8, /device:TPU:1, one launch (start us, length us, event | category | flops | bytes accessed | tf_op | source)
XLA Modules:
  0.0 150.4 jit_solution(18157265417785953753)
XLA Ops:
  0.6 1.1 shard_map.121
  1.7 33.2 %all-gather = bf16[2176,128]{1,0:T(8,128)(2,1)S(1)} all-gather(bf16[272,128]{1,0:T(8,128)(2,1)S(1)} %shard_map.121), channel_id=2, replica_groups={{0,64,128,192,256,320,384,448},{4,68,132,196,260,324,388,452},{8,72,136..., dimensions={0}, use_global_device_ids=true | all-gather | bytes 626688 | tf_op jit(solution)/shard_map/all_gather | solution.py:317
  34.9 0.1 dynamic-slice_convert_fusion
  35.0 0.0 copy-start.5
  35.0 1.8 %shard_map.122 = bf16[16,272,128]{2,1,0:T(8,128)(2,1)} custom-call(s32[8,16]{1,0:T(8,128)S(1)} %bitcast.22, bf16[8,272,128]{2,1,0:T(8,128)(2,1)S(1)} %bitcast.20), custom_call_target="tpu_custom_call" | custom-call | flops 1000000 | bytes 1000000 | tf_op jit(solution)/shard_map/pallas_call | solution.py:322
  36.7 0.0 copy-start
  36.8 11.2 %all-to-all-start = ((bf16[16,272,128]{2,1,0:T(8,128)(2,1)}), bf16[16,272,128]{2,1,0:T(8,128)(2,1)S(1)}, u32[]{:S(2)}, u32[]{:S(2)}) async-start(bf16[16,272,128]{2,1,0:T(8,128)(2,1)} %shard_map.122), calls=%async_computation | async-start | bytes 2228224 | tf_op jit(solution)/shard_map/all_to_all | solution.py:282
  48.0 0.0 copy-start.6
  48.0 0.0 copy-start.3
  48.7 0.0 copy-done.5
  48.7 0.8 reshape.32
  49.5 1.1 copy.13
  50.6 12.2 %all_gather.11.cot = bf16[256,512]{1,0:T(8,128)(2,1)} all-gather(bf16[64,512]{1,0:T(8,128)(2,1)} %param.19), channel_id=1, replica_groups=mesh['row'=128,'col'=4] {'col'}, dimensions={0}, use_global_device_ids=true | all-gather | bytes 327680 | tf_op jit(solution)/shard_map/all_gather | solution.py:330
  62.9 0.0 copy-done.6
  62.9 0.0 all-to-all-done.came
  62.9 0.0 copy-done
  62.9 0.0 copy-done.3
  62.9 0.0 copy-start.1
  62.9 0.0 copy-start.2
  62.9 0.0 copy-start.4
  62.9 2.9 %shard_map.123 = bf16[4,64,512]{2,1,0:T(8,128)(2,1)S(1)} custom-call(s32[128]{0:T(128)S(1)} %compare_select_fusion.target, bf16[16,272,128]{2,1,0:T(8,128)(2,1)S(1)} %all-to-all-done.came, bf16[128,64,128]{2,1,0:T(8,128)(2,1)S(1)} %copy-done, bf16[64,512]{1,0:T(8,128)(2,1)S(1)} %copy-done.3, bf16[256,512]{1,0:T(8,128)(2,1)S(1)} %bitcast.17, ...), custom_call_target="tpu_custom_call" | custom-call | flops 1000000 | bytes 1000000 | tf_op jit(solution)/shard_map/pallas_call | solution.py:332
  65.8 8.3 %all_to_all.25 = bf16[4,64,512]{2,1,0:T(8,128)(2,1)S(1)} all-to-all(bf16[4,64,512]{2,1,0:T(8,128)(2,1)S(1)} %shard_map.123), channel_id=1, replica_groups=mesh['row'=128,'col'=4] {'col'}, dimensions={0} | all-to-all | bytes 524288 | tf_op jit(solution)/shard_map/all_to_all | solution.py:282
  74.1 0.0 copy-done.1
  74.1 0.0 copy-done.2
  74.1 0.0 copy-done.4
  74.1 3.8 %shard_map.124 = (bf16[64,512]{1,0:T(8,128)(2,1)}, bf16[16,272,128]{2,1,0:T(8,128)(2,1)S(1)}, f32[64,512]{1,0:T(8,128)S(1)}) custom-call(s32[1]{0:T(128)} %bitcast.2.col, s32[128]{0:T(128)S(1)} %compare_select_fusion.target, bf16[256,512]{1,0:T(8,128)(2,1)S(1)} %bitcast.21, bf16[128,64,128]{2,1,0:T(8,128)(2,1)S(1)} %copy-done, ...), custom_call_target="tpu_custom_call" | custom-call | flops 1000000 | bytes 1000000 | tf_op jit(solution)/shard_map/pallas_call | solution.py:344
  77.9 23.9 %all_to_all.26.came = bf16[16,272,128]{2,1,0:T(8,128)(2,1)S(1)} all-to-all(bf16[16,272,128]{2,1,0:T(8,128)(2,1)S(1)} %get-tuple-element.19), channel_id=1, replica_groups={{28,0,48,12,36,56,20,40,4,60,24,8,52,32,16,44},{92,64,112,76,100,120,84..., dimensions={0} | all-to-all | bytes 2228224 | tf_op jit(solution)/shard_map/all_to_all | solution.py:282
  101.8 1.3 shard_map.125
  103.1 36.4 %all_to_all.27.came = bf16[8,272,128]{2,1,0:T(8,128)(2,1)S(1)} all-to-all(bf16[8,272,128]{2,1,0:T(8,128)(2,1)S(1)} %shard_map.125), channel_id=1, replica_groups={{384,128,448,0,320,192,64,256},{388,68,196,4,324,260,132,452},{392,136,..., dimensions={0} | all-to-all | bytes 1114112 | tf_op jit(solution)/shard_map/all_to_all | solution.py:282
  139.5 0.6 shard_map.127
  140.1 5.8 %all-to-all-start.4 = ((f32[16,8,128]{2,1,0:T(8,128)}), f32[16,8,128]{2,1,0:T(8,128)S(1)}, u32[]{:S(2)}, u32[]{:S(2)}) async-start(f32[16,8,128]{2,1,0:T(8,128)} %shard_map.127), calls=%async_computation.4 | async-start | bytes 131072 | tf_op jit(solution)/shard_map/all_to_all | solution.py:282
  145.9 1.7 %shard_map.126 = bf16[64,512]{1,0:T(8,128)(2,1)} custom-call(s32[1,2]{1,0:T(1,128)} %hubs.3, bf16[8,272,128]{2,1,0:T(8,128)(2,1)S(1)} %all_to_all.27.came, f32[64,512]{1,0:T(8,128)S(1)} %get-tuple-element.20.own_grad), custom_call_target="tpu_custom_call" | custom-call | flops 1000000 | bytes 1000000 | tf_op jit(solution)/shard_map/pallas_call | solution.py:361
  147.6 2.2 %all-to-all-done.4 = f32[16,8,128]{2,1,0:T(8,128)S(1)} async-done(((f32[16,8,128]{2,1,0:T(8,128)}), f32[16,8,128]{2,1,0:T(8,128)S(1)}, u32[]{:S(2)}, u32[]{:S(2)}) %all-to-all-start.4) | async-done | bytes 65568 | tf_op jit(solution)/shard_map/all_to_all | solution.py:282
  149.8 0.6 copy.16
  (2 shorter events, 0.0 us)
Async XLA Ops:
  35.0 13.7 %copy-start.5 = (bf16[256,512]{1,0:T(8,128)(2,1)S(1)}, bf16[256,512]{1,0:T(8,128)(2,1)}, u32[]{:S(2)}) copy-start(bf16[256,512]{1,0:T(8,128)(2,1)} %param.17) | copy-start | bytes 786436
  36.7 26.1 %copy-start = (bf16[128,64,128]{2,1,0:T(8,128)(2,1)S(1)}, bf16[128,64,128]{2,1,0:T(8,128)(2,1)}, u32[]{:S(2)}) copy-start(bf16[128,64,128]{2,1,0:T(8,128)(2,1)} %remote.3) | copy-start | bytes 6291460
  36.8 26.1 %all-to-all-start = ((bf16[16,272,128]{2,1,0:T(8,128)(2,1)}), bf16[16,272,128]{2,1,0:T(8,128)(2,1)S(1)}, u32[]{:S(2)}, u32[]{:S(2)}) async-start(bf16[16,272,128]{2,1,0:T(8,128)(2,1)} %shard_map.122), calls=%async_computation | async-start | bytes 2228224 | tf_op jit(solution)/shard_map/all_to_all | solution.py:282
  48.0 14.9 %copy-start.6 = (s32[1,128]{1,0:T(1,128)S(1)}, s32[1,128]{1,0:T(1,128)}, u32[]{:S(2)}) copy-start(s32[1,128]{1,0:T(1,128)} %param.12) | copy-start | bytes 1540
  48.0 14.9 %copy-start.3 = (bf16[64,512]{1,0:T(8,128)(2,1)S(1)}, bf16[64,512]{1,0:T(8,128)(2,1)}, u32[]{:S(2)}) copy-start(bf16[64,512]{1,0:T(8,128)(2,1)} %feats.3) | copy-start | bytes 196612
  62.9 11.2 %copy-start.1 = (bf16[256,512]{1,0:T(8,128)(2,1)S(1)}, bf16[256,512]{1,0:T(8,128)(2,1)}, u32[]{:S(2)}) copy-start(bf16[256,512]{1,0:T(8,128)(2,1)} %all_gather.11.cot) | copy-start | bytes 786436
  62.9 11.2 %copy-start.2 = (bf16[4,128,128]{2,1,0:T(8,128)(2,1)S(1)}, bf16[4,128,128]{2,1,0:T(8,128)(2,1)}, u32[]{:S(2)}) copy-start(bf16[4,128,128]{2,1,0:T(8,128)(2,1)} %local.1) | copy-start | bytes 393220
  62.9 11.2 %copy-start.4 = (bf16[256,256]{1,0:T(8,128)(2,1)S(1)}, bf16[256,256]{1,0:T(8,128)(2,1)}, u32[]{:S(2)}) copy-start(bf16[256,256]{1,0:T(8,128)(2,1)} %weight.1) | copy-start | bytes 393220
  140.1 9.7 %all-to-all-start.4 = ((f32[16,8,128]{2,1,0:T(8,128)}), f32[16,8,128]{2,1,0:T(8,128)S(1)}, u32[]{:S(2)}, u32[]{:S(2)}) async-start(f32[16,8,128]{2,1,0:T(8,128)} %shard_map.127), calls=%async_computation.4 | async-start | bytes 131072 | tf_op jit(solution)/shard_map/all_to_all | solution.py:282

commit v9 on v7

--- a/solution.py
+++ b/solution.py
@@ -149,20 +149,28 @@
 
 
 def forward_body(
+    col,
     target,
     came,
     remote,
-    feats_far,
+    feats,
+    adj,
     local_far,
-    adj_far,
+    cot_0,
+    cot_1,
+    cot_2,
+    cot_3,
     out,
-    feats,
+    cot,
     local,
-    adj,
     total,
     sems,
 ):
-    copies = start_all([(feats_far, feats), (local_far, local), (adj_far, adj)], sems)
+    pairs = [(local_far, local)]
+    for hop, value in enumerate((cot_0, cot_1, cot_2, cot_3)):
+        source = lax.rem(col[0] + COLS - hop, COLS)
+        pairs.append((value, cot.at[pl.ds(pl.multiple_of(source * FEAT, FEAT), FEAT)]))
+    copies = start_all(pairs, sems)
     total[...] = jnp.zeros_like(total)
 
     for s in range(FAR):
@@ -193,9 +201,9 @@
     agg,
     remote,
     weight,
-    cot,
     local,
     adj,
+    cot,
     output,
     back,
     own_grad,
@@ -231,7 +239,7 @@
     hub = jnp.concatenate([hub[:PEERS], hub[PEERS:]], axis=1)
     for n in range(NEAR):
         m = ORDER[n]
-        i, j = m // 2, m % 2
+        i, j = n // 2, n % 2
         tile = weight_grad[i * 8 : (i + 1) * 8, j * 128 : (j + 1) * 128]
         back[n, FAR * HALF :, :] = jnp.concatenate([hub[m * 8 : (m + 1) * 8], tile], axis=0).astype(BF)
 
@@ -340,28 +348,29 @@
     )(piece, gathered)
     picked, cotangent = lax.optimization_barrier((picked, cotangent))
     came = exchange(picked, "row", NEAR_GROUPS)
-    cot = lax.all_gather(cotangent, "col", axis=0, tiled=True)
-    came, cot, col, place = lax.optimization_barrier((came, cot, col, place))
-    small = [pltpu.VMEM((BLOCKS, BLK, BLK), BF), pltpu.VMEM((2 * PEERS, ROWS), BF)]
-    (agg,) = call(
+    cots = [cotangent]
+    for hop in range(1, COLS):
+        turn = [(c, (c + hop) % COLS) for c in range(COLS)]
+        cots.append(lax.ppermute(cotangent, "col", turn))
+    came, cots, col, place = lax.optimization_barrier((came, cots, col, place))
+    wide = (COLS * FEAT, ROWS)
+    agg, cot = call(
         forward_body,
-        [smem(), vmem(), vmem()] + [away()] * 3,
-        [((COLS, FEAT, ROWS), BF, vmem())],
-        [pltpu.VMEM((FEAT, ROWS), BF)]
-        + small
-        + [
+        [smem(), smem()] + [vmem()] * 4 + [away()] * 5,
+        [((COLS, FEAT, ROWS), BF, vmem()), (wide, BF, vmem())],
+        [
+            pltpu.VMEM((BLOCKS, BLK, BLK), BF),
             pltpu.VMEM((BLOCKS + 1, HALF, 2 * BLK), F32),
-            pltpu.SemaphoreType.DMA((3,)),
+            pltpu.SemaphoreType.DMA((1 + COLS,)),
         ],
-    )(target, came, remote_values, *map(stay, (features, local_values, adj)))
-    wide = (COLS * FEAT, ROWS)
+    )(col, target, came, remote_values, features, adj, *map(stay, (local_values, *cots)))
     agg = exchange(agg, "col").reshape(wide)
     output, back, own_grad = call(
         middle_body,
         [smem(), smem()] + [vmem()] * 6,
         [((FEAT, ROWS), BF, vmem()), (near_all, BF, vmem()), ((FEAT, ROWS), F32, vmem())],
         [pltpu.VMEM(wide, BF), pltpu.VMEM((BLOCKS + 1, FEAT, BLK), BF)],
-    )(col, target, agg, remote_values, weight, cot, local_values, adj)
+    )(col, target, agg, remote_values, weight, local_values, adj, cot)
     back = exchange(back, "row", NEAR_GROUPS)
     far_all = (FAR, BACK_ROWS, 128)
     (sums,) = call(
@@ -372,7 +381,7 @@
     )(place, piece, back)
     sums = exchange(sums, "row", FAR_GROUPS)
     (chunk,) = call(chunk_body, [vmem()], [((NEAR, 8, 128), F32, vmem())])(sums)
-    tiles = exchange(chunk, "row", NEAR_IDS)
+    tiles = exchange(chunk, "row", NEAR_GROUPS)
     (grad_input,) = call(
         final_body, [smem(), vmem(), vmem()], [((FEAT, ROWS), BF, vmem())]
     )(stay(hub_rows), sums, own_grad)

time: 152 us -> 151 us (level)
  starting transfers between devices: 16.4 us -> 27.8 us
  blocking collectives: 113 us -> 103 us
  waiting for transfers between devices: 4.57 us -> 2.3 us
    ppermute x0 -> x3, starting transfers between devices: none -> 10.9 us  [shards(): cots.append(lax.ppermute(cotangent, 'col', turn))]
    all_gather x1 -> x0, blocking collectives: 10.6 us -> none  [shards(): cot = lax.all_gather(cotangent, 'col', axis=0, tiled=True)]
    all_to_all x2, waiting for transfers between devices: 4.57 us -> 2.29 us  [exchange(): lax.all_to_all(values, axis, split_axis=0, concat_axis=0, tiled=True, axi...]
  transfers between devices with their start and end apart: 2 -> 5, of which waited for: 2 -> 2; matrix products, arithmetic and copies ran while one was open for 1% -> 1% of each run, Pallas kernels for 1% -> 1%
where the time goes in v9:
time: 151 us; the launch traced here: 150 us
  blocking collectives  103 us (68%)
  starting transfers between devices  27.8 us (18%)
  Pallas kernels  13.2 us (9%)
  local copies, waits for them, and re-layouts  2.57 us (2%)
  waiting for transfers between devices  2.3 us (2%)
    all_to_all x3, blocking collectives, exchange(): lax.all_to_all(values, axis, split_axis=0, concat_axis=0, tiled=True, axi...  69.3 us
    all_gather x1, blocking collectives, shards(): gathered = lax.all_gather(packed, 'row', axis=0, axis_index_groups=FAR_IDS)  33.2 us
    all_to_all x2, starting transfers between devices, exchange(): lax.all_to_all(values, axis, split_axis=0, concat_axis=0, tiled=True, axi...  16.9 us
    ppermute x3, starting transfers between devices, shards(): cots.append(lax.ppermute(cotangent, 'col', turn))  10.9 us
    pallas_call x1, Pallas kernels, shards(): call(middle_body, [smem(), smem()] + [vmem()] * 6, [((FEAT, ROWS), BF, vm...  3.81 us
    pallas_call x1, Pallas kernels, shards(): call(forward_body, [smem(), smem()] + [vmem()] * 4 + [away()] * 5, [((COL...  3.04 us
  transfers between devices with their start and end apart: 5, of which 2 were waited for; matrix products, arithmetic and copies ran while one was open for 1% of the time, Pallas kernels for 1%

profile of v9, /device:TPU:1, one launch (start us, length us, event | category | flops | bytes accessed | tf_op | source)
XLA Modules:
  0.0 150.0 jit_solution(12899603528784248132)
XLA Ops:
  0.6 1.1 shard_map.121
  1.7 33.2 %all-gather = bf16[2176,128]{1,0:T(8,128)(2,1)S(1)} all-gather(bf16[272,128]{1,0:T(8,128)(2,1)S(1)} %shard_map.121), channel_id=2, replica_groups={{0,64,128,192,256,320,384,448},{4,68,132,196,260,324,388,452},{8,72,136..., dimensions={0}, use_global_device_ids=true | all-gather | bytes 626688 | tf_op jit(solution)/shard_map/all_gather | solution.py:338
  34.9 0.1 dynamic-slice_convert_fusion
  35.0 0.0 copy-start.4
  35.0 1.8 %shard_map.122 = bf16[16,272,128]{2,1,0:T(8,128)(2,1)} custom-call(s32[8,16]{1,0:T(8,128)S(1)} %bitcast.22, bf16[8,272,128]{2,1,0:T(8,128)(2,1)S(1)} %bitcast.20), custom_call_target="tpu_custom_call" | custom-call | flops 1000000 | bytes 1000000 | tf_op jit(solution)/shard_map/pallas_call | solution.py:343
  36.7 0.0 copy-start.5
  36.8 0.0 copy-start
  36.8 11.2 %all-to-all-start = ((bf16[16,272,128]{2,1,0:T(8,128)(2,1)}), bf16[16,272,128]{2,1,0:T(8,128)(2,1)S(1)}, u32[]{:S(2)}, u32[]{:S(2)}) async-start(bf16[16,272,128]{2,1,0:T(8,128)(2,1)} %shard_map.122), calls=%async_computation | async-start | bytes 2228224 | tf_op jit(solution)/shard_map/all_to_all | solution.py:303
  48.0 0.0 copy-start.2
  48.0 3.3 %collective-permute-start = (bf16[64,512]{1,0:T(8,128)(2,1)}, bf16[64,512]{1,0:T(8,128)(2,1)}, u32[]{:S(2)}, u32[]{:S(2)}) collective-permute-start(bf16[64,512]{1,0:T(8,128)(2,1)} %cot_0), channel_id=1, source_target_pairs={{0,1},{1,2},{2,3},{3,0},{4,5},{5,6},{6,7},{7,4},{8,9},{9,10},{10,1... | collective-permute-start | bytes 196616 | tf_op jit(solution)/shard_map/ppermute | solution.py:354
  51.4 4.5 %collective-permute-start.1 = (bf16[64,512]{1,0:T(8,128)(2,1)}, bf16[64,512]{1,0:T(8,128)(2,1)}, u32[]{:S(2)}, u32[]{:S(2)}) collective-permute-start(bf16[64,512]{1,0:T(8,128)(2,1)} %cot_0), channel_id=1, source_target_pairs={{0,2},{1,3},{2,0},{3,1},{4,6},{5,7},{6,4},{7,5},{8,10},{9,11},{10,... | collective-permute-start | bytes 196616 | tf_op jit(solution)/shard_map/ppermute | solution.py:354
  55.9 3.0 %collective-permute-start.2 = (bf16[64,512]{1,0:T(8,128)(2,1)}, bf16[64,512]{1,0:T(8,128)(2,1)}, u32[]{:S(2)}, u32[]{:S(2)}) collective-permute-start(bf16[64,512]{1,0:T(8,128)(2,1)} %cot_0), channel_id=1, source_target_pairs={{0,3},{1,0},{2,1},{3,2},{4,7},{5,4},{6,5},{7,6},{8,11},{9,8},{10,9... | collective-permute-start | bytes 196616 | tf_op jit(solution)/shard_map/ppermute | solution.py:354
  59.5 0.0 copy-done.5
  59.6 0.0 copy-done.4
  59.6 0.8 reshape.32
  60.4 1.1 copy.13
  61.5 0.0 collective-permute-done.cot_1
  61.5 0.0 collective-permute-done.1.cot_2
  61.6 0.0 collective-permute-done.2.cot_3
  61.6 0.1 all-to-all-done.came
  61.7 0.0 copy-done
  61.7 0.0 copy-done.2
  61.7 0.0 copy-start.1
  61.7 0.0 copy-start.3
  61.7 3.0 %shard_map.123 = (bf16[4,64,512]{2,1,0:T(8,128)(2,1)S(1)}, bf16[256,512]{1,0:T(8,128)(2,1)S(1)}) custom-call(s32[1]{0:T(128)} %bitcast.2.col, s32[128]{0:T(128)S(1)} %compare_select_fusion.target, bf16[16,272,128]{2,1,0:T(8,128)(2,1)S(1)} %all-to-all-done.came, bf16[128,64,128]{2,1,0:T(8,128)(2,1)S(1)} %copy-done, bf16[64,512]{1,0:T(8,128)(2,1)S(1)} %copy-done.2, ...), custom_call_target="tpu_custom_call" | custom-call | flops 1000000 | bytes 1000000 | tf_op jit(solution)/shard_map/pallas_call | solution.py:357
  64.7 9.5 %all_to_all.25 = bf16[4,64,512]{2,1,0:T(8,128)(2,1)S(1)} all-to-all(bf16[4,64,512]{2,1,0:T(8,128)(2,1)S(1)} %get-tuple-element.25), channel_id=1, replica_groups=mesh['row'=128,'col'=4] {'col'}, dimensions={0} | all-to-all | bytes 524288 | tf_op jit(solution)/shard_map/all_to_all | solution.py:303
  74.3 0.0 copy-done.1
  74.3 0.0 copy-done.3
  74.3 3.8 %shard_map.124 = (bf16[64,512]{1,0:T(8,128)(2,1)}, bf16[16,272,128]{2,1,0:T(8,128)(2,1)S(1)}, f32[64,512]{1,0:T(8,128)S(1)}) custom-call(s32[1]{0:T(128)} %bitcast.2.col, s32[128]{0:T(128)S(1)} %compare_select_fusion.target, bf16[256,512]{1,0:T(8,128)(2,1)S(1)} %bitcast.21, bf16[128,64,128]{2,1,0:T(8,128)(2,1)S(1)} %copy-done, ...), custom_call_target="tpu_custom_call" | custom-call | flops 1000000 | bytes 1000000 | tf_op jit(solution)/shard_map/pallas_call | solution.py:368
  78.1 23.3 %all_to_all.26.came = bf16[16,272,128]{2,1,0:T(8,128)(2,1)S(1)} all-to-all(bf16[16,272,128]{2,1,0:T(8,128)(2,1)S(1)} %get-tuple-element.29), channel_id=1, replica_groups={{28,0,48,12,36,56,20,40,4,60,24,8,52,32,16,44},{92,64,112,76,100,120,84..., dimensions={0} | all-to-all | bytes 2228224 | tf_op jit(solution)/shard_map/all_to_all | solution.py:303
  101.4 1.2 shard_map.125
  102.7 36.5 %all_to_all.27.came = bf16[8,272,128]{2,1,0:T(8,128)(2,1)S(1)} all-to-all(bf16[8,272,128]{2,1,0:T(8,128)(2,1)S(1)} %shard_map.125), channel_id=1, replica_groups={{384,128,448,0,320,192,64,256},{388,68,196,4,324,260,132,452},{392,136,..., dimensions={0} | all-to-all | bytes 1114112 | tf_op jit(solution)/shard_map/all_to_all | solution.py:303
  139.1 0.6 shard_map.127
  139.8 5.7 %all-to-all-start.4 = ((f32[16,8,128]{2,1,0:T(8,128)}), f32[16,8,128]{2,1,0:T(8,128)S(1)}, u32[]{:S(2)}, u32[]{:S(2)}) async-start(f32[16,8,128]{2,1,0:T(8,128)} %shard_map.127), calls=%async_computation.4 | async-start | bytes 131072 | tf_op jit(solution)/shard_map/all_to_all | solution.py:303
  145.5 1.7 %shard_map.126 = bf16[64,512]{1,0:T(8,128)(2,1)} custom-call(s32[1,2]{1,0:T(1,128)} %hubs.3, bf16[8,272,128]{2,1,0:T(8,128)(2,1)S(1)} %all_to_all.27.came, f32[64,512]{1,0:T(8,128)S(1)} %get-tuple-element.30.own_grad), custom_call_target="tpu_custom_call" | custom-call | flops 1000000 | bytes 1000000 | tf_op jit(solution)/shard_map/pallas_call | solution.py:385
  147.2 2.2 %all-to-all-done.4 = f32[16,8,128]{2,1,0:T(8,128)S(1)} async-done(((f32[16,8,128]{2,1,0:T(8,128)}), f32[16,8,128]{2,1,0:T(8,128)S(1)}, u32[]{:S(2)}, u32[]{:S(2)}) %all-to-all-start.4) | async-done | bytes 65568 | tf_op jit(solution)/shard_map/all_to_all | solution.py:303
  149.3 0.6 copy.16
  (2 shorter events, 0.0 us)
Async XLA Ops:
  35.0 24.6 %copy-start.4 = (bf16[256,512]{1,0:T(8,128)(2,1)S(1)}, bf16[256,512]{1,0:T(8,128)(2,1)}, u32[]{:S(2)}) copy-start(bf16[256,512]{1,0:T(8,128)(2,1)} %param.17) | copy-start | bytes 786436
  36.7 22.8 %copy-start.5 = (s32[1,128]{1,0:T(1,128)S(1)}, s32[1,128]{1,0:T(1,128)}, u32[]{:S(2)}) copy-start(s32[1,128]{1,0:T(1,128)} %param.12) | copy-start | bytes 1540
  36.8 24.9 %copy-start = (bf16[128,64,128]{2,1,0:T(8,128)(2,1)S(1)}, bf16[128,64,128]{2,1,0:T(8,128)(2,1)}, u32[]{:S(2)}) copy-start(bf16[128,64,128]{2,1,0:T(8,128)(2,1)} %remote.3) | copy-start | bytes 6291460
  36.8 24.9 %all-to-all-start = ((bf16[16,272,128]{2,1,0:T(8,128)(2,1)}), bf16[16,272,128]{2,1,0:T(8,128)(2,1)S(1)}, u32[]{:S(2)}, u32[]{:S(2)}) async-start(bf16[16,272,128]{2,1,0:T(8,128)(2,1)} %shard_map.122), calls=%async_computation | async-start | bytes 2228224 | tf_op jit(solution)/shard_map/all_to_all | solution.py:303
  48.0 13.7 %copy-start.2 = (bf16[64,512]{1,0:T(8,128)(2,1)S(1)}, bf16[64,512]{1,0:T(8,128)(2,1)}, u32[]{:S(2)}) copy-start(bf16[64,512]{1,0:T(8,128)(2,1)} %feats.3) | copy-start | bytes 196612
  48.0 13.5 %collective-permute-start = (bf16[64,512]{1,0:T(8,128)(2,1)}, bf16[64,512]{1,0:T(8,128)(2,1)}, u32[]{:S(2)}, u32[]{:S(2)}) collective-permute-start(bf16[64,512]{1,0:T(8,128)(2,1)} %cot_0), channel_id=1, source_target_pairs={{0,1},{1,2},{2,3},{3,0},{4,5},{5,6},{6,7},{7,4},{8,9},{9,10},{10,1... | collective-permute-start | bytes 196616 | tf_op jit(solution)/shard_map/ppermute | solution.py:354
  51.4 10.2 %collective-permute-start.1 = (bf16[64,512]{1,0:T(8,128)(2,1)}, bf16[64,512]{1,0:T(8,128)(2,1)}, u32[]{:S(2)}, u32[]{:S(2)}) collective-permute-start(bf16[64,512]{1,0:T(8,128)(2,1)} %cot_0), channel_id=1, source_target_pairs={{0,2},{1,3},{2,0},{3,1},{4,6},{5,7},{6,4},{7,5},{8,10},{9,11},{10,... | collective-permute-start | bytes 196616 | tf_op jit(solution)/shard_map/ppermute | solution.py:354
  55.9 5.7 %collective-permute-start.2 = (bf16[64,512]{1,0:T(8,128)(2,1)}, bf16[64,512]{1,0:T(8,128)(2,1)}, u32[]{:S(2)}, u32[]{:S(2)}) collective-permute-start(bf16[64,512]{1,0:T(8,128)(2,1)} %cot_0), channel_id=1, source_target_pairs={{0,3},{1,0},{2,1},{3,2},{4,7},{5,4},{6,5},{7,6},{8,11},{9,8},{10,9... | collective-permute-start | bytes 196616 | tf_op jit(solution)/shard_map/ppermute | solution.py:354
  61.7 12.6 %copy-start.1 = (bf16[4,128,128]{2,1,0:T(8,128)(2,1)S(1)}, bf16[4,128,128]{2,1,0:T(8,128)(2,1)}, u32[]{:S(2)}) copy-start(bf16[4,128,128]{2,1,0:T(8,128)(2,1)} %local.1) | copy-start | bytes 393220
  61.7 12.6 %copy-start.3 = (bf16[256,256]{1,0:T(8,128)(2,1)S(1)}, bf16[256,256]{1,0:T(8,128)(2,1)}, u32[]{:S(2)}) copy-start(bf16[256,256]{1,0:T(8,128)(2,1)} %weight.1) | copy-start | bytes 393220
  139.8 9.6 %all-to-all-start.4 = ((f32[16,8,128]{2,1,0:T(8,128)}), f32[16,8,128]{2,1,0:T(8,128)S(1)}, u32[]{:S(2)}, u32[]{:S(2)}) async-start(f32[16,8,128]{2,1,0:T(8,128)} %shard_map.127), calls=%async_computation.4 | async-start | bytes 131072 | tf_op jit(solution)/shard_map/all_to_all | solution.py:303

commit v10 on v9

--- a/solution.py
+++ b/solution.py
@@ -24,7 +24,7 @@
 NEAR_ROWS = FAR * HALF + 16
 BACK_ROWS = NEAR_ROWS
 VMEM_BYTES = 30 * 1024 * 1024
-ORDER = (7, 0, 12, 3, 9, 14, 5, 10, 1, 15, 6, 2, 13, 8, 4, 11)
+ORDER = (1, 5, 4, 2, 8, 13, 14, 9, 0, 15, 11, 3, 6, 7, 10, 12)
 FAR_ORDERS = (
     (6, 2, 7, 0, 5, 3, 1, 4),
     (6, 1, 3, 0, 5, 4, 2, 7),
@@ -173,14 +173,19 @@
     copies = start_all(pairs, sems)
     total[...] = jnp.zeros_like(total)
 
-    for s in range(FAR):
-        for first in range(0, NEAR, 8):
-            parts = []
-            for n in range(first, first + 8):
-                q = s * NEAR + ORDER[n]
-                parts.append(dot(came[n, s * HALF : (s + 1) * HALF, :], twice(remote[q])))
-            for n in range(first, first + 8):
-                total[target[s * NEAR + ORDER[n]]] += parts[n - first]
+    def step(i, carry):
+        for s in (4 * i + k for k in range(4)):
+            start = pl.multiple_of(s * HALF, HALF)
+            for first in range(0, NEAR, 8):
+                parts = []
+                for n in range(first, first + 8):
+                    q = s * NEAR + ORDER[n]
+                    parts.append(dot(came[n, pl.ds(start, HALF), :], twice(remote[q])))
+                for n in range(first, first + 8):
+                    total[target[s * NEAR + ORDER[n]]] += parts[n - first]
+        return carry
+
+    lax.fori_loop(0, FAR // 4, step, 0)
     for copy in copies:
         copy.wait()
     hub_rows = jnp.concatenate([came[SLOT[n], FAR * HALF :, :][:8] for n in range(NEAR)], axis=0)

time: 151 us -> 150 us (level)
  waiting for transfers between devices: 2.3 us -> 5.89 us
  starting transfers between devices: 27.8 us -> 25.1 us
    all_to_all x2, waiting for transfers between devices: 2.29 us -> 5.89 us  [exchange(): lax.all_to_all(values, axis, split_axis=0, concat_axis=0, tiled=True, axi...]
    all_to_all x2, starting transfers between devices: 16.9 us -> 14.2 us  [exchange(): lax.all_to_all(values, axis, split_axis=0, concat_axis=0, tiled=True, axi...]
where the time goes in v10:
time: 150 us
  blocking collectives  102 us (68%)
  starting transfers between devices  25.1 us (17%)
  Pallas kernels  12.5 us (8%)
  waiting for transfers between devices  5.89 us (4%)
  local copies, waits for them, and re-layouts  2.57 us (2%)
    all_to_all x3, blocking collectives, exchange(): lax.all_to_all(values, axis, split_axis=0, concat_axis=0, tiled=True, axi...  68.9 us
    all_gather x1, blocking collectives, shards(): gathered = lax.all_gather(packed, 'row', axis=0, axis_index_groups=FAR_IDS)  33.2 us
    all_to_all x2, starting transfers between devices, exchange(): lax.all_to_all(values, axis, split_axis=0, concat_axis=0, tiled=True, axi...  14.2 us
    ppermute x3, starting transfers between devices, shards(): cots.append(lax.ppermute(cotangent, 'col', turn))  10.9 us
    all_to_all x2, waiting for transfers between devices, exchange(): lax.all_to_all(values, axis, split_axis=0, concat_axis=0, tiled=True, axi...  5.89 us
    pallas_call x1, Pallas kernels, shards(): call(middle_body, [smem(), smem()] + [vmem()] * 6, [((FEAT, ROWS), BF, vm...  3.81 us
  transfers between devices with their start and end apart: 5, of which 2 were waited for; matrix products, arithmetic and copies ran while one was open for 1% of the time, Pallas kernels for 1%

profile of v10, /device:TPU:1, one launch (start us, length us, event | category | flops | bytes accessed | tf_op | source)
XLA Modules:
  0.0 149.7 jit_solution(11578764860976626045)
XLA Ops:
  0.6 1.1 shard_map.121
  1.7 33.2 %all-gather = bf16[2176,128]{1,0:T(8,128)(2,1)S(1)} all-gather(bf16[272,128]{1,0:T(8,128)(2,1)S(1)} %shard_map.121), channel_id=2, replica_groups={{0,64,128,192,256,320,384,448},{4,68,132,196,260,324,388,452},{8,72,136..., dimensions={0}, use_global_device_ids=true | all-gather | bytes 626688 | tf_op jit(solution)/shard_map/all_gather | solution.py:343
  34.9 0.1 dynamic-slice_convert_fusion
  35.0 0.0 copy-start.4
  35.0 1.8 %shard_map.122 = bf16[16,272,128]{2,1,0:T(8,128)(2,1)} custom-call(s32[8,16]{1,0:T(8,128)S(1)} %bitcast.22, bf16[8,272,128]{2,1,0:T(8,128)(2,1)S(1)} %bitcast.20), custom_call_target="tpu_custom_call" | custom-call | flops 1000000 | bytes 1000000 | tf_op jit(solution)/shard_map/pallas_call | solution.py:348
  36.7 0.0 copy-start.5
  36.8 0.0 copy-start
  36.8 10.4 %all-to-all-start = ((bf16[16,272,128]{2,1,0:T(8,128)(2,1)}), bf16[16,272,128]{2,1,0:T(8,128)(2,1)S(1)}, u32[]{:S(2)}, u32[]{:S(2)}) async-start(bf16[16,272,128]{2,1,0:T(8,128)(2,1)} %shard_map.122), calls=%async_computation | async-start | bytes 2228224 | tf_op jit(solution)/shard_map/all_to_all | solution.py:308
  47.2 0.0 copy-start.2
  47.2 3.3 %collective-permute-start = (bf16[64,512]{1,0:T(8,128)(2,1)}, bf16[64,512]{1,0:T(8,128)(2,1)}, u32[]{:S(2)}, u32[]{:S(2)}) collective-permute-start(bf16[64,512]{1,0:T(8,128)(2,1)} %cot_0), channel_id=1, source_target_pairs={{0,1},{1,2},{2,3},{3,0},{4,5},{5,6},{6,7},{7,4},{8,9},{9,10},{10,1... | collective-permute-start | bytes 196616 | tf_op jit(solution)/shard_map/ppermute | solution.py:359
  50.6 4.5 %collective-permute-start.1 = (bf16[64,512]{1,0:T(8,128)(2,1)}, bf16[64,512]{1,0:T(8,128)(2,1)}, u32[]{:S(2)}, u32[]{:S(2)}) collective-permute-start(bf16[64,512]{1,0:T(8,128)(2,1)} %cot_0), channel_id=1, source_target_pairs={{0,2},{1,3},{2,0},{3,1},{4,6},{5,7},{6,4},{7,5},{8,10},{9,11},{10,... | collective-permute-start | bytes 196616 | tf_op jit(solution)/shard_map/ppermute | solution.py:359
  55.1 3.0 %collective-permute-start.2 = (bf16[64,512]{1,0:T(8,128)(2,1)}, bf16[64,512]{1,0:T(8,128)(2,1)}, u32[]{:S(2)}, u32[]{:S(2)}) collective-permute-start(bf16[64,512]{1,0:T(8,128)(2,1)} %cot_0), channel_id=1, source_target_pairs={{0,3},{1,0},{2,1},{3,2},{4,7},{5,4},{6,5},{7,6},{8,11},{9,8},{10,9... | collective-permute-start | bytes 196616 | tf_op jit(solution)/shard_map/ppermute | solution.py:359
  58.8 0.0 copy-done.5
  58.8 0.0 copy-done.4
  58.8 0.8 reshape.32
  59.6 1.1 copy.13
  60.7 0.0 collective-permute-done.cot_1
  60.8 0.0 collective-permute-done.1.cot_2
  60.8 0.0 collective-permute-done.2.cot_3
  60.8 1.9 %all-to-all-done.came = bf16[16,272,128]{2,1,0:T(8,128)(2,1)S(1)} async-done(((bf16[16,272,128]{2,1,0:T(8,128)(2,1)}), bf16[16,272,128]{2,1,0:T(8,128)(2,1)S(1)}, u32[]{:S(2)}, u32[]{:S(2)}) %all-to-all-start) | async-done | bytes 1114144 | tf_op jit(solution)/shard_map/all_to_all | solution.py:308
  62.7 0.0 copy-done
  62.7 0.0 copy-done.2
  62.7 0.0 copy-start.1
  62.7 0.0 copy-start.3
  62.7 2.3 %shard_map.123 = (bf16[4,64,512]{2,1,0:T(8,128)(2,1)S(1)}, bf16[256,512]{1,0:T(8,128)(2,1)S(1)}) custom-call(s32[1]{0:T(128)} %bitcast.2.col, s32[128]{0:T(128)S(1)} %compare_select_fusion.target, bf16[16,272,128]{2,1,0:T(8,128)(2,1)S(1)} %all-to-all-done.came, bf16[128,64,128]{2,1,0:T(8,128)(2,1)S(1)} %copy-done, bf16[64,512]{1,0:T(8,128)(2,1)S(1)} %copy-done.2, ...), custom_call_target="tpu_custom_call" | custom-call | flops 1000000 | bytes 1000000 | tf_op jit(solution)/shard_map/pallas_call | solution.py:362
  65.0 9.5 %all_to_all.25 = bf16[4,64,512]{2,1,0:T(8,128)(2,1)S(1)} all-to-all(bf16[4,64,512]{2,1,0:T(8,128)(2,1)S(1)} %get-tuple-element.25), channel_id=1, replica_groups=mesh['row'=128,'col'=4] {'col'}, dimensions={0} | all-to-all | bytes 524288 | tf_op jit(solution)/shard_map/all_to_all | solution.py:308
  74.5 0.0 copy-done.1
  74.5 0.0 copy-done.3
  74.5 3.8 %shard_map.124 = (bf16[64,512]{1,0:T(8,128)(2,1)}, bf16[16,272,128]{2,1,0:T(8,128)(2,1)S(1)}, f32[64,512]{1,0:T(8,128)S(1)}) custom-call(s32[1]{0:T(128)} %bitcast.2.col, s32[128]{0:T(128)S(1)} %compare_select_fusion.target, bf16[256,512]{1,0:T(8,128)(2,1)S(1)} %bitcast.21, bf16[128,64,128]{2,1,0:T(8,128)(2,1)S(1)} %copy-done, ...), custom_call_target="tpu_custom_call" | custom-call | flops 1000000 | bytes 1000000 | tf_op jit(solution)/shard_map/pallas_call | solution.py:373
  78.3 22.6 %all_to_all.26.came = bf16[16,272,128]{2,1,0:T(8,128)(2,1)S(1)} all-to-all(bf16[16,272,128]{2,1,0:T(8,128)(2,1)S(1)} %get-tuple-element.29), channel_id=1, replica_groups={{4,20,16,8,32,52,56,36,0,60,44,12,24,28,40,48},{68,84,80,72,96,116,120,..., dimensions={0} | all-to-all | bytes 2228224 | tf_op jit(solution)/shard_map/all_to_all | solution.py:308
  100.9 1.3 shard_map.125
  102.2 36.8 %all_to_all.27.came = bf16[8,272,128]{2,1,0:T(8,128)(2,1)S(1)} all-to-all(bf16[8,272,128]{2,1,0:T(8,128)(2,1)S(1)} %shard_map.125), channel_id=1, replica_groups={{384,128,448,0,320,192,64,256},{388,68,196,4,324,260,132,452},{392,136,..., dimensions={0} | all-to-all | bytes 1114112 | tf_op jit(solution)/shard_map/all_to_all | solution.py:308
  138.9 0.6 shard_map.127
  139.6 3.8 %all-to-all-start.4 = ((f32[16,8,128]{2,1,0:T(8,128)}), f32[16,8,128]{2,1,0:T(8,128)S(1)}, u32[]{:S(2)}, u32[]{:S(2)}) async-start(f32[16,8,128]{2,1,0:T(8,128)} %shard_map.127), calls=%async_computation.4 | async-start | bytes 131072 | tf_op jit(solution)/shard_map/all_to_all | solution.py:308
  143.4 1.7 %shard_map.126 = bf16[64,512]{1,0:T(8,128)(2,1)} custom-call(s32[1,2]{1,0:T(1,128)} %hubs.3, bf16[8,272,128]{2,1,0:T(8,128)(2,1)S(1)} %all_to_all.27.came, f32[64,512]{1,0:T(8,128)S(1)} %get-tuple-element.30.own_grad), custom_call_target="tpu_custom_call" | custom-call | flops 1000000 | bytes 1000000 | tf_op jit(solution)/shard_map/pallas_call | solution.py:390
  145.1 4.0 %all-to-all-done.4 = f32[16,8,128]{2,1,0:T(8,128)S(1)} async-done(((f32[16,8,128]{2,1,0:T(8,128)}), f32[16,8,128]{2,1,0:T(8,128)S(1)}, u32[]{:S(2)}, u32[]{:S(2)}) %all-to-all-start.4) | async-done | bytes 65568 | tf_op jit(solution)/shard_map/all_to_all | solution.py:308
  149.1 0.6 copy.16
  (2 shorter events, 0.0 us)
Async XLA Ops:
  35.0 23.8 %copy-start.4 = (bf16[256,512]{1,0:T(8,128)(2,1)S(1)}, bf16[256,512]{1,0:T(8,128)(2,1)}, u32[]{:S(2)}) copy-start(bf16[256,512]{1,0:T(8,128)(2,1)} %param.17) | copy-start | bytes 786436
  36.7 22.0 %copy-start.5 = (s32[1,128]{1,0:T(1,128)S(1)}, s32[1,128]{1,0:T(1,128)}, u32[]{:S(2)}) copy-start(s32[1,128]{1,0:T(1,128)} %param.12) | copy-start | bytes 1540
  36.8 25.9 %copy-start = (bf16[128,64,128]{2,1,0:T(8,128)(2,1)S(1)}, bf16[128,64,128]{2,1,0:T(8,128)(2,1)}, u32[]{:S(2)}) copy-start(bf16[128,64,128]{2,1,0:T(8,128)(2,1)} %remote.3) | copy-start | bytes 6291460
  36.8 25.9 %all-to-all-start = ((bf16[16,272,128]{2,1,0:T(8,128)(2,1)}), bf16[16,272,128]{2,1,0:T(8,128)(2,1)S(1)}, u32[]{:S(2)}, u32[]{:S(2)}) async-start(bf16[16,272,128]{2,1,0:T(8,128)(2,1)} %shard_map.122), calls=%async_computation | async-start | bytes 2228224 | tf_op jit(solution)/shard_map/all_to_all | solution.py:308
  47.2 15.4 %copy-start.2 = (bf16[64,512]{1,0:T(8,128)(2,1)S(1)}, bf16[64,512]{1,0:T(8,128)(2,1)}, u32[]{:S(2)}) copy-start(bf16[64,512]{1,0:T(8,128)(2,1)} %feats.3) | copy-start | bytes 196612
  47.2 13.5 %collective-permute-start = (bf16[64,512]{1,0:T(8,128)(2,1)}, bf16[64,512]{1,0:T(8,128)(2,1)}, u32[]{:S(2)}, u32[]{:S(2)}) collective-permute-start(bf16[64,512]{1,0:T(8,128)(2,1)} %cot_0), channel_id=1, source_target_pairs={{0,1},{1,2},{2,3},{3,0},{4,5},{5,6},{6,7},{7,4},{8,9},{9,10},{10,1... | collective-permute-start | bytes 196616 | tf_op jit(solution)/shard_map/ppermute | solution.py:359
  50.6 10.2 %collective-permute-start.1 = (bf16[64,512]{1,0:T(8,128)(2,1)}, bf16[64,512]{1,0:T(8,128)(2,1)}, u32[]{:S(2)}, u32[]{:S(2)}) collective-permute-start(bf16[64,512]{1,0:T(8,128)(2,1)} %cot_0), channel_id=1, source_target_pairs={{0,2},{1,3},{2,0},{3,1},{4,6},{5,7},{6,4},{7,5},{8,10},{9,11},{10,... | collective-permute-start | bytes 196616 | tf_op jit(solution)/shard_map/ppermute | solution.py:359
  55.1 5.7 %collective-permute-start.2 = (bf16[64,512]{1,0:T(8,128)(2,1)}, bf16[64,512]{1,0:T(8,128)(2,1)}, u32[]{:S(2)}, u32[]{:S(2)}) collective-permute-start(bf16[64,512]{1,0:T(8,128)(2,1)} %cot_0), channel_id=1, source_target_pairs={{0,3},{1,0},{2,1},{3,2},{4,7},{5,4},{6,5},{7,6},{8,11},{9,8},{10,9... | collective-permute-start | bytes 196616 | tf_op jit(solution)/shard_map/ppermute | solution.py:359
  62.7 11.9 %copy-start.1 = (bf16[4,128,128]{2,1,0:T(8,128)(2,1)S(1)}, bf16[4,128,128]{2,1,0:T(8,128)(2,1)}, u32[]{:S(2)}) copy-start(bf16[4,128,128]{2,1,0:T(8,128)(2,1)} %local.1) | copy-start | bytes 393220
  62.7 11.9 %copy-start.3 = (bf16[256,256]{1,0:T(8,128)(2,1)S(1)}, bf16[256,256]{1,0:T(8,128)(2,1)}, u32[]{:S(2)}) copy-start(bf16[256,256]{1,0:T(8,128)(2,1)} %weight.1) | copy-start | bytes 393220
  139.6 9.5 %all-to-all-start.4 = ((f32[16,8,128]{2,1,0:T(8,128)}), f32[16,8,128]{2,1,0:T(8,128)S(1)}, u32[]{:S(2)}, u32[]{:S(2)}) async-start(f32[16,8,128]{2,1,0:T(8,128)} %shard_map.127), calls=%async_computation.4 | async-start | bytes 131072 | tf_op jit(solution)/shard_map/all_to_all | solution.py:308

commit v11 on v10

--- a/solution.py
+++ b/solution.py
@@ -248,12 +248,17 @@
         tile = weight_grad[i * 8 : (i + 1) * 8, j * 128 : (j + 1) * 128]
         back[n, FAR * HALF :, :] = jnp.concatenate([hub[m * 8 : (m + 1) * 8], tile], axis=0).astype(BF)
 
-    for s in range(FAR):
-        for n in range(NEAR):
-            q = s * NEAR + ORDER[n]
-            tile = dot(pick[target[q]], remote[q], NT)
-            tile = jnp.concatenate([tile[:HALF], tile[HALF:]], axis=1)
-            back[n, s * HALF : (s + 1) * HALF, :] = tile.astype(BF)
+    def step(i, carry):
+        for s in (4 * i + k for k in range(4)):
+            start = pl.multiple_of(s * HALF, HALF)
+            for n in range(NEAR):
+                q = s * NEAR + ORDER[n]
+                tile = dot(pick[target[q]], remote[q], NT)
+                tile = jnp.concatenate([tile[:HALF], tile[HALF:]], axis=1)
+                back[n, pl.ds(start, HALF), :] = tile.astype(BF)
+        return carry
+
+    lax.fori_loop(0, FAR // 4, step, 0)
 
 
 def gather_body(place, piece, came, out, total):

time: 150 us -> 151 us (level)
  no operation moved by 1% of the time
where the time goes in v11:
time: 151 us; the launch traced here: 150 us
  blocking collectives  102 us (68%)
  starting transfers between devices  25.1 us (17%)
  Pallas kernels  13.1 us (9%)
  waiting for transfers between devices  5.89 us (4%)
  local copies, waits for them, and re-layouts  2.57 us (2%)
    all_to_all x3, blocking collectives, exchange(): lax.all_to_all(values, axis, split_axis=0, concat_axis=0, tiled=True, axi...  68.9 us
    all_gather x1, blocking collectives, shards(): gathered = lax.all_gather(packed, 'row', axis=0, axis_index_groups=FAR_IDS)  33.2 us
    all_to_all x2, starting transfers between devices, exchange(): lax.all_to_all(values, axis, split_axis=0, concat_axis=0, tiled=True, axi...  14.2 us
    ppermute x3, starting transfers between devices, shards(): cots.append(lax.ppermute(cotangent, 'col', turn))  10.9 us
    all_to_all x2, waiting for transfers between devices, exchange(): lax.all_to_all(values, axis, split_axis=0, concat_axis=0, tiled=True, axi...  5.89 us
    pallas_call x1, Pallas kernels, shards(): call(middle_body, [smem(), smem()] + [vmem()] * 6, [((FEAT, ROWS), BF, vm...  4.31 us
  transfers between devices with their start and end apart: 5, of which 2 were waited for; matrix products, arithmetic and copies ran while one was open for 1% of the time, Pallas kernels for 1%

profile of v11, /device:TPU:1, one launch (start us, length us, event | category | flops | bytes accessed | tf_op | source)
XLA Modules:
  0.0 150.2 jit_solution(13925666280041522306)
XLA Ops:
  0.6 1.1 shard_map.121
  1.7 33.2 %all-gather = bf16[2176,128]{1,0:T(8,128)(2,1)S(1)} all-gather(bf16[272,128]{1,0:T(8,128)(2,1)S(1)} %shard_map.121), channel_id=2, replica_groups={{0,64,128,192,256,320,384,448},{4,68,132,196,260,324,388,452},{8,72,136..., dimensions={0}, use_global_device_ids=true | all-gather | bytes 626688 | tf_op jit(solution)/shard_map/all_gather | solution.py:348
  34.9 0.1 dynamic-slice_convert_fusion
  35.0 0.0 copy-start.4
  35.0 1.8 %shard_map.122 = bf16[16,272,128]{2,1,0:T(8,128)(2,1)} custom-call(s32[8,16]{1,0:T(8,128)S(1)} %bitcast.22, bf16[8,272,128]{2,1,0:T(8,128)(2,1)S(1)} %bitcast.20), custom_call_target="tpu_custom_call" | custom-call | flops 1000000 | bytes 1000000 | tf_op jit(solution)/shard_map/pallas_call | solution.py:353
  36.7 0.0 copy-start.5
  36.8 0.0 copy-start
  36.8 10.4 %all-to-all-start = ((bf16[16,272,128]{2,1,0:T(8,128)(2,1)}), bf16[16,272,128]{2,1,0:T(8,128)(2,1)S(1)}, u32[]{:S(2)}, u32[]{:S(2)}) async-start(bf16[16,272,128]{2,1,0:T(8,128)(2,1)} %shard_map.122), calls=%async_computation | async-start | bytes 2228224 | tf_op jit(solution)/shard_map/all_to_all | solution.py:313
  47.2 0.0 copy-start.2
  47.2 3.3 %collective-permute-start = (bf16[64,512]{1,0:T(8,128)(2,1)}, bf16[64,512]{1,0:T(8,128)(2,1)}, u32[]{:S(2)}, u32[]{:S(2)}) collective-permute-start(bf16[64,512]{1,0:T(8,128)(2,1)} %cot_0), channel_id=1, source_target_pairs={{0,1},{1,2},{2,3},{3,0},{4,5},{5,6},{6,7},{7,4},{8,9},{9,10},{10,1... | collective-permute-start | bytes 196616 | tf_op jit(solution)/shard_map/ppermute | solution.py:364
  50.6 4.5 %collective-permute-start.1 = (bf16[64,512]{1,0:T(8,128)(2,1)}, bf16[64,512]{1,0:T(8,128)(2,1)}, u32[]{:S(2)}, u32[]{:S(2)}) collective-permute-start(bf16[64,512]{1,0:T(8,128)(2,1)} %cot_0), channel_id=1, source_target_pairs={{0,2},{1,3},{2,0},{3,1},{4,6},{5,7},{6,4},{7,5},{8,10},{9,11},{10,... | collective-permute-start | bytes 196616 | tf_op jit(solution)/shard_map/ppermute | solution.py:364
  55.1 3.0 %collective-permute-start.2 = (bf16[64,512]{1,0:T(8,128)(2,1)}, bf16[64,512]{1,0:T(8,128)(2,1)}, u32[]{:S(2)}, u32[]{:S(2)}) collective-permute-start(bf16[64,512]{1,0:T(8,128)(2,1)} %cot_0), channel_id=1, source_target_pairs={{0,3},{1,0},{2,1},{3,2},{4,7},{5,4},{6,5},{7,6},{8,11},{9,8},{10,9... | collective-permute-start | bytes 196616 | tf_op jit(solution)/shard_map/ppermute | solution.py:364
  58.8 0.0 copy-done.5
  58.8 0.0 copy-done.4
  58.8 0.8 reshape.32
  59.6 1.1 copy.13
  60.7 0.0 collective-permute-done.cot_1
  60.8 0.0 collective-permute-done.1.cot_2
  60.8 0.0 collective-permute-done.2.cot_3
  60.8 1.9 %all-to-all-done.came = bf16[16,272,128]{2,1,0:T(8,128)(2,1)S(1)} async-done(((bf16[16,272,128]{2,1,0:T(8,128)(2,1)}), bf16[16,272,128]{2,1,0:T(8,128)(2,1)S(1)}, u32[]{:S(2)}, u32[]{:S(2)}) %all-to-all-start) | async-done | bytes 1114144 | tf_op jit(solution)/shard_map/all_to_all | solution.py:313
  62.7 0.0 copy-done
  62.7 0.0 copy-done.2
  62.7 0.0 copy-start.1
  62.7 0.0 copy-start.3
  62.7 2.3 %shard_map.123 = (bf16[4,64,512]{2,1,0:T(8,128)(2,1)S(1)}, bf16[256,512]{1,0:T(8,128)(2,1)S(1)}) custom-call(s32[1]{0:T(128)} %bitcast.2.col, s32[128]{0:T(128)S(1)} %compare_select_fusion.target, bf16[16,272,128]{2,1,0:T(8,128)(2,1)S(1)} %all-to-all-done.came, bf16[128,64,128]{2,1,0:T(8,128)(2,1)S(1)} %copy-done, bf16[64,512]{1,0:T(8,128)(2,1)S(1)} %copy-done.2, ...), custom_call_target="tpu_custom_call" | custom-call | flops 1000000 | bytes 1000000 | tf_op jit(solution)/shard_map/pallas_call | solution.py:367
  65.0 9.5 %all_to_all.25 = bf16[4,64,512]{2,1,0:T(8,128)(2,1)S(1)} all-to-all(bf16[4,64,512]{2,1,0:T(8,128)(2,1)S(1)} %get-tuple-element.25), channel_id=1, replica_groups=mesh['row'=128,'col'=4] {'col'}, dimensions={0} | all-to-all | bytes 524288 | tf_op jit(solution)/shard_map/all_to_all | solution.py:313
  74.5 0.0 copy-done.1
  74.5 0.0 copy-done.3
  74.5 4.3 %shard_map.124 = (bf16[64,512]{1,0:T(8,128)(2,1)}, bf16[16,272,128]{2,1,0:T(8,128)(2,1)S(1)}, f32[64,512]{1,0:T(8,128)S(1)}) custom-call(s32[1]{0:T(128)} %bitcast.2.col, s32[128]{0:T(128)S(1)} %compare_select_fusion.target, bf16[256,512]{1,0:T(8,128)(2,1)S(1)} %bitcast.21, bf16[128,64,128]{2,1,0:T(8,128)(2,1)S(1)} %copy-done, ...), custom_call_target="tpu_custom_call" | custom-call | flops 1000000 | bytes 1000000 | tf_op jit(solution)/shard_map/pallas_call | solution.py:378
  78.8 22.6 %all_to_all.26.came = bf16[16,272,128]{2,1,0:T(8,128)(2,1)S(1)} all-to-all(bf16[16,272,128]{2,1,0:T(8,128)(2,1)S(1)} %get-tuple-element.29), channel_id=1, replica_groups={{4,20,16,8,32,52,56,36,0,60,44,12,24,28,40,48},{68,84,80,72,96,116,120,..., dimensions={0} | all-to-all | bytes 2228224 | tf_op jit(solution)/shard_map/all_to_all | solution.py:313
  101.4 1.3 shard_map.125
  102.7 36.8 %all_to_all.27.came = bf16[8,272,128]{2,1,0:T(8,128)(2,1)S(1)} all-to-all(bf16[8,272,128]{2,1,0:T(8,128)(2,1)S(1)} %shard_map.125), channel_id=1, replica_groups={{384,128,448,0,320,192,64,256},{388,68,196,4,324,260,132,452},{392,136,..., dimensions={0} | all-to-all | bytes 1114112 | tf_op jit(solution)/shard_map/all_to_all | solution.py:313
  139.5 0.6 shard_map.127
  140.1 3.8 %all-to-all-start.4 = ((f32[16,8,128]{2,1,0:T(8,128)}), f32[16,8,128]{2,1,0:T(8,128)S(1)}, u32[]{:S(2)}, u32[]{:S(2)}) async-start(f32[16,8,128]{2,1,0:T(8,128)} %shard_map.127), calls=%async_computation.4 | async-start | bytes 131072 | tf_op jit(solution)/shard_map/all_to_all | solution.py:313
  143.9 1.7 %shard_map.126 = bf16[64,512]{1,0:T(8,128)(2,1)} custom-call(s32[1,2]{1,0:T(1,128)} %hubs.3, bf16[8,272,128]{2,1,0:T(8,128)(2,1)S(1)} %all_to_all.27.came, f32[64,512]{1,0:T(8,128)S(1)} %get-tuple-element.30.own_grad), custom_call_target="tpu_custom_call" | custom-call | flops 1000000 | bytes 1000000 | tf_op jit(solution)/shard_map/pallas_call | solution.py:395
  145.6 4.0 %all-to-all-done.4 = f32[16,8,128]{2,1,0:T(8,128)S(1)} async-done(((f32[16,8,128]{2,1,0:T(8,128)}), f32[16,8,128]{2,1,0:T(8,128)S(1)}, u32[]{:S(2)}, u32[]{:S(2)}) %all-to-all-start.4) | async-done | bytes 65568 | tf_op jit(solution)/shard_map/all_to_all | solution.py:313
  149.6 0.6 copy.16
  (2 shorter events, 0.0 us)
Async XLA Ops:
  35.0 23.8 %copy-start.4 = (bf16[256,512]{1,0:T(8,128)(2,1)S(1)}, bf16[256,512]{1,0:T(8,128)(2,1)}, u32[]{:S(2)}) copy-start(bf16[256,512]{1,0:T(8,128)(2,1)} %param.17) | copy-start | bytes 786436
  36.7 22.0 %copy-start.5 = (s32[1,128]{1,0:T(1,128)S(1)}, s32[1,128]{1,0:T(1,128)}, u32[]{:S(2)}) copy-start(s32[1,128]{1,0:T(1,128)} %param.12) | copy-start | bytes 1540
  36.8 25.9 %copy-start = (bf16[128,64,128]{2,1,0:T(8,128)(2,1)S(1)}, bf16[128,64,128]{2,1,0:T(8,128)(2,1)}, u32[]{:S(2)}) copy-start(bf16[128,64,128]{2,1,0:T(8,128)(2,1)} %remote.3) | copy-start | bytes 6291460
  36.8 25.9 %all-to-all-start = ((bf16[16,272,128]{2,1,0:T(8,128)(2,1)}), bf16[16,272,128]{2,1,0:T(8,128)(2,1)S(1)}, u32[]{:S(2)}, u32[]{:S(2)}) async-start(bf16[16,272,128]{2,1,0:T(8,128)(2,1)} %shard_map.122), calls=%async_computation | async-start | bytes 2228224 | tf_op jit(solution)/shard_map/all_to_all | solution.py:313
  47.2 15.4 %copy-start.2 = (bf16[64,512]{1,0:T(8,128)(2,1)S(1)}, bf16[64,512]{1,0:T(8,128)(2,1)}, u32[]{:S(2)}) copy-start(bf16[64,512]{1,0:T(8,128)(2,1)} %feats.3) | copy-start | bytes 196612
  47.2 13.5 %collective-permute-start = (bf16[64,512]{1,0:T(8,128)(2,1)}, bf16[64,512]{1,0:T(8,128)(2,1)}, u32[]{:S(2)}, u32[]{:S(2)}) collective-permute-start(bf16[64,512]{1,0:T(8,128)(2,1)} %cot_0), channel_id=1, source_target_pairs={{0,1},{1,2},{2,3},{3,0},{4,5},{5,6},{6,7},{7,4},{8,9},{9,10},{10,1... | collective-permute-start | bytes 196616 | tf_op jit(solution)/shard_map/ppermute | solution.py:364
  50.6 10.2 %collective-permute-start.1 = (bf16[64,512]{1,0:T(8,128)(2,1)}, bf16[64,512]{1,0:T(8,128)(2,1)}, u32[]{:S(2)}, u32[]{:S(2)}) collective-permute-start(bf16[64,512]{1,0:T(8,128)(2,1)} %cot_0), channel_id=1, source_target_pairs={{0,2},{1,3},{2,0},{3,1},{4,6},{5,7},{6,4},{7,5},{8,10},{9,11},{10,... | collective-permute-start | bytes 196616 | tf_op jit(solution)/shard_map/ppermute | solution.py:364
  55.1 5.7 %collective-permute-start.2 = (bf16[64,512]{1,0:T(8,128)(2,1)}, bf16[64,512]{1,0:T(8,128)(2,1)}, u32[]{:S(2)}, u32[]{:S(2)}) collective-permute-start(bf16[64,512]{1,0:T(8,128)(2,1)} %cot_0), channel_id=1, source_target_pairs={{0,3},{1,0},{2,1},{3,2},{4,7},{5,4},{6,5},{7,6},{8,11},{9,8},{10,9... | collective-permute-start | bytes 196616 | tf_op jit(solution)/shard_map/ppermute | solution.py:364
  62.7 11.9 %copy-start.1 = (bf16[4,128,128]{2,1,0:T(8,128)(2,1)S(1)}, bf16[4,128,128]{2,1,0:T(8,128)(2,1)}, u32[]{:S(2)}) copy-start(bf16[4,128,128]{2,1,0:T(8,128)(2,1)} %local.1) | copy-start | bytes 393220
  62.7 11.9 %copy-start.3 = (bf16[256,256]{1,0:T(8,128)(2,1)S(1)}, bf16[256,256]{1,0:T(8,128)(2,1)}, u32[]{:S(2)}) copy-start(bf16[256,256]{1,0:T(8,128)(2,1)} %weight.1) | copy-start | bytes 393220
  140.1 9.5 %all-to-all-start.4 = ((f32[16,8,128]{2,1,0:T(8,128)}), f32[16,8,128]{2,1,0:T(8,128)S(1)}, u32[]{:S(2)}, u32[]{:S(2)}) async-start(f32[16,8,128]{2,1,0:T(8,128)} %shard_map.127), calls=%async_computation.4 | async-start | bytes 131072 | tf_op jit(solution)/shard_map/all_to_all | solution.py:313

commit v12 on v10

--- a/solution.py
+++ b/solution.py
@@ -129,14 +129,27 @@
         tail = gathered[s, DENSE:, :].astype(F32)
         extra = jnp.where(place == s, jnp.broadcast_to(tail[1:2], (16, 128)), extra)
     extra = extra.astype(BF)
-    copies = []
     for n in range(NEAR):
-        for s in range(FAR):
-            start = pl.multiple_of(piece[s, ORDER[n]] * HALF, HALF)
-            held[n, s * HALF : (s + 1) * HALF, :] = gathered[s, pl.ds(start, HALF), :]
         held[n, FAR * HALF :, :] = extra
-        copies.append(pltpu.make_async_copy(held.at[n], out.at[n], sems.at[n]))
-        copies[-1].start()
+    ends = slice(FAR * HALF, NEAR_ROWS)
+    copies = [pltpu.make_async_copy(held.at[:, ends, :], out.at[:, ends, :], sems.at[2])]
+    copies[0].start()
+    rows = FAR * HALF // 2
+    halves = [slice(i * rows, (i + 1) * rows) for i in range(2)]
+    for i, half in enumerate(halves):
+        copies.append(pltpu.make_async_copy(held.at[:, half, :], out.at[:, half, :], sems.at[i]))
+
+    def step(i, carry):
+        for s in (4 * i + k for k in range(4)):
+            to = pl.multiple_of(s * HALF, HALF)
+            for n in range(NEAR):
+                start = pl.multiple_of(piece[s, ORDER[n]] * HALF, HALF)
+                held[n, pl.ds(to, HALF), :] = gathered[s, pl.ds(start, HALF), :]
+        half = pl.ds(pl.multiple_of(i * rows, rows), rows)
+        pltpu.make_async_copy(held.at[:, half, :], out.at[:, half, :], sems.at[i]).start()
+        return carry
+
+    lax.fori_loop(0, 2, step, 0)
     for copy in copies:
         copy.wait()
 
@@ -349,7 +362,7 @@
         pick_body,
         [smem(), vmem()],
         [(near_all, BF, away())],
-        [pltpu.VMEM(near_all, BF), pltpu.SemaphoreType.DMA((NEAR,))],
+        [pltpu.VMEM(near_all, BF), pltpu.SemaphoreType.DMA((3,))],
     )(piece, gathered)
     picked, cotangent = lax.optimization_barrier((picked, cotangent))
     came = exchange(picked, "row", NEAR_GROUPS)

time: 150 us -> 150 us (level)
  no operation moved by 1% of the time
where the time goes in v12:
time: 150 us
  blocking collectives  102 us (68%)
  starting transfers between devices  25 us (17%)
  Pallas kernels  12.6 us (8%)
  waiting for transfers between devices  5.89 us (4%)
  local copies, waits for them, and re-layouts  2.57 us (2%)
    all_to_all x3, blocking collectives, exchange(): lax.all_to_all(values, axis, split_axis=0, concat_axis=0, tiled=True, axi...  68.9 us
    all_gather x1, blocking collectives, shards(): gathered = lax.all_gather(packed, 'row', axis=0, axis_index_groups=FAR_IDS)  33.2 us
    all_to_all x2, starting transfers between devices, exchange(): lax.all_to_all(values, axis, split_axis=0, concat_axis=0, tiled=True, axi...  14.2 us
    ppermute x3, starting transfers between devices, shards(): cots.append(lax.ppermute(cotangent, 'col', turn))  10.9 us
    all_to_all x2, waiting for transfers between devices, exchange(): lax.all_to_all(values, axis, split_axis=0, concat_axis=0, tiled=True, axi...  5.89 us
    pallas_call x1, Pallas kernels, shards(): call(middle_body, [smem(), smem()] + [vmem()] * 6, [((FEAT, ROWS), BF, vm...  3.81 us
  transfers between devices with their start and end apart: 5, of which 2 were waited for; matrix products, arithmetic and copies ran while one was open for 1% of the time, Pallas kernels for 1%

profile of v12, /device:TPU:1, one launch (start us, length us, event | category | flops | bytes accessed | tf_op | source)
XLA Modules:
  0.0 149.8 jit_solution(8952479736244454106)
XLA Ops:
  0.6 1.1 shard_map.121
  1.7 33.2 %all-gather = bf16[2176,128]{1,0:T(8,128)(2,1)S(1)} all-gather(bf16[272,128]{1,0:T(8,128)(2,1)S(1)} %shard_map.121), channel_id=2, replica_groups={{0,64,128,192,256,320,384,448},{4,68,132,196,260,324,388,452},{8,72,136..., dimensions={0}, use_global_device_ids=true | all-gather | bytes 626688 | tf_op jit(solution)/shard_map/all_gather | solution.py:356
  34.9 0.1 dynamic-slice_convert_fusion
  35.0 0.0 copy-start.4
  35.0 1.8 %shard_map.122 = bf16[16,272,128]{2,1,0:T(8,128)(2,1)} custom-call(s32[8,16]{1,0:T(8,128)S(1)} %bitcast.22, bf16[8,272,128]{2,1,0:T(8,128)(2,1)S(1)} %bitcast.20), custom_call_target="tpu_custom_call" | custom-call | flops 1000000 | bytes 1000000 | tf_op jit(solution)/shard_map/pallas_call | solution.py:361
  36.8 0.0 copy-start.5
  36.8 0.0 copy-start
  36.8 10.4 %all-to-all-start = ((bf16[16,272,128]{2,1,0:T(8,128)(2,1)}), bf16[16,272,128]{2,1,0:T(8,128)(2,1)S(1)}, u32[]{:S(2)}, u32[]{:S(2)}) async-start(bf16[16,272,128]{2,1,0:T(8,128)(2,1)} %shard_map.122), calls=%async_computation | async-start | bytes 2228224 | tf_op jit(solution)/shard_map/all_to_all | solution.py:321
  47.3 0.0 copy-start.2
  47.3 3.3 %collective-permute-start = (bf16[64,512]{1,0:T(8,128)(2,1)}, bf16[64,512]{1,0:T(8,128)(2,1)}, u32[]{:S(2)}, u32[]{:S(2)}) collective-permute-start(bf16[64,512]{1,0:T(8,128)(2,1)} %cot_0), channel_id=1, source_target_pairs={{0,1},{1,2},{2,3},{3,0},{4,5},{5,6},{6,7},{7,4},{8,9},{9,10},{10,1... | collective-permute-start | bytes 196616 | tf_op jit(solution)/shard_map/ppermute | solution.py:372
  50.7 4.5 %collective-permute-start.1 = (bf16[64,512]{1,0:T(8,128)(2,1)}, bf16[64,512]{1,0:T(8,128)(2,1)}, u32[]{:S(2)}, u32[]{:S(2)}) collective-permute-start(bf16[64,512]{1,0:T(8,128)(2,1)} %cot_0), channel_id=1, source_target_pairs={{0,2},{1,3},{2,0},{3,1},{4,6},{5,7},{6,4},{7,5},{8,10},{9,11},{10,... | collective-permute-start | bytes 196616 | tf_op jit(solution)/shard_map/ppermute | solution.py:372
  55.2 3.0 %collective-permute-start.2 = (bf16[64,512]{1,0:T(8,128)(2,1)}, bf16[64,512]{1,0:T(8,128)(2,1)}, u32[]{:S(2)}, u32[]{:S(2)}) collective-permute-start(bf16[64,512]{1,0:T(8,128)(2,1)} %cot_0), channel_id=1, source_target_pairs={{0,3},{1,0},{2,1},{3,2},{4,7},{5,4},{6,5},{7,6},{8,11},{9,8},{10,9... | collective-permute-start | bytes 196616 | tf_op jit(solution)/shard_map/ppermute | solution.py:372
  58.8 0.0 copy-done.5
  58.9 0.0 copy-done.4
  58.9 0.8 reshape.32
  59.7 1.1 copy.13
  60.8 0.0 collective-permute-done.cot_1
  60.8 0.0 collective-permute-done.1.cot_2
  60.8 0.0 collective-permute-done.2.cot_3
  60.9 1.9 %all-to-all-done.came = bf16[16,272,128]{2,1,0:T(8,128)(2,1)S(1)} async-done(((bf16[16,272,128]{2,1,0:T(8,128)(2,1)}), bf16[16,272,128]{2,1,0:T(8,128)(2,1)S(1)}, u32[]{:S(2)}, u32[]{:S(2)}) %all-to-all-start) | async-done | bytes 1114144 | tf_op jit(solution)/shard_map/all_to_all | solution.py:321
  62.7 0.0 copy-done
  62.7 0.0 copy-done.2
  62.7 0.0 copy-start.1
  62.7 0.0 copy-start.3
  62.7 2.3 %shard_map.123 = (bf16[4,64,512]{2,1,0:T(8,128)(2,1)S(1)}, bf16[256,512]{1,0:T(8,128)(2,1)S(1)}) custom-call(s32[1]{0:T(128)} %bitcast.2.col, s32[128]{0:T(128)S(1)} %compare_select_fusion.target, bf16[16,272,128]{2,1,0:T(8,128)(2,1)S(1)} %all-to-all-done.came, bf16[128,64,128]{2,1,0:T(8,128)(2,1)S(1)} %copy-done, bf16[64,512]{1,0:T(8,128)(2,1)S(1)} %copy-done.2, ...), custom_call_target="tpu_custom_call" | custom-call | flops 1000000 | bytes 1000000 | tf_op jit(solution)/shard_map/pallas_call | solution.py:375
  65.1 9.5 %all_to_all.25 = bf16[4,64,512]{2,1,0:T(8,128)(2,1)S(1)} all-to-all(bf16[4,64,512]{2,1,0:T(8,128)(2,1)S(1)} %get-tuple-element.25), channel_id=1, replica_groups=mesh['row'=128,'col'=4] {'col'}, dimensions={0} | all-to-all | bytes 524288 | tf_op jit(solution)/shard_map/all_to_all | solution.py:321
  74.6 0.0 copy-done.1
  74.6 0.0 copy-done.3
  74.6 3.8 %shard_map.124 = (bf16[64,512]{1,0:T(8,128)(2,1)}, bf16[16,272,128]{2,1,0:T(8,128)(2,1)S(1)}, f32[64,512]{1,0:T(8,128)S(1)}) custom-call(s32[1]{0:T(128)} %bitcast.2.col, s32[128]{0:T(128)S(1)} %compare_select_fusion.target, bf16[256,512]{1,0:T(8,128)(2,1)S(1)} %bitcast.21, bf16[128,64,128]{2,1,0:T(8,128)(2,1)S(1)} %copy-done, ...), custom_call_target="tpu_custom_call" | custom-call | flops 1000000 | bytes 1000000 | tf_op jit(solution)/shard_map/pallas_call | solution.py:386
  78.4 22.6 %all_to_all.26.came = bf16[16,272,128]{2,1,0:T(8,128)(2,1)S(1)} all-to-all(bf16[16,272,128]{2,1,0:T(8,128)(2,1)S(1)} %get-tuple-element.29), channel_id=1, replica_groups={{4,20,16,8,32,52,56,36,0,60,44,12,24,28,40,48},{68,84,80,72,96,116,120,..., dimensions={0} | all-to-all | bytes 2228224 | tf_op jit(solution)/shard_map/all_to_all | solution.py:321
  101.0 1.3 shard_map.125
  102.2 36.8 %all_to_all.27.came = bf16[8,272,128]{2,1,0:T(8,128)(2,1)S(1)} all-to-all(bf16[8,272,128]{2,1,0:T(8,128)(2,1)S(1)} %shard_map.125), channel_id=1, replica_groups={{384,128,448,0,320,192,64,256},{388,68,196,4,324,260,132,452},{392,136,..., dimensions={0} | all-to-all | bytes 1114112 | tf_op jit(solution)/shard_map/all_to_all | solution.py:321
  139.1 0.6 shard_map.127
  139.7 3.7 %all-to-all-start.4 = ((f32[16,8,128]{2,1,0:T(8,128)}), f32[16,8,128]{2,1,0:T(8,128)S(1)}, u32[]{:S(2)}, u32[]{:S(2)}) async-start(f32[16,8,128]{2,1,0:T(8,128)} %shard_map.127), calls=%async_computation.4 | async-start | bytes 131072 | tf_op jit(solution)/shard_map/all_to_all | solution.py:321
  143.5 1.7 %shard_map.126 = bf16[64,512]{1,0:T(8,128)(2,1)} custom-call(s32[1,2]{1,0:T(1,128)} %hubs.3, bf16[8,272,128]{2,1,0:T(8,128)(2,1)S(1)} %all_to_all.27.came, f32[64,512]{1,0:T(8,128)S(1)} %get-tuple-element.30.own_grad), custom_call_target="tpu_custom_call" | custom-call | flops 1000000 | bytes 1000000 | tf_op jit(solution)/shard_map/pallas_call | solution.py:403
  145.1 4.0 %all-to-all-done.4 = f32[16,8,128]{2,1,0:T(8,128)S(1)} async-done(((f32[16,8,128]{2,1,0:T(8,128)}), f32[16,8,128]{2,1,0:T(8,128)S(1)}, u32[]{:S(2)}, u32[]{:S(2)}) %all-to-all-start.4) | async-done | bytes 65568 | tf_op jit(solution)/shard_map/all_to_all | solution.py:321
  149.2 0.6 copy.16
  (2 shorter events, 0.0 us)
Async XLA Ops:
  35.0 23.9 %copy-start.4 = (bf16[256,512]{1,0:T(8,128)(2,1)S(1)}, bf16[256,512]{1,0:T(8,128)(2,1)}, u32[]{:S(2)}) copy-start(bf16[256,512]{1,0:T(8,128)(2,1)} %param.17) | copy-start | bytes 786436
  36.8 22.0 %copy-start.5 = (s32[1,128]{1,0:T(1,128)S(1)}, s32[1,128]{1,0:T(1,128)}, u32[]{:S(2)}) copy-start(s32[1,128]{1,0:T(1,128)} %param.12) | copy-start | bytes 1540
  36.8 25.9 %copy-start = (bf16[128,64,128]{2,1,0:T(8,128)(2,1)S(1)}, bf16[128,64,128]{2,1,0:T(8,128)(2,1)}, u32[]{:S(2)}) copy-start(bf16[128,64,128]{2,1,0:T(8,128)(2,1)} %remote.3) | copy-start | bytes 6291460
  36.8 25.9 %all-to-all-start = ((bf16[16,272,128]{2,1,0:T(8,128)(2,1)}), bf16[16,272,128]{2,1,0:T(8,128)(2,1)S(1)}, u32[]{:S(2)}, u32[]{:S(2)}) async-start(bf16[16,272,128]{2,1,0:T(8,128)(2,1)} %shard_map.122), calls=%async_computation | async-start | bytes 2228224 | tf_op jit(solution)/shard_map/all_to_all | solution.py:321
  47.3 15.4 %copy-start.2 = (bf16[64,512]{1,0:T(8,128)(2,1)S(1)}, bf16[64,512]{1,0:T(8,128)(2,1)}, u32[]{:S(2)}) copy-start(bf16[64,512]{1,0:T(8,128)(2,1)} %feats.3) | copy-start | bytes 196612
  47.3 13.5 %collective-permute-start = (bf16[64,512]{1,0:T(8,128)(2,1)}, bf16[64,512]{1,0:T(8,128)(2,1)}, u32[]{:S(2)}, u32[]{:S(2)}) collective-permute-start(bf16[64,512]{1,0:T(8,128)(2,1)} %cot_0), channel_id=1, source_target_pairs={{0,1},{1,2},{2,3},{3,0},{4,5},{5,6},{6,7},{7,4},{8,9},{9,10},{10,1... | collective-permute-start | bytes 196616 | tf_op jit(solution)/shard_map/ppermute | solution.py:372
  50.7 10.2 %collective-permute-start.1 = (bf16[64,512]{1,0:T(8,128)(2,1)}, bf16[64,512]{1,0:T(8,128)(2,1)}, u32[]{:S(2)}, u32[]{:S(2)}) collective-permute-start(bf16[64,512]{1,0:T(8,128)(2,1)} %cot_0), channel_id=1, source_target_pairs={{0,2},{1,3},{2,0},{3,1},{4,6},{5,7},{6,4},{7,5},{8,10},{9,11},{10,... | collective-permute-start | bytes 196616 | tf_op jit(solution)/shard_map/ppermute | solution.py:372
  55.2 5.7 %collective-permute-start.2 = (bf16[64,512]{1,0:T(8,128)(2,1)}, bf16[64,512]{1,0:T(8,128)(2,1)}, u32[]{:S(2)}, u32[]{:S(2)}) collective-permute-start(bf16[64,512]{1,0:T(8,128)(2,1)} %cot_0), channel_id=1, source_target_pairs={{0,3},{1,0},{2,1},{3,2},{4,7},{5,4},{6,5},{7,6},{8,11},{9,8},{10,9... | collective-permute-start | bytes 196616 | tf_op jit(solution)/shard_map/ppermute | solution.py:372
  62.7 11.9 %copy-start.1 = (bf16[4,128,128]{2,1,0:T(8,128)(2,1)S(1)}, bf16[4,128,128]{2,1,0:T(8,128)(2,1)}, u32[]{:S(2)}) copy-start(bf16[4,128,128]{2,1,0:T(8,128)(2,1)} %local.1) | copy-start | bytes 393220
  62.7 11.9 %copy-start.3 = (bf16[256,256]{1,0:T(8,128)(2,1)S(1)}, bf16[256,256]{1,0:T(8,128)(2,1)}, u32[]{:S(2)}) copy-start(bf16[256,256]{1,0:T(8,128)(2,1)} %weight.1) | copy-start | bytes 393220
  139.7 9.5 %all-to-all-start.4 = ((f32[16,8,128]{2,1,0:T(8,128)}), f32[16,8,128]{2,1,0:T(8,128)S(1)}, u32[]{:S(2)}, u32[]{:S(2)}) async-start(f32[16,8,128]{2,1,0:T(8,128)} %shard_map.127), calls=%async_computation.4 | async-start | bytes 131072 | tf_op jit(solution)/shard_map/all_to_all | solution.py:321

commit v13 on v12

--- a/solution.py
+++ b/solution.py
@@ -279,11 +279,17 @@
         hub = jnp.broadcast_to(extra[s : s + 1], (8, 128))
         out[slot[s], DENSE:, :] = jnp.concatenate([hub, extra[8:]], axis=0).astype(BF)
 
-    for s in range(FAR):
-        for n in range(NEAR):
-            at = pl.multiple_of(piece[s, ORDER[n]] * HALF, HALF)
-            total[s, pl.ds(at, HALF), :] += came[n, s * HALF : (s + 1) * HALF, :].astype(F32)
-        out[slot[s], :DENSE, :] = total[s].astype(BF)
+    def step(i, carry):
+        for k in range(4):
+            s = 4 * i + k
+            start = pl.multiple_of(s * HALF, HALF)
+            for n in range(NEAR):
+                at = pl.multiple_of(piece[s, ORDER[n]] * HALF, HALF)
+                total[s, pl.ds(at, HALF), :] += came[n, pl.ds(start, HALF), :].astype(F32)
+            out[jnp.where(i == 0, slot[k], slot[4 + k]), :DENSE, :] = total[s].astype(BF)
+        return carry
+
+    lax.fori_loop(0, FAR // 4, step, 0)
 
 
 def chunk_body(came, chunk):

time: 150 us -> 150 us (level)
  no operation moved by 1% of the time
where the time goes in v13:
time: 150 us
  blocking collectives  102 us (68%)
  starting transfers between devices  25.1 us (17%)
  Pallas kernels  12.7 us (8%)
  waiting for transfers between devices  5.89 us (4%)
  local copies, waits for them, and re-layouts  2.57 us (2%)
    all_to_all x3, blocking collectives, exchange(): lax.all_to_all(values, axis, split_axis=0, concat_axis=0, tiled=True, axi...  68.9 us
    all_gather x1, blocking collectives, shards(): gathered = lax.all_gather(packed, 'row', axis=0, axis_index_groups=FAR_IDS)  33.2 us
    all_to_all x2, starting transfers between devices, exchange(): lax.all_to_all(values, axis, split_axis=0, concat_axis=0, tiled=True, axi...  14.2 us
    ppermute x3, starting transfers between devices, shards(): cots.append(lax.ppermute(cotangent, 'col', turn))  10.9 us
    all_to_all x2, waiting for transfers between devices, exchange(): lax.all_to_all(values, axis, split_axis=0, concat_axis=0, tiled=True, axi...  5.89 us
    pallas_call x1, Pallas kernels, shards(): call(middle_body, [smem(), smem()] + [vmem()] * 6, [((FEAT, ROWS), BF, vm...  3.8 us
  transfers between devices with their start and end apart: 5, of which 2 were waited for; matrix products, arithmetic and copies ran while one was open for 1% of the time, Pallas kernels for 1%

profile of v13, /device:TPU:1, one launch (start us, length us, event | category | flops | bytes accessed | tf_op | source)
XLA Modules:
  0.0 149.9 jit_solution(12531379004849705274)
XLA Ops:
  0.6 1.1 shard_map.121
  1.7 33.2 %all-gather = bf16[2176,128]{1,0:T(8,128)(2,1)S(1)} all-gather(bf16[272,128]{1,0:T(8,128)(2,1)S(1)} %shard_map.121), channel_id=2, replica_groups={{0,64,128,192,256,320,384,448},{4,68,132,196,260,324,388,452},{8,72,136..., dimensions={0}, use_global_device_ids=true | all-gather | bytes 626688 | tf_op jit(solution)/shard_map/all_gather | solution.py:362
  34.9 0.1 dynamic-slice_convert_fusion
  35.0 0.0 copy-start.4
  35.0 1.8 %shard_map.122 = bf16[16,272,128]{2,1,0:T(8,128)(2,1)} custom-call(s32[8,16]{1,0:T(8,128)S(1)} %bitcast.22, bf16[8,272,128]{2,1,0:T(8,128)(2,1)S(1)} %bitcast.20), custom_call_target="tpu_custom_call" | custom-call | flops 1000000 | bytes 1000000 | tf_op jit(solution)/shard_map/pallas_call | solution.py:367
  36.8 0.0 copy-start.5
  36.8 0.0 copy-start
  36.9 10.4 %all-to-all-start = ((bf16[16,272,128]{2,1,0:T(8,128)(2,1)}), bf16[16,272,128]{2,1,0:T(8,128)(2,1)S(1)}, u32[]{:S(2)}, u32[]{:S(2)}) async-start(bf16[16,272,128]{2,1,0:T(8,128)(2,1)} %shard_map.122), calls=%async_computation | async-start | bytes 2228224 | tf_op jit(solution)/shard_map/all_to_all | solution.py:327
  47.3 0.0 copy-start.2
  47.3 3.3 %collective-permute-start = (bf16[64,512]{1,0:T(8,128)(2,1)}, bf16[64,512]{1,0:T(8,128)(2,1)}, u32[]{:S(2)}, u32[]{:S(2)}) collective-permute-start(bf16[64,512]{1,0:T(8,128)(2,1)} %cot_0), channel_id=1, source_target_pairs={{0,1},{1,2},{2,3},{3,0},{4,5},{5,6},{6,7},{7,4},{8,9},{9,10},{10,1... | collective-permute-start | bytes 196616 | tf_op jit(solution)/shard_map/ppermute | solution.py:378
  50.7 4.5 %collective-permute-start.1 = (bf16[64,512]{1,0:T(8,128)(2,1)}, bf16[64,512]{1,0:T(8,128)(2,1)}, u32[]{:S(2)}, u32[]{:S(2)}) collective-permute-start(bf16[64,512]{1,0:T(8,128)(2,1)} %cot_0), channel_id=1, source_target_pairs={{0,2},{1,3},{2,0},{3,1},{4,6},{5,7},{6,4},{7,5},{8,10},{9,11},{10,... | collective-permute-start | bytes 196616 | tf_op jit(solution)/shard_map/ppermute | solution.py:378
  55.2 3.0 %collective-permute-start.2 = (bf16[64,512]{1,0:T(8,128)(2,1)}, bf16[64,512]{1,0:T(8,128)(2,1)}, u32[]{:S(2)}, u32[]{:S(2)}) collective-permute-start(bf16[64,512]{1,0:T(8,128)(2,1)} %cot_0), channel_id=1, source_target_pairs={{0,3},{1,0},{2,1},{3,2},{4,7},{5,4},{6,5},{7,6},{8,11},{9,8},{10,9... | collective-permute-start | bytes 196616 | tf_op jit(solution)/shard_map/ppermute | solution.py:378
  58.8 0.0 copy-done.5
  58.9 0.0 copy-done.4
  58.9 0.8 reshape.32
  59.7 1.1 copy.13
  60.8 0.0 collective-permute-done.cot_1
  60.8 0.0 collective-permute-done.1.cot_2
  60.8 0.0 collective-permute-done.2.cot_3
  60.9 1.9 %all-to-all-done.came = bf16[16,272,128]{2,1,0:T(8,128)(2,1)S(1)} async-done(((bf16[16,272,128]{2,1,0:T(8,128)(2,1)}), bf16[16,272,128]{2,1,0:T(8,128)(2,1)S(1)}, u32[]{:S(2)}, u32[]{:S(2)}) %all-to-all-start) | async-done | bytes 1114144 | tf_op jit(solution)/shard_map/all_to_all | solution.py:327
  62.7 0.0 copy-done
  62.7 0.0 copy-done.2
  62.7 0.0 copy-start.1
  62.7 0.0 copy-start.3
  62.7 2.3 %shard_map.123 = (bf16[4,64,512]{2,1,0:T(8,128)(2,1)S(1)}, bf16[256,512]{1,0:T(8,128)(2,1)S(1)}) custom-call(s32[1]{0:T(128)} %bitcast.2.col, s32[128]{0:T(128)S(1)} %compare_select_fusion.target, bf16[16,272,128]{2,1,0:T(8,128)(2,1)S(1)} %all-to-all-done.came, bf16[128,64,128]{2,1,0:T(8,128)(2,1)S(1)} %copy-done, bf16[64,512]{1,0:T(8,128)(2,1)S(1)} %copy-done.2, ...), custom_call_target="tpu_custom_call" | custom-call | flops 1000000 | bytes 1000000 | tf_op jit(solution)/shard_map/pallas_call | solution.py:381
  65.1 9.5 %all_to_all.25 = bf16[4,64,512]{2,1,0:T(8,128)(2,1)S(1)} all-to-all(bf16[4,64,512]{2,1,0:T(8,128)(2,1)S(1)} %get-tuple-element.25), channel_id=1, replica_groups=mesh['row'=128,'col'=4] {'col'}, dimensions={0} | all-to-all | bytes 524288 | tf_op jit(solution)/shard_map/all_to_all | solution.py:327
  74.6 0.0 copy-done.1
  74.6 0.0 copy-done.3
  74.6 3.8 %shard_map.124 = (bf16[64,512]{1,0:T(8,128)(2,1)}, bf16[16,272,128]{2,1,0:T(8,128)(2,1)S(1)}, f32[64,512]{1,0:T(8,128)S(1)}) custom-call(s32[1]{0:T(128)} %bitcast.2.col, s32[128]{0:T(128)S(1)} %compare_select_fusion.target, bf16[256,512]{1,0:T(8,128)(2,1)S(1)} %bitcast.21, bf16[128,64,128]{2,1,0:T(8,128)(2,1)S(1)} %copy-done, ...), custom_call_target="tpu_custom_call" | custom-call | flops 1000000 | bytes 1000000 | tf_op jit(solution)/shard_map/pallas_call | solution.py:392
  78.4 22.6 %all_to_all.26.came = bf16[16,272,128]{2,1,0:T(8,128)(2,1)S(1)} all-to-all(bf16[16,272,128]{2,1,0:T(8,128)(2,1)S(1)} %get-tuple-element.29), channel_id=1, replica_groups={{4,20,16,8,32,52,56,36,0,60,44,12,24,28,40,48},{68,84,80,72,96,116,120,..., dimensions={0} | all-to-all | bytes 2228224 | tf_op jit(solution)/shard_map/all_to_all | solution.py:327
  101.0 1.3 shard_map.125
  102.3 36.8 %all_to_all.27.came = bf16[8,272,128]{2,1,0:T(8,128)(2,1)S(1)} all-to-all(bf16[8,272,128]{2,1,0:T(8,128)(2,1)S(1)} %shard_map.125), channel_id=1, replica_groups={{384,128,448,0,320,192,64,256},{388,68,196,4,324,260,132,452},{392,136,..., dimensions={0} | all-to-all | bytes 1114112 | tf_op jit(solution)/shard_map/all_to_all | solution.py:327
  139.1 0.6 shard_map.127
  139.8 3.8 %all-to-all-start.4 = ((f32[16,8,128]{2,1,0:T(8,128)}), f32[16,8,128]{2,1,0:T(8,128)S(1)}, u32[]{:S(2)}, u32[]{:S(2)}) async-start(f32[16,8,128]{2,1,0:T(8,128)} %shard_map.127), calls=%async_computation.4 | async-start | bytes 131072 | tf_op jit(solution)/shard_map/all_to_all | solution.py:327
  143.5 1.7 %shard_map.126 = bf16[64,512]{1,0:T(8,128)(2,1)} custom-call(s32[1,2]{1,0:T(1,128)} %hubs.3, bf16[8,272,128]{2,1,0:T(8,128)(2,1)S(1)} %all_to_all.27.came, f32[64,512]{1,0:T(8,128)S(1)} %get-tuple-element.30.own_grad), custom_call_target="tpu_custom_call" | custom-call | flops 1000000 | bytes 1000000 | tf_op jit(solution)/shard_map/pallas_call | solution.py:409
  145.2 4.0 %all-to-all-done.4 = f32[16,8,128]{2,1,0:T(8,128)S(1)} async-done(((f32[16,8,128]{2,1,0:T(8,128)}), f32[16,8,128]{2,1,0:T(8,128)S(1)}, u32[]{:S(2)}, u32[]{:S(2)}) %all-to-all-start.4) | async-done | bytes 65568 | tf_op jit(solution)/shard_map/all_to_all | solution.py:327
  149.3 0.6 copy.16
  (2 shorter events, 0.0 us)
Async XLA Ops:
  35.0 23.9 %copy-start.4 = (bf16[256,512]{1,0:T(8,128)(2,1)S(1)}, bf16[256,512]{1,0:T(8,128)(2,1)}, u32[]{:S(2)}) copy-start(bf16[256,512]{1,0:T(8,128)(2,1)} %param.17) | copy-start | bytes 786436
  36.8 22.0 %copy-start.5 = (s32[1,128]{1,0:T(1,128)S(1)}, s32[1,128]{1,0:T(1,128)}, u32[]{:S(2)}) copy-start(s32[1,128]{1,0:T(1,128)} %param.12) | copy-start | bytes 1540
  36.8 25.9 %copy-start = (bf16[128,64,128]{2,1,0:T(8,128)(2,1)S(1)}, bf16[128,64,128]{2,1,0:T(8,128)(2,1)}, u32[]{:S(2)}) copy-start(bf16[128,64,128]{2,1,0:T(8,128)(2,1)} %remote.3) | copy-start | bytes 6291460
  36.9 25.9 %all-to-all-start = ((bf16[16,272,128]{2,1,0:T(8,128)(2,1)}), bf16[16,272,128]{2,1,0:T(8,128)(2,1)S(1)}, u32[]{:S(2)}, u32[]{:S(2)}) async-start(bf16[16,272,128]{2,1,0:T(8,128)(2,1)} %shard_map.122), calls=%async_computation | async-start | bytes 2228224 | tf_op jit(solution)/shard_map/all_to_all | solution.py:327
  47.3 15.4 %copy-start.2 = (bf16[64,512]{1,0:T(8,128)(2,1)S(1)}, bf16[64,512]{1,0:T(8,128)(2,1)}, u32[]{:S(2)}) copy-start(bf16[64,512]{1,0:T(8,128)(2,1)} %feats.3) | copy-start | bytes 196612
  47.3 13.5 %collective-permute-start = (bf16[64,512]{1,0:T(8,128)(2,1)}, bf16[64,512]{1,0:T(8,128)(2,1)}, u32[]{:S(2)}, u32[]{:S(2)}) collective-permute-start(bf16[64,512]{1,0:T(8,128)(2,1)} %cot_0), channel_id=1, source_target_pairs={{0,1},{1,2},{2,3},{3,0},{4,5},{5,6},{6,7},{7,4},{8,9},{9,10},{10,1... | collective-permute-start | bytes 196616 | tf_op jit(solution)/shard_map/ppermute | solution.py:378
  50.7 10.2 %collective-permute-start.1 = (bf16[64,512]{1,0:T(8,128)(2,1)}, bf16[64,512]{1,0:T(8,128)(2,1)}, u32[]{:S(2)}, u32[]{:S(2)}) collective-permute-start(bf16[64,512]{1,0:T(8,128)(2,1)} %cot_0), channel_id=1, source_target_pairs={{0,2},{1,3},{2,0},{3,1},{4,6},{5,7},{6,4},{7,5},{8,10},{9,11},{10,... | collective-permute-start | bytes 196616 | tf_op jit(solution)/shard_map/ppermute | solution.py:378
  55.2 5.7 %collective-permute-start.2 = (bf16[64,512]{1,0:T(8,128)(2,1)}, bf16[64,512]{1,0:T(8,128)(2,1)}, u32[]{:S(2)}, u32[]{:S(2)}) collective-permute-start(bf16[64,512]{1,0:T(8,128)(2,1)} %cot_0), channel_id=1, source_target_pairs={{0,3},{1,0},{2,1},{3,2},{4,7},{5,4},{6,5},{7,6},{8,11},{9,8},{10,9... | collective-permute-start | bytes 196616 | tf_op jit(solution)/shard_map/ppermute | solution.py:378
  62.7 11.8 %copy-start.1 = (bf16[4,128,128]{2,1,0:T(8,128)(2,1)S(1)}, bf16[4,128,128]{2,1,0:T(8,128)(2,1)}, u32[]{:S(2)}) copy-start(bf16[4,128,128]{2,1,0:T(8,128)(2,1)} %local.1) | copy-start | bytes 393220
  62.7 11.8 %copy-start.3 = (bf16[256,256]{1,0:T(8,128)(2,1)S(1)}, bf16[256,256]{1,0:T(8,128)(2,1)}, u32[]{:S(2)}) copy-start(bf16[256,256]{1,0:T(8,128)(2,1)} %weight.1) | copy-start | bytes 393220
  139.8 9.5 %all-to-all-start.4 = ((f32[16,8,128]{2,1,0:T(8,128)}), f32[16,8,128]{2,1,0:T(8,128)S(1)}, u32[]{:S(2)}, u32[]{:S(2)}) async-start(f32[16,8,128]{2,1,0:T(8,128)} %shard_map.127), calls=%async_computation.4 | async-start | bytes 131072 | tf_op jit(solution)/shard_map/all_to_all | solution.py:327
